TPU v7x, 32 devices: a whole 2x2x4 slice. The times are simulated.
32 devices in a mesh: grp: 2 (over y), ep: 16 (over z, x, core), tp: 1.
Axes of the slice: x: 2, y: 2, z: 4, core: 2. Of those that a mesh axis runs over, the one named last changes fastest.
Arguments:
- queries: bfloat16 [2048, 16, 128], P(('grp', 'ep'), 'tp'), parts along dimension 0, may hold values from -8 to 8
- new_keys: bfloat16 [2048, 2, 128], P(('grp', 'ep'), 'tp'), parts along dimension 0, may hold values from -8 to 8
- new_values: bfloat16 [2048, 2, 128], P(('grp', 'ep'), 'tp'), parts along dimension 0, may hold values from -6 to 6
- cache_keys: bfloat16 [2048, 2, 96, 128], P(('grp', 'ep'), 'tp'), parts along dimension 0, may hold values from -8 to 8
- cache_values: bfloat16 [2048, 2, 96, 128], P(('grp', 'ep'), 'tp'), parts along dimension 0, may hold values from -6 to 6
- cache_lengths: int32 [2048], P(('grp', 'ep')), parts along dimension 0, may hold values from 1 to 96, 24576 in all
- residual: bfloat16 [2048, 2048], P(('grp', 'ep')), parts along dimension 0, may hold values from -6 to 6
- out_weight: bfloat16 [2048, 2048], P('tp'), may hold values from -0.125 to 0.125
- norm_gain: float32 [2048], replicated, may hold values from 0.25 to 1.75
- expert_ids: int32 [2048, 8], P(('grp', 'ep')), parts along dimension 0, may hold values from 0 to 15, all different within a row; in each aligned block of 64 rows (0 to 63, 64 to 127, ...) at most 64 rows name the same one
- route_weights: float32 [2048, 8], P(('grp', 'ep')), parts along dimension 0, may hold values from 0.05 to 0.25
- learner_weights: bfloat16 [16, 3, 2048, 768], P(None, None, 'ep', 'tp'), may hold values from -0.125 to 0.125
Outputs:
- hidden_out: bfloat16 [2048, 2048], P(('grp', 'ep'), 'tp'), parts along dimension 0
There are 2 independent parts, one for each index of `grp`. A program takes and returns all parts, laid end to end along the dimension named above; an argument that names none is the same for every part. Nothing has to cross between parts.
Inputs may be any that keep to these rules, and one draw needn't show every extreme that they name: `expert_ids`: each row names 8 different experts. Among the 64 rows of one index of ep no expert is named by more than 64 rows, a bound that some block reaches. `cache_lengths`: the 1024 lengths of one rollout group sum to 24576, and some sequence of each group has all 96 slots live; the whole array, which holds every group laid end to end, sums to that total times the number of groups.
All inputs are finite; a program needn't handle non-finite values.
Results may differ from a plain program's by a relative error of at most 0.0095.
Values may be sent and summed in bfloat16 or wider, within the bound.
No kernel may reach another device: no remote copies, remote signals or barrier semaphores. Data moves between devices by JAX's collectives and lax.ppermute only.
A program may use at most 128 MiB of HBM per device.

v0:
```python
import jax
import jax.numpy as jnp
from jax import lax
from jax.sharding import PartitionSpec as P


def attend(queries, new_keys, new_values, cache_keys, cache_values, cache_lengths):
    seq_count, q_heads, head_size = queries.shape
    kv_heads = cache_keys.shape[1]
    length = cache_keys.shape[2]
    groups = q_heads // kv_heads
    score_scale = head_size ** (-0.5)
    grouped = queries.reshape(seq_count, kv_heads, groups, head_size)
    scores = (
        jnp.einsum("skgd,skld->skgl", grouped, cache_keys, preferred_element_type=jnp.float32)
        * score_scale
    )
    own_score = (
        jnp.einsum("skgd,skd->skg", grouped, new_keys, preferred_element_type=jnp.float32)
        * score_scale
    )
    live_mask = (
        jnp.arange(length, dtype=jnp.int32)[None, None, None, :]
        < cache_lengths[:, None, None, None]
    )
    masked = jnp.where(live_mask, scores, -1e30)
    row_top = jnp.maximum(jnp.max(masked, axis=-1), own_score)
    cache_exp = jnp.where(live_mask, jnp.exp(masked - row_top[..., None]), 0.0)
    own_exp = jnp.exp(own_score - row_top)
    row_total = jnp.sum(cache_exp, axis=-1) + own_exp
    probs_cache = (cache_exp / row_total[..., None]).astype(jnp.bfloat16)
    probs_own = (own_exp / row_total).astype(jnp.bfloat16)
    context = jnp.einsum(
        "skgl,skld->skgd", probs_cache, cache_values, preferred_element_type=jnp.float32
    )
    context = (
        context
        + probs_own.astype(jnp.float32)[..., None] * new_values.astype(jnp.float32)[:, :, None, :]
    )
    return context.astype(jnp.bfloat16).reshape(seq_count, q_heads * head_size)


def route_slots(expert_ids, experts, capacity):
    flat_ids = expert_ids.reshape(-1)
    onehot = (flat_ids[:, None] == jnp.arange(experts, dtype=jnp.int32)[None, :]).astype(jnp.int32)
    before = jnp.cumsum(onehot, axis=0) - onehot
    route_rank = jnp.sum(before * onehot, axis=1)
    return flat_ids * capacity + route_rank


def shards(
    queries,
    new_keys,
    new_values,
    cache_keys,
    cache_values,
    cache_lengths,
    residual,
    out_weight,
    norm_gain,
    expert_ids,
    route_weights,
    learner_weights,
):
    seq_count, model_width = residual.shape
    top_count = expert_ids.shape[1]
    experts = learner_weights.shape[0]
    capacity = min(seq_count, 16 * seq_count // experts)
    half_width = model_width // lax.axis_size("tp")
    offset = lax.axis_index("tp") * half_width
    context = attend(queries, new_keys, new_values, cache_keys, cache_values, cache_lengths)
    partial_value = jnp.dot(context, out_weight, preferred_element_type=jnp.float32)
    owned_weights = lax.all_to_all(learner_weights, "ep", split_axis=0, concat_axis=2, tiled=True)[
        0
    ]
    route_slot = route_slots(expert_ids, experts, capacity)
    route_count = seq_count * top_count
    source = (
        jnp.full((experts * capacity,), route_count, jnp.int32)
        .at[route_slot]
        .set(jnp.arange(route_count, dtype=jnp.int32))
    )
    token_of_slot = source // top_count
    attn_sum = lax.psum(partial_value, "tp")
    full_stream = residual.astype(jnp.float32) + attn_sum
    mean_square = jnp.mean(full_stream * full_stream, axis=1, keepdims=True)
    normed = (full_stream * lax.rsqrt(mean_square + 1e-06) * norm_gain).astype(jnp.bfloat16)
    stream = lax.dynamic_slice_in_dim(full_stream, offset, half_width, 1)
    padded = jnp.concatenate([normed, jnp.zeros((1, model_width), jnp.bfloat16)], axis=0)
    outgoing = padded[token_of_slot].reshape(experts, capacity, model_width)
    arrived = lax.all_to_all(outgoing, "ep", split_axis=0, concat_axis=0, tiled=True)
    src_count = arrived.shape[0]
    item_count = arrived.shape[1]
    slot_rows = arrived.reshape(src_count * item_count, model_width)
    gate_act = jnp.dot(slot_rows, owned_weights[0], preferred_element_type=jnp.float32)
    up_act = jnp.dot(slot_rows, owned_weights[1], preferred_element_type=jnp.float32)
    hidden = (jax.nn.silu(gate_act) * up_act).astype(jnp.bfloat16)
    expert_terms = lax.dot_general(
        hidden, owned_weights[2], (((1,), (1,)), ((), ())), preferred_element_type=jnp.float32
    )
    expert_terms = expert_terms.reshape(src_count, item_count, model_width).astype(jnp.bfloat16)
    returned = lax.all_to_all(expert_terms, "ep", split_axis=0, concat_axis=0, tiled=True)
    expert_out = lax.psum_scatter(
        returned.astype(jnp.float32).astype(jnp.bfloat16), "tp", scatter_dimension=2, tiled=True
    )
    gathered = expert_out.reshape(experts * capacity, half_width)[route_slot]
    gathered = gathered.reshape(seq_count, top_count, half_width).astype(jnp.float32)
    mixture = jnp.einsum("stk,st->sk", gathered, route_weights, precision=lax.Precision.HIGHEST)
    return (stream + mixture).astype(jnp.bfloat16)


def solution(mesh):
    return jax.shard_map(
        shards,
        mesh=mesh,
        in_specs=(
            P(("grp", "ep"), "tp", None),
            P(("grp", "ep"), "tp", None),
            P(("grp", "ep"), "tp", None),
            P(("grp", "ep"), "tp", None, None),
            P(("grp", "ep"), "tp", None, None),
            P(("grp", "ep")),
            P(("grp", "ep"), None),
            P("tp", None),
            P(),
            P(("grp", "ep"), None),
            P(("grp", "ep"), None),
            P(None, None, "ep", "tp"),
        ),
        out_specs=P(("grp", "ep"), "tp"),
        check_vma=False,
    )
```

profile of v0, /device:TPU:11, one launch (start us, length us, event | category | flops | bytes accessed | tf_op | source)
XLA Modules:
  0.0 437.2 jit_solution(17093866013520005315)
XLA Ops:
  0.0 0.0 copy-start
  0.0 0.0 copy-start.7
  0.0 0.0 copy-start.5
  0.0 0.0 copy-start.6
  0.0 6.8 %all-to-all-start.1 = ((bf16[16,3,128,768]{3,2,1,0:T(8,128)(2,1)}), bf16[16,3,128,768]{3,2,1,0:T(8,128)(2,1)}, u32[]{:S(2)}, u32[]{:S(2)}) async-start(bf16[16,3,128,768]{3,2,1,0:T(8,128)(2,1)} %param.23), calls=%async_computation.1 | async-start | bytes 18874368 | tf_op jit(solution)/shard_map/all_to_all | solution.py:73
  6.9 0.0 copy-done.7
  6.9 0.1 copy.30
  6.9 0.1 eq.29
  7.0 0.1 eq.25
  7.1 0.1 copy.29
  7.2 0.7 mul.85
  7.9 1.1 reduce-window.6
  9.0 0.2 slice_reduce_fusion
  9.3 0.0 copy-start.8
  9.3 0.0 copy-done.5
  9.3 1.0 fusion.8
  10.3 0.1 copy.34
  10.4 0.0 copy-done.6
  10.4 0.7 convert_element_type.44
  11.1 0.7 iota_compare_fusion.2
  11.8 4.5 %fusion.30 = (f32[64,2,8]{2,1,0:T(2,128)S(1)}, f32[64,2,8,96]{3,2,1,0:T(8,128)}) fusion(bf16[64,2,96,128]{3,2,1,0:T(8,128)(2,1)} %param.15, bf16[64,16,128]{2,1,0:T(8,128)(2,1)S(1)} %copy-done.5, pred[64,96]{1,0:T(8,128)(4,1)S(1)} %iota_compare_fusion.2), kind=kOutput, calls=%fused_computation.62 | convolution fusion | flops 25459712 | bytes 3811328 | tf_op jit(solution)/shard_map/skgd,skld->skgl/dot_general | solution.py:15
  16.3 0.1 copy.24
  16.4 0.1 copy.25
  16.5 1.4 fusion.5
  17.9 0.1 copy.26
  18.0 0.1 copy.27
  18.1 0.1 copy.28
  18.3 0.0 copy-done
  18.3 0.0 copy-start.4
  18.3 2.1 fusion.3
  20.4 0.0 copy-done.8
  20.4 0.0 copy-done.4
  20.4 0.0 copy-start.9
  20.4 0.0 slice-start
  20.4 0.0 copy-start.10
  20.4 5.1 %multiply_reduce_fusion = (f32[64]{0:T(128)S(1)}, f32[64,2048]{1,0:T(8,128)S(1)}) fusion(bf16[2048,2048]{1,0:T(8,128)(2,1)} %param.19, bf16[8,8,16,128]{3,2,1,0:T(8,128)(2,1)S(1)} %bitcast.87, bf16[64,2048]{1,0:T(8,128)(2,1)S(1)} %copy-done.4), kind=kOutput, calls=%fused_computation.15 | convolution fusion | flops 537395136 | bytes 9437440 | tf_op jit(solution)/shard_map/dot_general | solution.py:72
  25.5 0.0 copy-start.2
  25.5 0.8 copy-done.2
  26.3 0.0 copy-done.9
  26.3 0.1 multiply_convert_fusion.1
  26.4 0.0 slice-done
  26.4 0.1 fusion.18
  26.5 0.0 copy-done.10
  26.6 2.4 scatter_custom_fusion
  29.0 6.0 %gather_fusion = bf16[1024,2048]{1,0:T(8,128)(2,1)} fusion(bf16[65,2048]{1,0:T(8,128)(2,1)S(1)} %concatenate.3, s32[1024]{0:T(1024)S(1)} %fusion.23), kind=kCustom, calls=%fused_computation | custom fusion | bytes 8392704 | tf_op jit(solution)/shard_map/gather | solution.py:90
  35.0 176.6 %all-to-all-done.1 = bf16[16,3,128,768]{3,2,1,0:T(8,128)(2,1)} async-done(((bf16[16,3,128,768]{3,2,1,0:T(8,128)(2,1)}), bf16[16,3,128,768]{3,2,1,0:T(8,128)(2,1)}, u32[]{:S(2)}, u32[]{:S(2)}) %all-to-all-start.1) | async-done | bytes 9437216 | tf_op jit(solution)/shard_map/all_to_all | solution.py:73
  211.7 4.9 %all-to-all-start = ((bf16[16,64,2048]{2,1,0:T(8,128)(2,1)}), bf16[16,64,2048]{2,1,0:T(8,128)(2,1)}, u32[]{:S(2)}, u32[]{:S(2)}) async-start(bf16[16,64,2048]{2,1,0:T(8,128)(2,1)} %bitcast.83), calls=%async_computation | async-start | bytes 8388608 | tf_op jit(solution)/shard_map/all_to_all | solution.py:91
  216.6 6.0 %fusion.29 = (bf16[1,1,16,128,768]{4,3,1,2,0:T(8,128)(2,1)S(1)}, bf16[1,1,16,128,768]{4,3,1,2,0:T(8,128)(2,1)}, bf16[1,1,16,128,768]{4,3,1,2,0:T(8,128)(2,1)}) fusion(bf16[1,3,16,128,768]{4,3,1,2,0:T(8,128)(2,1)} %bitcast.9), kind=kLoop, calls=%fused_computation.61 | loop fusion | bytes 18874368 | tf_op jit(solution)/shard_map/slice | solution.py:99
  222.6 86.5 %all-to-all-done = bf16[16,64,2048]{2,1,0:T(8,128)(2,1)} async-done(((bf16[16,64,2048]{2,1,0:T(8,128)(2,1)}), bf16[16,64,2048]{2,1,0:T(8,128)(2,1)}, u32[]{:S(2)}, u32[]{:S(2)}) %all-to-all-start) | async-done | bytes 4194336 | tf_op jit(solution)/shard_map/all_to_all | solution.py:91
  309.0 0.0 copy-start.3
  309.0 6.3 %fusion.31 = f32[1024,768]{1,0:T(8,128)S(1)} fusion(bf16[1024,2048]{1,0:T(8,128)(2,1)} %bitcast.7, bf16[2048,768]{1,0:T(8,128)(2,1)} %bitcast.86), kind=kOutput, calls=%fused_computation.63 | convolution fusion | flops 3221225472 | bytes 10485760 | tf_op jit(solution)/shard_map/dot_general | solution.py:95
  315.3 0.0 copy-done.3
  315.3 5.8 %multiply_convert_fusion = bf16[1024,768]{1,0:T(8,128)(2,1)S(1)} fusion(f32[1024,768]{1,0:T(8,128)S(1)} %fusion.31, bf16[1024,2048]{1,0:T(8,128)(2,1)} %bitcast.7, bf16[2048,768]{1,0:T(8,128)(2,1)S(1)} %bitcast.85), kind=kOutput, calls=%fused_computation.4 | convolution fusion | flops 3225944064 | bytes 12058624 | tf_op jit(solution)/shard_map/dot_general | solution.py:96
  321.2 5.1 %convolution_convert_fusion = bf16[16,64,2048]{2,1,0:T(8,128)(2,1)} fusion(bf16[16,64,768]{2,1,0:T(8,128)(2,1)S(1)} %bitcast.93, bf16[2048,768,1]{1,0,2:T(8,128)(2,1)S(1)} %bitcast.84), kind=kOutput, calls=%fused_computation.3 | convolution fusion | flops 3223322624 | bytes 8912896 | tf_op jit(solution)/shard_map/dot_general | solution.py:98
  326.2 0.0 copy-start.11
  326.2 5.0 %all-to-all-start.2 = ((bf16[16,64,2048]{2,1,0:T(8,128)(2,1)}), bf16[16,64,2048]{2,1,0:T(8,128)(2,1)}, u32[]{:S(2)}, u32[]{:S(2)}) async-start(bf16[16,64,2048]{2,1,0:T(8,128)(2,1)} %convolution_convert_fusion), calls=%async_computation.2 | async-start | bytes 8388608 | tf_op jit(solution)/shard_map/all_to_all | solution.py:102
  331.3 0.0 copy-done.11
  331.3 0.1 copy.35
  331.4 92.4 %all-to-all-done.2 = bf16[16,64,2048]{2,1,0:T(8,128)(2,1)} async-done(((bf16[16,64,2048]{2,1,0:T(8,128)(2,1)}), bf16[16,64,2048]{2,1,0:T(8,128)(2,1)}, u32[]{:S(2)}, u32[]{:S(2)}) %all-to-all-start.2) | async-done | bytes 4194336 | tf_op jit(solution)/shard_map/all_to_all | solution.py:102
  423.7 0.0 copy-start.1
  423.7 8.1 %gather_fusion.1 = bf16[512,2048]{1,0:T(8,128)(2,1)} fusion(bf16[1024,2048]{1,0:T(8,128)(2,1)} %bitcast.16, s32[1024]{0:T(1024)S(1)} %pad_clamp_fusion), kind=kCustom, calls=%fused_computation.1 | custom fusion | bytes 4196352 | tf_op jit(solution)/shard_map/gather | solution.py:106
  431.9 3.4 fusion
  435.3 1.9 fusion.4
  437.2 0.0 copy-done.1
  (11 shorter events, 0.1 us)
Async XLA Ops:
  0.0 18.3 %copy-start = (bf16[64,2,96,128]{3,2,1,0:T(8,128)(2,1)S(1)}, bf16[64,2,96,128]{3,2,1,0:T(8,128)(2,1)}, u32[]{:S(2)}) copy-start(bf16[64,2,96,128]{3,2,1,0:T(8,128)(2,1)} %param.16) | copy-start | bytes 9437188
  0.0 6.8 %copy-start.7 = (s32[64,8]{0,1:T(8,128)S(1)}, s32[64,8]{0,1:T(8,128)}, u32[]{:S(2)}) copy-start(s32[64,8]{0,1:T(8,128)} %param.21) | copy-start | bytes 6148
  0.0 9.3 %copy-start.5 = (bf16[64,16,128]{2,1,0:T(8,128)(2,1)S(1)}, bf16[64,16,128]{2,1,0:T(8,128)(2,1)}, u32[]{:S(2)}) copy-start(bf16[64,16,128]{2,1,0:T(8,128)(2,1)} %param.12) | copy-start | bytes 786436
  0.0 10.4 %copy-start.6 = (bf16[64,2,128]{2,1,0:T(2,128)(2,1)S(1)}, bf16[64,2,128]{2,1,0:T(2,128)(2,1)}, u32[]{:S(2)}) copy-start(bf16[64,2,128]{2,1,0:T(2,128)(2,1)} %param.14) | copy-start | bytes 98308
  0.0 211.7 %all-to-all-start.1 = ((bf16[16,3,128,768]{3,2,1,0:T(8,128)(2,1)}), bf16[16,3,128,768]{3,2,1,0:T(8,128)(2,1)}, u32[]{:S(2)}, u32[]{:S(2)}) async-start(bf16[16,3,128,768]{3,2,1,0:T(8,128)(2,1)} %param.23), calls=%async_computation.1 | async-start | bytes 18874368 | tf_op jit(solution)/shard_map/all_to_all | solution.py:73
  9.3 11.1 %copy-start.8 = (s32[16,5]{0,1:T(8,128)}, s32[16,5]{0,1:T(8,128)S(1)}, u32[]{:S(2)}) copy-start(s32[16,5]{0,1:T(8,128)S(1)} %reduce-window.9) | copy-start | bytes 964
  18.3 2.1 copy-start.4
  20.4 5.9 %copy-start.9 = (f32[2048]{0:T(1024)S(1)}, f32[2048]{0:T(1024)}, u32[]{:S(2)}) copy-start(f32[2048]{0:T(1024)} %param.20) | copy-start | bytes 24580
  20.4 6.1 %slice-start = ((s32[16,5]{0,1:T(8,128)}), s32[16,4]{0,1:T(4,128)S(1)}, s32[]{:S(2)}) async-start(s32[16,5]{0,1:T(8,128)} %copy-done.8), calls=%async_computation.3 | async-start | bytes 4096 | tf_op jit(solution)/shard_map/slice.1
  20.4 6.1 %copy-start.10 = (s32[512,1]{0,1:T(1,128)S(1)}, s32[512,1]{0,1:T(1,128)}, u32[]{:S(2)}) copy-start(s32[512,1]{0,1:T(1,128)} %mul.85) | copy-start | bytes 6148
  25.5 0.8 copy-start.2
  211.7 97.4 %all-to-all-start = ((bf16[16,64,2048]{2,1,0:T(8,128)(2,1)}), bf16[16,64,2048]{2,1,0:T(8,128)(2,1)}, u32[]{:S(2)}, u32[]{:S(2)}) async-start(bf16[16,64,2048]{2,1,0:T(8,128)(2,1)} %bitcast.83), calls=%async_computation | async-start | bytes 8388608 | tf_op jit(solution)/shard_map/all_to_all | solution.py:91
  309.0 6.3 %copy-start.3 = (bf16[1,1,16,128,768]{4,3,1,2,0:T(8,128)(2,1)S(1)}, bf16[1,1,16,128,768]{4,3,1,2,0:T(8,128)(2,1)}, u32[]{:S(2)}) copy-start(bf16[1,1,16,128,768]{4,3,1,2,0:T(8,128)(2,1)} %get-tuple-element.6) | copy-start | bytes 9437188
  326.2 5.0 %copy-start.11 = (f32[64,8]{0,1:T(8,128)S(1)}, f32[64,8]{0,1:T(8,128)}, u32[]{:S(2)}) copy-start(f32[64,8]{0,1:T(8,128)} %param.22) | copy-start | bytes 6148
  326.2 97.5 %all-to-all-start.2 = ((bf16[16,64,2048]{2,1,0:T(8,128)(2,1)}), bf16[16,64,2048]{2,1,0:T(8,128)(2,1)}, u32[]{:S(2)}, u32[]{:S(2)}) async-start(bf16[16,64,2048]{2,1,0:T(8,128)(2,1)} %convolution_convert_fusion), calls=%async_computation.2 | async-start | bytes 8388608 | tf_op jit(solution)/shard_map/all_to_all | solution.py:102
  423.7 13.5 %copy-start.1 = (bf16[64,2,96,128]{3,2,1,0:T(8,128)(2,1)S(1)}, bf16[64,2,96,128]{3,2,1,0:T(8,128)(2,1)}, u32[]{:S(2)}) copy-start(bf16[64,2,96,128]{3,2,1,0:T(8,128)(2,1)} %param.16) | copy-start | bytes 9437188
where the time goes:
time: 438 us; the launch traced here: 437 us
  waiting for transfers between devices  356 us (81%)
  matrix products  33.2 us (8%)
  local copies, waits for them, and re-layouts  25.3 us (6%)
  starting transfers between devices  16.8 us (4%)
  other arithmetic  6.22 us (1%)
    all_to_all x1, waiting for transfers between devices, shards(): lax.all_to_all(learner_weights, 'ep', split_axis=0, concat_axis=2, tiled=...  177 us
    all_to_all x1, waiting for transfers between devices, shards(): lax.all_to_all(expert_terms, 'ep', split_axis=0, concat_axis=0, tiled=True)  92.4 us
    all_to_all x1, waiting for transfers between devices, shards(): lax.all_to_all(outgoing, 'ep', split_axis=0, concat_axis=0, tiled=True)  86.5 us
  transfers between devices with their start and end apart: 3, of which 3 were waited for; matrix products, arithmetic and copies ran while one was open for 8% of the time, Pallas kernels for 0%

commit v1 on v0

v1 whole, which is shorter than its diff:
```python
import functools

import jax
import jax.numpy as jnp
from jax import lax
from jax.experimental import pallas as pl
from jax.experimental.pallas import tpu as pltpu
from jax.sharding import PartitionSpec as P

LANES = 128


def attend(queries, new_keys, new_values, cache_keys, cache_values, cache_lengths):
    seq_count, q_heads, head_size = queries.shape
    kv_heads = cache_keys.shape[1]
    length = cache_keys.shape[2]
    groups = q_heads // kv_heads
    score_scale = head_size ** (-0.5)
    grouped = queries.reshape(seq_count, kv_heads, groups, head_size)
    scores = (
        jnp.einsum("skgd,skld->skgl", grouped, cache_keys, preferred_element_type=jnp.float32)
        * score_scale
    )
    own_score = (
        jnp.einsum("skgd,skd->skg", grouped, new_keys, preferred_element_type=jnp.float32)
        * score_scale
    )
    live_mask = (
        jnp.arange(length, dtype=jnp.int32)[None, None, None, :]
        < cache_lengths[:, None, None, None]
    )
    masked = jnp.where(live_mask, scores, -1e30)
    row_top = jnp.maximum(jnp.max(masked, axis=-1), own_score)
    cache_exp = jnp.where(live_mask, jnp.exp(masked - row_top[..., None]), 0.0)
    own_exp = jnp.exp(own_score - row_top)
    row_total = jnp.sum(cache_exp, axis=-1) + own_exp
    probs_cache = (cache_exp / row_total[..., None]).astype(jnp.bfloat16)
    probs_own = (own_exp / row_total).astype(jnp.bfloat16)
    context = jnp.einsum(
        "skgl,skld->skgd", probs_cache, cache_values, preferred_element_type=jnp.float32
    )
    context = (
        context
        + probs_own.astype(jnp.float32)[..., None] * new_values.astype(jnp.float32)[:, :, None, :]
    )
    return context.astype(jnp.bfloat16).reshape(seq_count, q_heads * head_size)


def swap_ep(x, bits):
    count = lax.axis_size("ep")
    return lax.ppermute(x, "ep", [(i, i ^ bits) for i in range(count)])


def swap_grp(x):
    return lax.ppermute(x, "grp", [(0, 1), (1, 0)])


def gather_weights(learner_weights, shared):
    ff = learner_weights.shape[3]
    count = lax.axis_size("ep")
    me = lax.axis_index("ep")
    grp = lax.axis_index("grp")
    rows = learner_weights.shape[2]
    half = ff // 2
    pieces = []
    for bits in range(count - 1, -1, -1):
        if bits in shared:
            block = lax.dynamic_slice(
                learner_weights, (me ^ bits, 0, 0, grp * half), (1, 3, rows, half)
            )[0]
            mine = swap_ep(block, bits)
            pieces.append((bits, 0, mine))
            pieces.append((bits, 1, swap_grp(mine)))
        else:
            block = lax.dynamic_index_in_dim(learner_weights, me ^ bits, 0, keepdims=False)
            pieces.append((bits, None, swap_ep(block, bits) if bits else block))
    return pieces


def expert_kernel(places, width, experts, where_ref, x_ref, *refs):
    piece_refs = refs[: len(places)]
    out_ref, weights, sems = refs[len(places) :]
    me, grp = where_ref[0], where_ref[1]
    rows, ff = piece_refs[0].shape[1], weights.shape[2]
    half = ff // 2

    @pl.when(pl.program_id(0) == 0)
    def load():
        copies = []
        for index, (bits, part) in enumerate(places):
            row = pl.ds(pl.multiple_of((me ^ bits) * rows, rows), rows)
            if part is None:
                target = weights.at[:, row, :]
            else:
                start = pl.multiple_of((grp ^ part) * half, LANES)
                target = weights.at[:, row, pl.ds(start, half)]
            copies.append(pltpu.make_async_copy(piece_refs[index], target, sems.at[index]))
        for copy in copies:
            copy.start()
        for copy in copies:
            copy.wait()

    x = x_ref[:, :width]
    extra = x_ref[:, width:].astype(jnp.float32)
    lane = lax.broadcasted_iota(jnp.int32, extra.shape, 1)
    picked = jnp.where((lane == me) | (lane == me + experts), extra, 0.0)
    coef = jnp.sum(picked, axis=1, keepdims=True)
    gate = jnp.dot(x, weights[0], preferred_element_type=jnp.float32)
    up = jnp.dot(x, weights[1], preferred_element_type=jnp.float32)
    hidden = (gate / (1.0 + jnp.exp(-gate)) * up).astype(jnp.bfloat16)
    down = lax.dot_general(
        hidden, weights[2], (((1,), (1,)), ((), ())), preferred_element_type=jnp.float32
    )
    out_ref[...] = (down * coef).astype(jnp.bfloat16)


def run_expert(tokens, pieces, width, experts):
    total, ext = tokens.shape
    ff = max(p[2].shape[2] for p in pieces)
    tile = 256 if total % 256 == 0 else total
    where = jnp.stack([lax.axis_index("ep"), lax.axis_index("grp")]).astype(jnp.int32)
    places = [(p[0], p[1]) for p in pieces]
    grid_spec = pltpu.PrefetchScalarGridSpec(
        num_scalar_prefetch=1,
        grid=(total // tile,),
        in_specs=[pl.BlockSpec((tile, ext), lambda i, w: (i, 0))]
        + [pl.BlockSpec(memory_space=pl.ANY)] * len(pieces),
        out_specs=pl.BlockSpec((tile, width), lambda i, w: (i, 0)),
        scratch_shapes=[
            pltpu.VMEM((3, width, ff), jnp.bfloat16),
            pltpu.SemaphoreType.DMA((len(pieces),)),
        ],
    )
    return pl.pallas_call(
        functools.partial(expert_kernel, places, width, experts),
        grid_spec=grid_spec,
        out_shape=jax.ShapeDtypeStruct((total, width), jnp.bfloat16),
        compiler_params=pltpu.CompilerParams(vmem_limit_bytes=40 * 1024 * 1024),
    )(where, tokens, *[p[2] for p in pieces])


def shards(
    queries,
    new_keys,
    new_values,
    cache_keys,
    cache_values,
    cache_lengths,
    residual,
    out_weight,
    norm_gain,
    expert_ids,
    route_weights,
    learner_weights,
):
    seq_count, width = residual.shape
    experts = learner_weights.shape[0]
    ff = learner_weights.shape[3]
    count = lax.axis_size("ep")
    parts = lax.axis_size("tp")
    stages = [1 << b for b in range(count.bit_length() - 2, -1, -1)]

    split = ff % (2 * LANES) == 0 and lax.axis_size("grp") == 2
    shared = set(range(count // 4, count)) if split else set()
    pieces = gather_weights(learner_weights, shared)

    context = attend(queries, new_keys, new_values, cache_keys, cache_values, cache_lengths)
    attn = jnp.dot(context, out_weight, preferred_element_type=jnp.float32)
    if parts > 1:
        attn = lax.psum(attn, "tp")
    stream = residual.astype(jnp.float32) + attn
    mean_square = jnp.mean(stream * stream, axis=1, keepdims=True)
    normed = (stream * lax.rsqrt(mean_square + 1e-06) * norm_gain).astype(jnp.bfloat16)

    hit = expert_ids[:, :, None] == jnp.arange(experts, dtype=jnp.int32)[None, None, :]
    coefs = jnp.sum(jnp.where(hit, route_weights[:, :, None], 0.0), axis=1)
    coarse = coefs.astype(jnp.bfloat16)
    fine = (coefs - coarse.astype(jnp.float32)).astype(jnp.bfloat16)
    tail = -(2 * experts) % LANES
    tokens = jnp.concatenate(
        [normed, coarse, fine, jnp.zeros((seq_count, tail), jnp.bfloat16)], axis=1
    )
    for bits in stages:
        tokens = jnp.concatenate([tokens, swap_ep(tokens, bits)], axis=0)

    terms = run_expert(tokens, pieces, width, experts)
    for bits in reversed(stages):
        keep = terms.shape[0] // 2
        other = swap_ep(terms[keep:], bits)
        terms = terms[:keep].astype(jnp.float32) + other.astype(jnp.float32)
        if bits != stages[0]:
            terms = terms.astype(jnp.bfloat16)
    if parts > 1:
        terms = lax.psum_scatter(terms, "tp", scatter_dimension=1, tiled=True)
        own = width // parts
        stream = lax.dynamic_slice_in_dim(stream, lax.axis_index("tp") * own, own, 1)
    return (stream + terms).astype(jnp.bfloat16)


def solution(mesh):
    return jax.shard_map(
        shards,
        mesh=mesh,
        in_specs=(
            P(("grp", "ep"), "tp", None),
            P(("grp", "ep"), "tp", None),
            P(("grp", "ep"), "tp", None),
            P(("grp", "ep"), "tp", None, None),
            P(("grp", "ep"), "tp", None, None),
            P(("grp", "ep")),
            P(("grp", "ep"), None),
            P("tp", None),
            P(),
            P(("grp", "ep"), None),
            P(("grp", "ep"), None),
            P(None, None, "ep", "tp"),
        ),
        out_specs=P(("grp", "ep"), "tp"),
        check_vma=False,
    )
```

time: 438 us -> 329 us (0.75)
  the two profiles are of different devices: /device:TPU:11 before, /device:TPU:0 now
where the time goes in v1:
time: 329 us
  waiting for transfers between devices  230 us (70%)
  starting transfers between devices  56.5 us (17%)
  Pallas kernels  13.8 us (4%)
  local copies, waits for them, and re-layouts  10.2 us (3%)
  matrix products  9.5 us (3%)
  other arithmetic  8.76 us (3%)
    ppermute x23, waiting for transfers between devices, swap_ep(): return lax.ppermute(x, 'ep', [(i, i ^ bits) for i in range(count)])  168 us
    ppermute x12, waiting for transfers between devices, swap_grp(): return lax.ppermute(x, 'grp', [(0, 1), (1, 0)])  62.2 us
    ppermute x23, starting transfers between devices, swap_ep(): return lax.ppermute(x, 'ep', [(i, i ^ bits) for i in range(count)])  41.2 us
    ppermute x12, starting transfers between devices, swap_grp(): return lax.ppermute(x, 'grp', [(0, 1), (1, 0)])  15.3 us
    pallas_call x1, Pallas kernels, run_expert(): pl.pallas_call(functools.partial(expert_kernel, places, width, experts),...  13.8 us
  transfers between devices with their start and end apart: 35, of which 27 were waited for; matrix products, arithmetic and copies ran while one was open for 3% of the time, Pallas kernels for 0%

profile of v1, /device:TPU:0, one launch (start us, length us, event | category | flops | bytes accessed | tf_op | source)
XLA Modules:
  0.0 328.9 jit_solution(10670428381154185736)
XLA Ops:
  0.0 0.9 select_reduce_fusion
  2.3 4.6 %fusion.17 = (f32[64,2,8]{2,1,0:T(2,128)S(1)}, f32[64,2,8,96]{3,2,1,0:T(8,128)}) fusion(bf16[64,2,96,128]{3,2,1,0:T(8,128)(2,1)} %param.15, bf16[64,16,128]{2,1,0:T(8,128)(2,1)} %param.12, pred[64,96]{1,0:T(8,128)(4,1)S(1)} %iota_compare_fusion.1), kind=kOutput, calls=%fused_computation.61 | convolution fusion | flops 25459712 | bytes 3811328 | tf_op jit(solution)/shard_map/skgd,skld->skgl/dot_general | solution.py:21
  6.9 1.0 fusion.5
  8.2 1.4 fusion.2
  10.0 2.2 fusion.1
  12.2 1.3 copy-done.2
  13.6 1.7 multiply_reduce_fusion
  15.7 4.1 %collective-permute-start = (bf16[64,2176]{1,0:T(8,128)(2,1)S(1)}, bf16[64,2176]{1,0:T(8,128)(2,1)S(1)}, u32[]{:S(2)}, u32[]{:S(2)}) collective-permute-start(bf16[64,2176]{1,0:T(8,128)(2,1)S(1)} %concatenate.18), channel_id=1, source_target_pairs={{0,8},{1,9},{2,10},{3,11},{4,12},{5,13},{6,14},{7,15},{8,0},{9,1},... | collective-permute-start | bytes 835592 | tf_op jit(solution)/shard_map/ppermute | solution.py:51
  19.8 12.6 %collective-permute-done = bf16[64,2176]{1,0:T(8,128)(2,1)S(1)} collective-permute-done((bf16[64,2176]{1,0:T(8,128)(2,1)S(1)}, bf16[64,2176]{1,0:T(8,128)(2,1)S(1)}, u32[]{:S(2)}, u32[]{:S(2)}) %collective-permute-start) | collective-permute-done | bytes 278560 | tf_op jit(solution)/shard_map/ppermute | solution.py:51
  32.4 0.8 collective-permute-start.1
  33.2 13.1 %collective-permute-done.1 = bf16[128,2176]{1,0:T(8,128)(2,1)S(1)} collective-permute-done((bf16[128,2176]{1,0:T(8,128)(2,1)S(1)}, bf16[128,2176]{1,0:T(8,128)(2,1)S(1)}, u32[]{:S(2)}, u32[]{:S(2)}) %collective-permute-start.1) | collective-permute-done | bytes 557088 | tf_op jit(solution)/shard_map/ppermute | solution.py:51
  46.3 1.1 pad_maximum_fusion.1
  47.4 1.3 collective-permute-start.2
  48.7 3.5 %dynamic-slice_bitcast_fusion.4 = (bf16[3,128,384]{2,1,0:T(8,128)(2,1)}, bf16[3,128,384]{2,1,0:T(8,128)(2,1)}, bf16[3,128,384]{2,1,0:T(8,128)(2,1)}, bf16[3,128,...) fusion(bf16[16,3,128,768]{3,2,1,0:T(8,128)(2,1)} %param.23, ...), kind=kLoop, calls=%fused_computation.21 | loop fusion | bytes 7077940 | tf_op jit(solution)/shard_map/squeeze | solution.py:68
  52.1 4.6 %collective-permute-start.10 = (bf16[3,128,384]{2,1,0:T(8,128)(2,1)S(1)}, bf16[3,128,384]{2,1,0:T(8,128)(2,1)S(1)}, u32[]{:S(2)}, u32[]{:S(2)}) collective-permute-start(bf16[3,128,384]{2,1,0:T(8,128)(2,1)S(1)} %get-tuple-element.17), channel_id=1, source_target_pairs={{0,12},{1,13},{2,14},{3,15},{4,8},{5,9},{6,10},{7,11},{8,4},{9,5},... | collective-permute-start | bytes 884744 | tf_op jit(solution)/shard_map/ppermute | solution.py:51
  56.7 15.7 %collective-permute-done.2 = bf16[256,2176]{1,0:T(8,128)(2,1)S(1)} collective-permute-done((bf16[256,2176]{1,0:T(8,128)(2,1)}, bf16[256,2176]{1,0:T(8,128)(2,1)S(1)}, u32[]{:S(2)}, u32[]{:S(2)}) %collective-permute-start.2) | collective-permute-done | bytes 1114144 | tf_op jit(solution)/shard_map/ppermute | solution.py:51
  72.4 1.6 pad_maximum_fusion
  74.1 5.3 %collective-permute-start.12 = (bf16[3,128,384]{2,1,0:T(8,128)(2,1)S(1)}, bf16[3,128,384]{2,1,0:T(8,128)(2,1)S(1)}, u32[]{:S(2)}, u32[]{:S(2)}) collective-permute-start(bf16[3,128,384]{2,1,0:T(8,128)(2,1)S(1)} %get-tuple-element.16), channel_id=1, source_target_pairs={{0,11},{1,10},{2,9},{3,8},{4,15},{5,14},{6,13},{7,12},{8,3},{9,2},... | collective-permute-start | bytes 884744 | tf_op jit(solution)/shard_map/ppermute | solution.py:51
  79.4 2.2 collective-permute-start.16
  82.3 29.7 %collective-permute-done.12.refs_8_ = bf16[3,128,384]{2,1,0:T(8,128)(2,1)S(1)} collective-permute-done((bf16[3,128,384]{2,1,0:T(8,128)(2,1)S(1)}, bf16[3,128,384]{2,1,0:T(8,128)(2,1)S(1)}, u32[]{:S(2)}, u32[]{:S(2)}) %collective-permute-start.12) | collective-permute-done | bytes 294944 | tf_op jit(solution)/shard_map/ppermute | solution.py:51
  112.3 6.5 %collective-permute-done.14.refs_10_ = bf16[3,128,384]{2,1,0:T(8,128)(2,1)S(1)} collective-permute-done((bf16[3,128,384]{2,1,0:T(8,128)(2,1)S(1)}, bf16[3,128,384]{2,1,0:T(8,128)(2,1)S(1)}, u32[]{:S(2)}, u32[]{:S(2)}) %collective-permute-start.14) | collective-permute-done | bytes 294944 | tf_op jit(solution)/shard_map/ppermute | solution.py:51
  119.3 4.6 %collective-permute-done.16.refs_12_ = bf16[3,128,384]{2,1,0:T(8,128)(2,1)S(1)} collective-permute-done((bf16[3,128,384]{2,1,0:T(8,128)(2,1)S(1)}, bf16[3,128,384]{2,1,0:T(8,128)(2,1)S(1)}, u32[]{:S(2)}, u32[]{:S(2)}) %collective-permute-start.16) | collective-permute-done | bytes 294944 | tf_op jit(solution)/shard_map/ppermute | solution.py:51
  123.8 1.2 collective-permute-start.24
  125.0 5.3 %collective-permute-done.18.refs_14_ = bf16[3,128,384]{2,1,0:T(8,128)(2,1)S(1)} collective-permute-done((bf16[3,128,384]{2,1,0:T(8,128)(2,1)S(1)}, bf16[3,128,384]{2,1,0:T(8,128)(2,1)S(1)}, u32[]{:S(2)}, u32[]{:S(2)}) %collective-permute-start.18) | collective-permute-done | bytes 294944 | tf_op jit(solution)/shard_map/ppermute | solution.py:51
  130.3 1.4 collective-permute-start.26
  131.9 1.9 dynamic-slice_bitcast_fusion
  133.8 3.7 %collective-permute-done.20.refs_16_ = bf16[3,128,384]{2,1,0:T(8,128)(2,1)S(1)} collective-permute-done((bf16[3,128,384]{2,1,0:T(8,128)(2,1)}, bf16[3,128,384]{2,1,0:T(8,128)(2,1)S(1)}, u32[]{:S(2)}, u32[]{:S(2)}) %collective-permute-start.20) | collective-permute-done | bytes 294944 | tf_op jit(solution)/shard_map/ppermute | solution.py:51
  137.5 4.0 %collective-permute-start.4 = (bf16[3,128,384]{2,1,0:T(8,128)(2,1)S(1)}, bf16[3,128,384]{2,1,0:T(8,128)(2,1)S(1)}, u32[]{:S(2)}, u32[]{:S(2)}) collective-permute-start(bf16[3,128,384]{2,1,0:T(8,128)(2,1)S(1)} %copy-done.12), channel_id=1, source_target_pairs={{0,15},{1,14},{2,13},{3,12},{4,11},{5,10},{6,9},{7,8},{8,7},{9,6},... | collective-permute-start | bytes 884744 | tf_op jit(solution)/shard_map/ppermute | solution.py:51
  141.5 8.7 %collective-permute-done.22.refs_18_ = bf16[3,128,384]{2,1,0:T(8,128)(2,1)S(1)} collective-permute-done((bf16[3,128,384]{2,1,0:T(8,128)(2,1)}, bf16[3,128,384]{2,1,0:T(8,128)(2,1)S(1)}, u32[]{:S(2)}, u32[]{:S(2)}) %collective-permute-start.22) | collective-permute-done | bytes 294944 | tf_op jit(solution)/shard_map/ppermute | solution.py:51
  150.2 4.3 %collective-permute-start.6 = (bf16[3,128,384]{2,1,0:T(8,128)(2,1)S(1)}, bf16[3,128,384]{2,1,0:T(8,128)(2,1)S(1)}, u32[]{:S(2)}, u32[]{:S(2)}) collective-permute-start(bf16[3,128,384]{2,1,0:T(8,128)(2,1)S(1)} %copy-done.11), channel_id=1, source_target_pairs={{0,14},{1,15},{2,12},{3,13},{4,10},{5,11},{6,8},{7,9},{8,6},{9,7},... | collective-permute-start | bytes 884744 | tf_op jit(solution)/shard_map/ppermute | solution.py:51
  154.4 7.4 %collective-permute-done.24.refs_20_ = bf16[3,128,384]{2,1,0:T(8,128)(2,1)S(1)} collective-permute-done((bf16[3,128,384]{2,1,0:T(8,128)(2,1)}, bf16[3,128,384]{2,1,0:T(8,128)(2,1)S(1)}, u32[]{:S(2)}, u32[]{:S(2)}) %collective-permute-start.24) | collective-permute-done | bytes 294944 | tf_op jit(solution)/shard_map/ppermute | solution.py:51
  161.8 4.0 %collective-permute-start.8 = (bf16[3,128,384]{2,1,0:T(8,128)(2,1)S(1)}, bf16[3,128,384]{2,1,0:T(8,128)(2,1)S(1)}, u32[]{:S(2)}, u32[]{:S(2)}) collective-permute-start(bf16[3,128,384]{2,1,0:T(8,128)(2,1)S(1)} %copy-done.10), channel_id=1, source_target_pairs={{0,13},{1,12},{2,15},{3,14},{4,9},{5,8},{6,11},{7,10},{8,5},{9,4},... | collective-permute-start | bytes 884744 | tf_op jit(solution)/shard_map/ppermute | solution.py:51
  165.9 8.6 %collective-permute-done.26.refs_22_ = bf16[3,128,384]{2,1,0:T(8,128)(2,1)S(1)} collective-permute-done((bf16[3,128,384]{2,1,0:T(8,128)(2,1)}, bf16[3,128,384]{2,1,0:T(8,128)(2,1)S(1)}, u32[]{:S(2)}, u32[]{:S(2)}) %collective-permute-start.26) | collective-permute-done | bytes 294944 | tf_op jit(solution)/shard_map/ppermute | solution.py:51
  174.5 1.5 collective-permute-start.11
  176.6 1.5 collective-permute-start.15
  178.6 5.7 %collective-permute-done.11.refs_7_ = bf16[3,128,384]{2,1,0:T(8,128)(2,1)S(1)} collective-permute-done((bf16[3,128,384]{2,1,0:T(8,128)(2,1)S(1)}, bf16[3,128,384]{2,1,0:T(8,128)(2,1)S(1)}, u32[]{:S(2)}, u32[]{:S(2)}) %collective-permute-start.11) | collective-permute-done | bytes 294944 | tf_op jit(solution)/shard_map/ppermute | solution.py:55
  184.3 1.5 collective-permute-start.19
  185.9 4.8 %collective-permute-done.13.refs_9_ = bf16[3,128,384]{2,1,0:T(8,128)(2,1)S(1)} collective-permute-done((bf16[3,128,384]{2,1,0:T(8,128)(2,1)S(1)}, bf16[3,128,384]{2,1,0:T(8,128)(2,1)S(1)}, u32[]{:S(2)}, u32[]{:S(2)}) %collective-permute-start.13) | collective-permute-done | bytes 294944 | tf_op jit(solution)/shard_map/ppermute | solution.py:55
  190.7 1.5 collective-permute-start.21
  192.2 4.8 %collective-permute-done.15.refs_11_ = bf16[3,128,384]{2,1,0:T(8,128)(2,1)S(1)} collective-permute-done((bf16[3,128,384]{2,1,0:T(8,128)(2,1)S(1)}, bf16[3,128,384]{2,1,0:T(8,128)(2,1)S(1)}, u32[]{:S(2)}, u32[]{:S(2)}) %collective-permute-start.15) | collective-permute-done | bytes 294944 | tf_op jit(solution)/shard_map/ppermute | solution.py:55
  197.0 1.5 collective-permute-start.23
  198.5 4.8 %collective-permute-done.17.refs_13_ = bf16[3,128,384]{2,1,0:T(8,128)(2,1)S(1)} collective-permute-done((bf16[3,128,384]{2,1,0:T(8,128)(2,1)S(1)}, bf16[3,128,384]{2,1,0:T(8,128)(2,1)S(1)}, u32[]{:S(2)}, u32[]{:S(2)}) %collective-permute-start.17) | collective-permute-done | bytes 294944 | tf_op jit(solution)/shard_map/ppermute | solution.py:55
  203.3 1.5 collective-permute-start.25
  204.8 4.8 %collective-permute-done.19.refs_15_ = bf16[3,128,384]{2,1,0:T(8,128)(2,1)S(1)} collective-permute-done((bf16[3,128,384]{2,1,0:T(8,128)(2,1)S(1)}, bf16[3,128,384]{2,1,0:T(8,128)(2,1)S(1)}, u32[]{:S(2)}, u32[]{:S(2)}) %collective-permute-start.19) | collective-permute-done | bytes 294944 | tf_op jit(solution)/shard_map/ppermute | solution.py:55
  209.6 1.5 collective-permute-start.27
  211.2 4.7 %collective-permute-done.21.refs_17_ = bf16[3,128,384]{2,1,0:T(8,128)(2,1)S(1)} collective-permute-done((bf16[3,128,384]{2,1,0:T(8,128)(2,1)S(1)}, bf16[3,128,384]{2,1,0:T(8,128)(2,1)S(1)}, u32[]{:S(2)}, u32[]{:S(2)}) %collective-permute-start.21) | collective-permute-done | bytes 294944 | tf_op jit(solution)/shard_map/ppermute | solution.py:55
  215.9 6.3 %collective-permute-done.23.refs_19_ = bf16[3,128,384]{2,1,0:T(8,128)(2,1)S(1)} collective-permute-done((bf16[3,128,384]{2,1,0:T(8,128)(2,1)S(1)}, bf16[3,128,384]{2,1,0:T(8,128)(2,1)S(1)}, u32[]{:S(2)}, u32[]{:S(2)}) %collective-permute-start.23) | collective-permute-done | bytes 294944 | tf_op jit(solution)/shard_map/ppermute | solution.py:55
  222.3 1.5 collective-permute-start.29
  223.8 4.8 %collective-permute-done.25.refs_21_ = bf16[3,128,384]{2,1,0:T(8,128)(2,1)S(1)} collective-permute-done((bf16[3,128,384]{2,1,0:T(8,128)(2,1)S(1)}, bf16[3,128,384]{2,1,0:T(8,128)(2,1)S(1)}, u32[]{:S(2)}, u32[]{:S(2)}) %collective-permute-start.25) | collective-permute-done | bytes 294944 | tf_op jit(solution)/shard_map/ppermute | solution.py:55
  228.6 5.4 %collective-permute-done.27.refs_23_ = bf16[3,128,384]{2,1,0:T(8,128)(2,1)S(1)} collective-permute-done((bf16[3,128,384]{2,1,0:T(8,128)(2,1)S(1)}, bf16[3,128,384]{2,1,0:T(8,128)(2,1)S(1)}, u32[]{:S(2)}, u32[]{:S(2)}) %collective-permute-start.27) | collective-permute-done | bytes 294944 | tf_op jit(solution)/shard_map/ppermute | solution.py:55
  234.0 1.5 collective-permute-start.5
  235.7 6.5 %collective-permute-done.5.refs_1_ = bf16[3,128,384]{2,1,0:T(8,128)(2,1)S(1)} collective-permute-done((bf16[3,128,384]{2,1,0:T(8,128)(2,1)S(1)}, bf16[3,128,384]{2,1,0:T(8,128)(2,1)S(1)}, u32[]{:S(2)}, u32[]{:S(2)}) %collective-permute-start.5) | collective-permute-done | bytes 294944 | tf_op jit(solution)/shard_map/ppermute | solution.py:55
  242.2 1.5 collective-permute-start.7
  244.2 1.9 constant_dynamic-update-slice_fusion.x_ref
  246.2 6.0 %collective-permute-done.7.refs_3_ = bf16[3,128,384]{2,1,0:T(8,128)(2,1)S(1)} collective-permute-done((bf16[3,128,384]{2,1,0:T(8,128)(2,1)S(1)}, bf16[3,128,384]{2,1,0:T(8,128)(2,1)S(1)}, u32[]{:S(2)}, u32[]{:S(2)}) %collective-permute-start.7) | collective-permute-done | bytes 294944 | tf_op jit(solution)/shard_map/ppermute | solution.py:55
  252.1 3.6 %collective-permute-done.9.refs_5_ = bf16[3,128,384]{2,1,0:T(8,128)(2,1)S(1)} collective-permute-done((bf16[3,128,384]{2,1,0:T(8,128)(2,1)S(1)}, bf16[3,128,384]{2,1,0:T(8,128)(2,1)S(1)}, u32[]{:S(2)}, u32[]{:S(2)}) %collective-permute-start.9) | collective-permute-done | bytes 294944 | tf_op jit(solution)/shard_map/ppermute | solution.py:55
  255.8 13.8 %shard_map.118 = bf16[1024,2048]{1,0:T(8,128)(2,1)S(1)} custom-call(s32[2]{0:T(128)S(1)} %pad_add_fusion.where_ref, bf16[1024,2176]{1,0:T(8,128)(2,1)} %copy-done.3, bf16[3,128,384]{2,1,0:T(8,128)(2,1)S(1)} %collective-permute-done.4.refs_0_, bf16[3,128,384]{2,1,0:T(8,128)(2,1)S(1)} %collective-permute-done.5.refs_1_, ...), custom_call_target="tpu_custom_call" | custom-call | tf_op jit(solution)/shard_map/pallas_call | solution.py:134
  269.9 4.1 %collective-permute-done.31 = bf16[512,2048]{1,0:T(8,128)(2,1)S(1)} collective-permute-done((bf16[512,2048]{1,0:T(8,128)(2,1)S(1)}, bf16[512,2048]{1,0:T(8,128)(2,1)S(1)}, u32[]{:S(2)}, u32[]{:S(2)}) %collective-permute-start.31) | collective-permute-done | bytes 2097184 | tf_op jit(solution)/shard_map/ppermute | solution.py:51
  274.1 0.8 add_convert_fusion
  275.0 1.6 collective-permute-start.32
  276.6 23.7 %collective-permute-done.32 = bf16[256,2048]{1,0:T(8,128)(2,1)S(1)} collective-permute-done((bf16[256,2048]{1,0:T(8,128)(2,1)S(1)}, bf16[256,2048]{1,0:T(8,128)(2,1)S(1)}, u32[]{:S(2)}, u32[]{:S(2)}) %collective-permute-start.32) | collective-permute-done | bytes 1048608 | tf_op jit(solution)/shard_map/ppermute | solution.py:51
  300.8 13.1 %collective-permute-done.33 = bf16[128,2048]{1,0:T(8,128)(2,1)S(1)} collective-permute-done((bf16[128,2048]{1,0:T(8,128)(2,1)S(1)}, bf16[128,2048]{1,0:T(8,128)(2,1)S(1)}, u32[]{:S(2)}, u32[]{:S(2)}) %collective-permute-start.33) | collective-permute-done | bytes 524320 | tf_op jit(solution)/shard_map/ppermute | solution.py:51
  314.1 3.2 collective-permute-start.34
  317.3 10.8 %collective-permute-done.34 = bf16[64,2048]{1,0:T(8,128)(2,1)S(1)} collective-permute-done((bf16[64,2048]{1,0:T(8,128)(2,1)S(1)}, bf16[64,2048]{1,0:T(8,128)(2,1)S(1)}, u32[]{:S(2)}, u32[]{:S(2)}) %collective-permute-start.34) | collective-permute-done | bytes 262176 | tf_op jit(solution)/shard_map/ppermute | solution.py:51
  (86 shorter events, 7.7 us)
Async XLA Ops:
  0.0 10.0 %copy-start = (bf16[64,2,96,128]{3,2,1,0:T(8,128)(2,1)S(1)}, bf16[64,2,96,128]{3,2,1,0:T(8,128)(2,1)}, u32[]{:S(2)}) copy-start(bf16[64,2,96,128]{3,2,1,0:T(8,128)(2,1)} %param.16) | copy-start | bytes 9437188
  0.0 6.9 %copy-start.14 = (bf16[64,16,128]{2,1,0:T(8,128)(2,1)S(1)}, bf16[64,16,128]{2,1,0:T(8,128)(2,1)}, u32[]{:S(2)}) copy-start(bf16[64,16,128]{2,1,0:T(8,128)(2,1)} %param.12) | copy-start | bytes 786436
  0.0 10.0 %copy-start.15 = (bf16[64,2,128]{2,1,0:T(2,128)(2,1)S(1)}, bf16[64,2,128]{2,1,0:T(2,128)(2,1)}, u32[]{:S(2)}) copy-start(bf16[64,2,128]{2,1,0:T(2,128)(2,1)} %param.14) | copy-start | bytes 98308
  10.0 3.5 %copy-start.2 = (bf16[2048,2048]{1,0:T(8,128)(2,1)S(1)}, bf16[2048,2048]{1,0:T(8,128)(2,1)}, u32[]{:S(2)}) copy-start(bf16[2048,2048]{1,0:T(8,128)(2,1)} %param.19) | copy-start | bytes 25165828
  10.0 3.5 %copy-start.13 = (bf16[64,2048]{1,0:T(8,128)(2,1)S(1)}, bf16[64,2048]{1,0:T(8,128)(2,1)}, u32[]{:S(2)}) copy-start(bf16[64,2048]{1,0:T(8,128)(2,1)} %param.18) | copy-start | bytes 786436
  13.6 1.7 copy-start.16
  13.6 1.9 copy-start.17
  15.3 36.9 %copy-start.4 = (f32[64,2048]{1,0:T(8,128)}, f32[64,2048]{1,0:T(8,128)S(1)}, u32[]{:S(2)}) copy-start(f32[64,2048]{1,0:T(8,128)S(1)} %get-tuple-element.26) | copy-start | bytes 1572868
  15.7 16.7 %collective-permute-start = (bf16[64,2176]{1,0:T(8,128)(2,1)S(1)}, bf16[64,2176]{1,0:T(8,128)(2,1)S(1)}, u32[]{:S(2)}, u32[]{:S(2)}) collective-permute-start(bf16[64,2176]{1,0:T(8,128)(2,1)S(1)} %concatenate.18), channel_id=1, source_target_pairs={{0,8},{1,9},{2,10},{3,11},{4,12},{5,13},{6,14},{7,15},{8,0},{9,1},... | collective-permute-start | bytes 835592 | tf_op jit(solution)/shard_map/ppermute | solution.py:51
  32.4 40.0 %copy-start.6 = (bf16[64,2176]{1,0:T(8,128)(2,1)}, bf16[64,2176]{1,0:T(8,128)(2,1)S(1)}, u32[]{:S(2)}) copy-start(bf16[64,2176]{1,0:T(8,128)(2,1)S(1)} %collective-permute-done) | copy-start | bytes 835588
  32.4 13.9 %collective-permute-start.1 = (bf16[128,2176]{1,0:T(8,128)(2,1)S(1)}, bf16[128,2176]{1,0:T(8,128)(2,1)S(1)}, u32[]{:S(2)}, u32[]{:S(2)}) collective-permute-start(bf16[128,2176]{1,0:T(8,128)(2,1)S(1)} %pad_maximum_fusion.2), channel_id=1, source_target_pairs={{0,4},{1,5},{2,6},{3,7},{4,0},{5,1},{6,2},{7,3},{8,12},{9,13},{10,... | collective-permute-start | bytes 1671176 | tf_op jit(solution)/shard_map/ppermute | solution.py:51
  47.4 25.0 %collective-permute-start.2 = (bf16[256,2176]{1,0:T(8,128)(2,1)}, bf16[256,2176]{1,0:T(8,128)(2,1)S(1)}, u32[]{:S(2)}, u32[]{:S(2)}) collective-permute-start(bf16[256,2176]{1,0:T(8,128)(2,1)} %pad_maximum_fusion.1), channel_id=1, source_target_pairs={{0,2},{1,3},{2,0},{3,1},{4,6},{5,7},{6,4},{7,5},{8,10},{9,11},{10,... | collective-permute-start | bytes 3342344 | tf_op jit(solution)/shard_map/ppermute | solution.py:51
  52.1 29.5 %collective-permute-start.10 = (bf16[3,128,384]{2,1,0:T(8,128)(2,1)S(1)}, bf16[3,128,384]{2,1,0:T(8,128)(2,1)S(1)}, u32[]{:S(2)}, u32[]{:S(2)}) collective-permute-start(bf16[3,128,384]{2,1,0:T(8,128)(2,1)S(1)} %get-tuple-element.17), channel_id=1, source_target_pairs={{0,12},{1,13},{2,14},{3,15},{4,8},{5,9},{6,10},{7,11},{8,4},{9,5},... | collective-permute-start | bytes 884744 | tf_op jit(solution)/shard_map/ppermute | solution.py:51
  72.4 7.0 %copy-start.8 = (bf16[256,2176]{1,0:T(8,128)(2,1)}, bf16[256,2176]{1,0:T(8,128)(2,1)S(1)}, u32[]{:S(2)}) copy-start(bf16[256,2176]{1,0:T(8,128)(2,1)S(1)} %collective-permute-done.2) | copy-start | bytes 3342340
  74.1 169.7 %collective-permute-start.3 = (bf16[512,2176]{1,0:T(8,128)(2,1)}, bf16[512,2176]{1,0:T(8,128)(2,1)}, u32[]{:S(2)}, u32[]{:S(2)}) collective-permute-start(bf16[512,2176]{1,0:T(8,128)(2,1)} %pad_maximum_fusion), channel_id=1, source_target_pairs={{0,1},{1,0},{2,3},{3,2},{4,5},{5,4},{6,7},{7,6},{8,9},{9,8},{10,11... | collective-permute-start | bytes 6684680 | tf_op jit(solution)/shard_map/ppermute | solution.py:51
  74.1 38.0 %collective-permute-start.12 = (bf16[3,128,384]{2,1,0:T(8,128)(2,1)S(1)}, bf16[3,128,384]{2,1,0:T(8,128)(2,1)S(1)}, u32[]{:S(2)}, u32[]{:S(2)}) collective-permute-start(bf16[3,128,384]{2,1,0:T(8,128)(2,1)S(1)} %get-tuple-element.16), channel_id=1, source_target_pairs={{0,11},{1,10},{2,9},{3,8},{4,15},{5,14},{6,13},{7,12},{8,3},{9,2},... | collective-permute-start | bytes 884744 | tf_op jit(solution)/shard_map/ppermute | solution.py:51
  79.4 39.4 %collective-permute-start.14 = (bf16[3,128,384]{2,1,0:T(8,128)(2,1)S(1)}, bf16[3,128,384]{2,1,0:T(8,128)(2,1)S(1)}, u32[]{:S(2)}, u32[]{:S(2)}) collective-permute-start(bf16[3,128,384]{2,1,0:T(8,128)(2,1)S(1)} %get-tuple-element.15), channel_id=1, source_target_pairs={{0,10},{1,11},{2,8},{3,9},{4,14},{5,15},{6,12},{7,13},{8,2},{9,3},... | collective-permute-start | bytes 884744 | tf_op jit(solution)/shard_map/ppermute | solution.py:51
  79.4 44.4 %collective-permute-start.16 = (bf16[3,128,384]{2,1,0:T(8,128)(2,1)S(1)}, bf16[3,128,384]{2,1,0:T(8,128)(2,1)S(1)}, u32[]{:S(2)}, u32[]{:S(2)}) collective-permute-start(bf16[3,128,384]{2,1,0:T(8,128)(2,1)S(1)} %get-tuple-element.14), channel_id=1, source_target_pairs={{0,9},{1,8},{2,11},{3,10},{4,13},{5,12},{6,15},{7,14},{8,1},{9,0},... | collective-permute-start | bytes 884744 | tf_op jit(solution)/shard_map/ppermute | solution.py:51
  81.6 48.7 %collective-permute-start.18 = (bf16[3,128,384]{2,1,0:T(8,128)(2,1)S(1)}, bf16[3,128,384]{2,1,0:T(8,128)(2,1)S(1)}, u32[]{:S(2)}, u32[]{:S(2)}) collective-permute-start(bf16[3,128,384]{2,1,0:T(8,128)(2,1)S(1)} %get-tuple-element.13), channel_id=1, source_target_pairs={{0,8},{1,9},{2,10},{3,11},{4,12},{5,13},{6,14},{7,15},{8,0},{9,1},... | collective-permute-start | bytes 884744 | tf_op jit(solution)/shard_map/ppermute | solution.py:51
  112.0 25.4 %collective-permute-start.20 = (bf16[3,128,384]{2,1,0:T(8,128)(2,1)}, bf16[3,128,384]{2,1,0:T(8,128)(2,1)S(1)}, u32[]{:S(2)}, u32[]{:S(2)}) collective-permute-start(bf16[3,128,384]{2,1,0:T(8,128)(2,1)} %get-tuple-element.12), channel_id=1, source_target_pairs={{0,7},{1,6},{2,5},{3,4},{4,3},{5,2},{6,1},{7,0},{8,15},{9,14},{10,... | collective-permute-start | bytes 884744 | tf_op jit(solution)/shard_map/ppermute | solution.py:51
  118.8 31.3 %collective-permute-start.22 = (bf16[3,128,384]{2,1,0:T(8,128)(2,1)}, bf16[3,128,384]{2,1,0:T(8,128)(2,1)S(1)}, u32[]{:S(2)}, u32[]{:S(2)}) collective-permute-start(bf16[3,128,384]{2,1,0:T(8,128)(2,1)} %get-tuple-element.11), channel_id=1, source_target_pairs={{0,6},{1,7},{2,4},{3,5},{4,2},{5,3},{6,0},{7,1},{8,14},{9,15},{10,... | collective-permute-start | bytes 884744 | tf_op jit(solution)/shard_map/ppermute | solution.py:51
  123.8 38.0 %collective-permute-start.24 = (bf16[3,128,384]{2,1,0:T(8,128)(2,1)}, bf16[3,128,384]{2,1,0:T(8,128)(2,1)S(1)}, u32[]{:S(2)}, u32[]{:S(2)}) collective-permute-start(bf16[3,128,384]{2,1,0:T(8,128)(2,1)} %get-tuple-element.10), channel_id=1, source_target_pairs={{0,5},{1,4},{2,7},{3,6},{4,1},{5,0},{6,3},{7,2},{8,13},{9,12},{10,... | collective-permute-start | bytes 884744 | tf_op jit(solution)/shard_map/ppermute | solution.py:51
  130.3 44.1 %collective-permute-start.26 = (bf16[3,128,384]{2,1,0:T(8,128)(2,1)}, bf16[3,128,384]{2,1,0:T(8,128)(2,1)S(1)}, u32[]{:S(2)}, u32[]{:S(2)}) collective-permute-start(bf16[3,128,384]{2,1,0:T(8,128)(2,1)} %get-tuple-element.9), channel_id=1, source_target_pairs={{0,4},{1,5},{2,6},{3,7},{4,0},{5,1},{6,2},{7,3},{8,12},{9,13},{10,... | collective-permute-start | bytes 884744 | tf_op jit(solution)/shard_map/ppermute | solution.py:51
  131.8 5.7 %copy-start.12 = (bf16[3,128,384]{2,1,0:T(8,128)(2,1)S(1)}, bf16[3,128,384]{2,1,0:T(8,128)(2,1)}, u32[]{:S(2)}) copy-start(bf16[3,128,384]{2,1,0:T(8,128)(2,1)} %get-tuple-element.20) | copy-start | bytes 884740
  131.8 18.4 %copy-start.11 = (bf16[3,128,384]{2,1,0:T(8,128)(2,1)S(1)}, bf16[3,128,384]{2,1,0:T(8,128)(2,1)}, u32[]{:S(2)}) copy-start(bf16[3,128,384]{2,1,0:T(8,128)(2,1)} %get-tuple-element.19) | copy-start | bytes 884740
  131.8 30.0 %copy-start.10 = (bf16[3,128,384]{2,1,0:T(8,128)(2,1)S(1)}, bf16[3,128,384]{2,1,0:T(8,128)(2,1)}, u32[]{:S(2)}) copy-start(bf16[3,128,384]{2,1,0:T(8,128)(2,1)} %get-tuple-element.18) | copy-start | bytes 884740
  131.8 54.1 %copy-start.7 = (bf16[64,2176]{1,0:T(8,128)(2,1)S(1)}, bf16[64,2176]{1,0:T(8,128)(2,1)}, u32[]{:S(2)}) copy-start(bf16[64,2176]{1,0:T(8,128)(2,1)} %copy-done.6) | copy-start | bytes 835588
  131.9 103.7 %copy-start.9 = (bf16[256,2176]{1,0:T(8,128)(2,1)S(1)}, bf16[256,2176]{1,0:T(8,128)(2,1)}, u32[]{:S(2)}) copy-start(bf16[256,2176]{1,0:T(8,128)(2,1)} %copy-done.8) | copy-start | bytes 3342340
  137.5 38.6 %collective-permute-start.4 = (bf16[3,128,384]{2,1,0:T(8,128)(2,1)S(1)}, bf16[3,128,384]{2,1,0:T(8,128)(2,1)S(1)}, u32[]{:S(2)}, u32[]{:S(2)}) collective-permute-start(bf16[3,128,384]{2,1,0:T(8,128)(2,1)S(1)} %copy-done.12), channel_id=1, source_target_pairs={{0,15},{1,14},{2,13},{3,12},{4,11},{5,10},{6,9},{7,8},{8,7},{9,6},... | collective-permute-start | bytes 884744 | tf_op jit(solution)/shard_map/ppermute | solution.py:51
  150.2 26.4 %collective-permute-start.6 = (bf16[3,128,384]{2,1,0:T(8,128)(2,1)S(1)}, bf16[3,128,384]{2,1,0:T(8,128)(2,1)S(1)}, u32[]{:S(2)}, u32[]{:S(2)}) collective-permute-start(bf16[3,128,384]{2,1,0:T(8,128)(2,1)S(1)} %copy-done.11), channel_id=1, source_target_pairs={{0,14},{1,15},{2,12},{3,13},{4,10},{5,11},{6,8},{7,9},{8,6},{9,7},... | collective-permute-start | bytes 884744 | tf_op jit(solution)/shard_map/ppermute | solution.py:51
  161.8 16.3 %collective-permute-start.8 = (bf16[3,128,384]{2,1,0:T(8,128)(2,1)S(1)}, bf16[3,128,384]{2,1,0:T(8,128)(2,1)S(1)}, u32[]{:S(2)}, u32[]{:S(2)}) collective-permute-start(bf16[3,128,384]{2,1,0:T(8,128)(2,1)S(1)} %copy-done.10), channel_id=1, source_target_pairs={{0,13},{1,12},{2,15},{3,14},{4,9},{5,8},{6,11},{7,10},{8,5},{9,4},... | collective-permute-start | bytes 884744 | tf_op jit(solution)/shard_map/ppermute | solution.py:51
  174.5 9.9 %collective-permute-start.11 = (bf16[3,128,384]{2,1,0:T(8,128)(2,1)S(1)}, bf16[3,128,384]{2,1,0:T(8,128)(2,1)S(1)}, u32[]{:S(2)}, u32[]{:S(2)}) collective-permute-start(bf16[3,128,384]{2,1,0:T(8,128)(2,1)S(1)} %collective-permute-done.10.refs_6_), channel_id=1, source_target_pairs={{0,16},{16,0},{1,17},{17,1},{2,18},{18,2},{3,19},{19,3},{4,20},{20... | collective-permute-start | bytes 884744 | tf_op jit(solution)/shard_map/ppermute | solution.py:55
  176.0 14.6 %collective-permute-start.13 = (bf16[3,128,384]{2,1,0:T(8,128)(2,1)S(1)}, bf16[3,128,384]{2,1,0:T(8,128)(2,1)S(1)}, u32[]{:S(2)}, u32[]{:S(2)}) collective-permute-start(bf16[3,128,384]{2,1,0:T(8,128)(2,1)S(1)} %collective-permute-done.12.refs_8_), channel_id=1, source_target_pairs={{0,16},{16,0},{1,17},{17,1},{2,18},{18,2},{3,19},{19,3},{4,20},{20... | collective-permute-start | bytes 884744 | tf_op jit(solution)/shard_map/ppermute | solution.py:55
  176.6 20.4 %collective-permute-start.15 = (bf16[3,128,384]{2,1,0:T(8,128)(2,1)S(1)}, bf16[3,128,384]{2,1,0:T(8,128)(2,1)S(1)}, u32[]{:S(2)}, u32[]{:S(2)}) collective-permute-start(bf16[3,128,384]{2,1,0:T(8,128)(2,1)S(1)} %collective-permute-done.14.refs_10_), channel_id=1, source_target_pairs={{0,16},{16,0},{1,17},{17,1},{2,18},{18,2},{3,19},{19,3},{4,20},{20... | collective-permute-start | bytes 884744 | tf_op jit(solution)/shard_map/ppermute | solution.py:55
  178.1 25.2 %collective-permute-start.17 = (bf16[3,128,384]{2,1,0:T(8,128)(2,1)S(1)}, bf16[3,128,384]{2,1,0:T(8,128)(2,1)S(1)}, u32[]{:S(2)}, u32[]{:S(2)}) collective-permute-start(bf16[3,128,384]{2,1,0:T(8,128)(2,1)S(1)} %collective-permute-done.16.refs_12_), channel_id=1, source_target_pairs={{0,16},{16,0},{1,17},{17,1},{2,18},{18,2},{3,19},{19,3},{4,20},{20... | collective-permute-start | bytes 884744 | tf_op jit(solution)/shard_map/ppermute | solution.py:55
  184.3 25.3 %collective-permute-start.19 = (bf16[3,128,384]{2,1,0:T(8,128)(2,1)S(1)}, bf16[3,128,384]{2,1,0:T(8,128)(2,1)S(1)}, u32[]{:S(2)}, u32[]{:S(2)}) collective-permute-start(bf16[3,128,384]{2,1,0:T(8,128)(2,1)S(1)} %collective-permute-done.18.refs_14_), channel_id=1, source_target_pairs={{0,16},{16,0},{1,17},{17,1},{2,18},{18,2},{3,19},{19,3},{4,20},{20... | collective-permute-start | bytes 884744 | tf_op jit(solution)/shard_map/ppermute | solution.py:55
  190.7 25.3 %collective-permute-start.21 = (bf16[3,128,384]{2,1,0:T(8,128)(2,1)S(1)}, bf16[3,128,384]{2,1,0:T(8,128)(2,1)S(1)}, u32[]{:S(2)}, u32[]{:S(2)}) collective-permute-start(bf16[3,128,384]{2,1,0:T(8,128)(2,1)S(1)} %collective-permute-done.20.refs_16_), channel_id=1, source_target_pairs={{0,16},{16,0},{1,17},{17,1},{2,18},{18,2},{3,19},{19,3},{4,20},{20... | collective-permute-start | bytes 884744 | tf_op jit(solution)/shard_map/ppermute | solution.py:55
  197.0 25.3 %collective-permute-start.23 = (bf16[3,128,384]{2,1,0:T(8,128)(2,1)S(1)}, bf16[3,128,384]{2,1,0:T(8,128)(2,1)S(1)}, u32[]{:S(2)}, u32[]{:S(2)}) collective-permute-start(bf16[3,128,384]{2,1,0:T(8,128)(2,1)S(1)} %collective-permute-done.22.refs_18_), channel_id=1, source_target_pairs={{0,16},{16,0},{1,17},{17,1},{2,18},{18,2},{3,19},{19,3},{4,20},{20... | collective-permute-start | bytes 884744 | tf_op jit(solution)/shard_map/ppermute | solution.py:55
  203.3 25.3 %collective-permute-start.25 = (bf16[3,128,384]{2,1,0:T(8,128)(2,1)S(1)}, bf16[3,128,384]{2,1,0:T(8,128)(2,1)S(1)}, u32[]{:S(2)}, u32[]{:S(2)}) collective-permute-start(bf16[3,128,384]{2,1,0:T(8,128)(2,1)S(1)} %collective-permute-done.24.refs_20_), channel_id=1, source_target_pairs={{0,16},{16,0},{1,17},{17,1},{2,18},{18,2},{3,19},{19,3},{4,20},{20... | collective-permute-start | bytes 884744 | tf_op jit(solution)/shard_map/ppermute | solution.py:55
  209.6 24.4 %collective-permute-start.27 = (bf16[3,128,384]{2,1,0:T(8,128)(2,1)S(1)}, bf16[3,128,384]{2,1,0:T(8,128)(2,1)S(1)}, u32[]{:S(2)}, u32[]{:S(2)}) collective-permute-start(bf16[3,128,384]{2,1,0:T(8,128)(2,1)S(1)} %collective-permute-done.26.refs_22_), channel_id=1, source_target_pairs={{0,16},{16,0},{1,17},{17,1},{2,18},{18,2},{3,19},{19,3},{4,20},{20... | collective-permute-start | bytes 884744 | tf_op jit(solution)/shard_map/ppermute | solution.py:55
  215.9 39.8 %collective-permute-start.28 = (bf16[3,128,768]{2,1,0:T(8,128)(2,1)S(1)}, bf16[3,128,768]{2,1,0:T(8,128)(2,1)S(1)}, u32[]{:S(2)}, u32[]{:S(2)}) collective-permute-start(bf16[3,128,768]{2,1,0:T(8,128)(2,1)S(1)} %get-tuple-element.7), channel_id=1, source_target_pairs={{0,3},{1,2},{2,1},{3,0},{4,7},{5,6},{6,5},{7,4},{8,11},{9,10},{10,... | collective-permute-start | bytes 1769480 | tf_op jit(solution)/shard_map/ppermute | solution.py:51
  222.3 33.5 %collective-permute-start.29 = (bf16[3,128,768]{2,1,0:T(8,128)(2,1)S(1)}, bf16[3,128,768]{2,1,0:T(8,128)(2,1)S(1)}, u32[]{:S(2)}, u32[]{:S(2)}) collective-permute-start(bf16[3,128,768]{2,1,0:T(8,128)(2,1)S(1)} %get-tuple-element.6), channel_id=1, source_target_pairs={{0,2},{1,3},{2,0},{3,1},{4,6},{5,7},{6,4},{7,5},{8,10},{9,11},{10,... | collective-permute-start | bytes 1769480 | tf_op jit(solution)/shard_map/ppermute | solution.py:51
  228.6 27.2 %collective-permute-start.30 = (bf16[3,128,768]{2,1,0:T(8,128)(2,1)S(1)}, bf16[3,128,768]{2,1,0:T(8,128)(2,1)S(1)}, u32[]{:S(2)}, u32[]{:S(2)}) collective-permute-start(bf16[3,128,768]{2,1,0:T(8,128)(2,1)S(1)} %get-tuple-element.8), channel_id=1, source_target_pairs={{0,1},{1,0},{2,3},{3,2},{4,5},{5,4},{6,7},{7,6},{8,9},{9,8},{10,11... | collective-permute-start | bytes 1769480 | tf_op jit(solution)/shard_map/ppermute | solution.py:51
  234.0 8.2 %collective-permute-start.5 = (bf16[3,128,384]{2,1,0:T(8,128)(2,1)S(1)}, bf16[3,128,384]{2,1,0:T(8,128)(2,1)S(1)}, u32[]{:S(2)}, u32[]{:S(2)}) collective-permute-start(bf16[3,128,384]{2,1,0:T(8,128)(2,1)S(1)} %collective-permute-done.4.refs_0_), channel_id=1, source_target_pairs={{0,16},{16,0},{1,17},{17,1},{2,18},{18,2},{3,19},{19,3},{4,20},{20... | collective-permute-start | bytes 884744 | tf_op jit(solution)/shard_map/ppermute | solution.py:55
  242.2 9.9 %collective-permute-start.7 = (bf16[3,128,384]{2,1,0:T(8,128)(2,1)S(1)}, bf16[3,128,384]{2,1,0:T(8,128)(2,1)S(1)}, u32[]{:S(2)}, u32[]{:S(2)}) collective-permute-start(bf16[3,128,384]{2,1,0:T(8,128)(2,1)S(1)} %collective-permute-done.6.refs_2_), channel_id=1, source_target_pairs={{0,16},{16,0},{1,17},{17,1},{2,18},{18,2},{3,19},{19,3},{4,20},{20... | collective-permute-start | bytes 884744 | tf_op jit(solution)/shard_map/ppermute | solution.py:55
  243.7 12.0 %collective-permute-start.9 = (bf16[3,128,384]{2,1,0:T(8,128)(2,1)S(1)}, bf16[3,128,384]{2,1,0:T(8,128)(2,1)S(1)}, u32[]{:S(2)}, u32[]{:S(2)}) collective-permute-start(bf16[3,128,384]{2,1,0:T(8,128)(2,1)S(1)} %collective-permute-done.8.refs_4_), channel_id=1, source_target_pairs={{0,16},{16,0},{1,17},{17,1},{2,18},{18,2},{3,19},{19,3},{4,20},{20... | collective-permute-start | bytes 884744 | tf_op jit(solution)/shard_map/ppermute | solution.py:55
  246.2 9.6 %copy-start.3 = (bf16[1024,2176]{1,0:T(8,128)(2,1)}, bf16[1024,2176]{1,0:T(8,128)(2,1)S(1)}, u32[]{:S(2)}) copy-start(bf16[1024,2176]{1,0:T(8,128)(2,1)S(1)} %constant_dynamic-update-slice_fusion.x_ref) | copy-start | bytes 13369348
  269.9 4.2 %collective-permute-start.31 = (bf16[512,2048]{1,0:T(8,128)(2,1)S(1)}, bf16[512,2048]{1,0:T(8,128)(2,1)S(1)}, u32[]{:S(2)}, u32[]{:S(2)}) collective-permute-start(bf16[512,2048]{1,0:T(8,128)(2,1)S(1)} %slice.33), channel_id=1, source_target_pairs={{0,1},{1,0},{2,3},{3,2},{4,5},{5,4},{6,7},{7,6},{8,9},{9,8},{10,11... | collective-permute-start | bytes 6291464 | tf_op jit(solution)/shard_map/ppermute | solution.py:51
  274.9 54.0 %copy-start.1 = (bf16[64,2,96,128]{3,2,1,0:T(8,128)(2,1)S(1)}, bf16[64,2,96,128]{3,2,1,0:T(8,128)(2,1)}, u32[]{:S(2)}) copy-start(bf16[64,2,96,128]{3,2,1,0:T(8,128)(2,1)} %param.16) | copy-start | bytes 9437188
  275.0 53.1 %copy-start.5 = (f32[64,2048]{1,0:T(8,128)S(1)}, f32[64,2048]{1,0:T(8,128)}, u32[]{:S(2)}) copy-start(f32[64,2048]{1,0:T(8,128)} %copy-done.4) | copy-start | bytes 1572868
  275.0 25.3 %collective-permute-start.32 = (bf16[256,2048]{1,0:T(8,128)(2,1)S(1)}, bf16[256,2048]{1,0:T(8,128)(2,1)S(1)}, u32[]{:S(2)}, u32[]{:S(2)}) collective-permute-start(bf16[256,2048]{1,0:T(8,128)(2,1)S(1)} %slice.35), channel_id=1, source_target_pairs={{0,2},{1,3},{2,0},{3,1},{4,6},{5,7},{6,4},{7,5},{8,10},{9,11},{10,... | collective-permute-start | bytes 3145736 | tf_op jit(solution)/shard_map/ppermute | solution.py:51
  300.7 13.2 %collective-permute-start.33 = (bf16[128,2048]{1,0:T(8,128)(2,1)S(1)}, bf16[128,2048]{1,0:T(8,128)(2,1)S(1)}, u32[]{:S(2)}, u32[]{:S(2)}) collective-permute-start(bf16[128,2048]{1,0:T(8,128)(2,1)S(1)} %slice.37), channel_id=1, source_target_pairs={{0,4},{1,5},{2,6},{3,7},{4,0},{5,1},{6,2},{7,3},{8,12},{9,13},{10,... | collective-permute-start | bytes 1572872 | tf_op jit(solution)/shard_map/ppermute | solution.py:51
  314.1 14.0 %collective-permute-start.34 = (bf16[64,2048]{1,0:T(8,128)(2,1)S(1)}, bf16[64,2048]{1,0:T(8,128)(2,1)S(1)}, u32[]{:S(2)}, u32[]{:S(2)}) collective-permute-start(bf16[64,2048]{1,0:T(8,128)(2,1)S(1)} %slice.39), channel_id=1, source_target_pairs={{0,8},{1,9},{2,10},{3,11},{4,12},{5,13},{6,14},{7,15},{8,0},{9,1},... | collective-permute-start | bytes 786440 | tf_op jit(solution)/shard_map/ppermute | solution.py:51

commit v2 on v1

v2 whole, which is shorter than its diff:
```python
import functools

import jax
import jax.numpy as jnp
from jax import lax
from jax.experimental import pallas as pl
from jax.experimental.pallas import tpu as pltpu
from jax.sharding import PartitionSpec as P

LANES = 128


def attend(queries, new_keys, new_values, cache_keys, cache_values, cache_lengths):
    seq_count, q_heads, head_size = queries.shape
    kv_heads = cache_keys.shape[1]
    length = cache_keys.shape[2]
    groups = q_heads // kv_heads
    score_scale = head_size ** (-0.5)
    grouped = queries.reshape(seq_count, kv_heads, groups, head_size)
    scores = (
        jnp.einsum("skgd,skld->skgl", grouped, cache_keys, preferred_element_type=jnp.float32)
        * score_scale
    )
    own_score = (
        jnp.einsum("skgd,skd->skg", grouped, new_keys, preferred_element_type=jnp.float32)
        * score_scale
    )
    live_mask = (
        jnp.arange(length, dtype=jnp.int32)[None, None, None, :]
        < cache_lengths[:, None, None, None]
    )
    masked = jnp.where(live_mask, scores, -1e30)
    row_top = jnp.maximum(jnp.max(masked, axis=-1), own_score)
    cache_exp = jnp.where(live_mask, jnp.exp(masked - row_top[..., None]), 0.0)
    own_exp = jnp.exp(own_score - row_top)
    row_total = jnp.sum(cache_exp, axis=-1) + own_exp
    probs_cache = (cache_exp / row_total[..., None]).astype(jnp.bfloat16)
    probs_own = (own_exp / row_total).astype(jnp.bfloat16)
    context = jnp.einsum(
        "skgl,skld->skgd", probs_cache, cache_values, preferred_element_type=jnp.float32
    )
    context = (
        context
        + probs_own.astype(jnp.float32)[..., None] * new_values.astype(jnp.float32)[:, :, None, :]
    )
    return context.astype(jnp.bfloat16).reshape(seq_count, q_heads * head_size)


def swap_ep(x, bits):
    count = lax.axis_size("ep")
    return lax.ppermute(x, "ep", [(i, i ^ bits) for i in range(count)])


def swap_grp(x):
    return lax.ppermute(x, "grp", [(0, 1), (1, 0)])


def after(values, others):
    if not others:
        return values
    return lax.optimization_barrier((tuple(values), tuple(others)))[0]


def load_weights(places, piece_refs, weights, sems, grp):
    half = weights.shape[-1] // 2
    copies = []
    for index, (lead, part) in enumerate(places):
        tail = (slice(None),) * (len(weights.shape) - 1 - len(lead))
        if part is None:
            target = weights.at[lead + tail]
        else:
            start = pl.multiple_of((grp ^ part) * half, LANES)
            target = weights.at[lead + tail + (pl.ds(start, half),)]
        copies.append(pltpu.make_async_copy(piece_refs[index], target, sems.at[index]))
    for copy in copies:
        copy.start()
    for copy in copies:
        copy.wait()


def hidden_kernel(places, where_ref, x_ref, *refs):
    piece_refs = refs[: len(places)]
    out_ref, weights, sems = refs[len(places) :]

    @pl.when(pl.program_id(0) == 0)
    def load():
        load_weights(places, piece_refs, weights, sems, where_ref[1])

    x = x_ref[...]
    gate = jnp.dot(x, weights[0], preferred_element_type=jnp.float32)
    up = jnp.dot(x, weights[1], preferred_element_type=jnp.float32)
    out_ref[...] = (gate / (1.0 + jnp.exp(-gate)) * up).astype(jnp.bfloat16)


def down_kernel(places, experts, where_ref, hidden_ref, extra_ref, *refs):
    piece_refs = refs[: len(places)]
    out_refs, (weights, sems) = refs[len(places) : -2], refs[-2:]
    me = where_ref[0]

    @pl.when(pl.program_id(0) == 0)
    def load():
        load_weights(places, piece_refs, weights, sems, where_ref[1])

    extra = extra_ref[...].astype(jnp.float32)
    lane = lax.broadcasted_iota(jnp.int32, extra.shape, 1)
    picked = jnp.where((lane == me) | (lane == me + experts), extra, 0.0)
    coef = jnp.sum(picked, axis=1, keepdims=True)
    matrix = weights[...]
    down = lax.dot_general(
        hidden_ref[...],
        matrix.reshape(-1, matrix.shape[-1]),
        (((1,), (1,)), ((), ())),
        preferred_element_type=jnp.float32,
    )
    down = (down * coef).astype(jnp.bfloat16)
    start = 0
    for out_ref in out_refs:
        out_ref[...] = down[:, start : start + out_ref.shape[1]]
        start += out_ref.shape[1]


def call_local(kernel, grid, in_specs, out_specs, out_shape, scratch, operands, pieces):
    where = jnp.stack([lax.axis_index("ep"), lax.axis_index("grp")]).astype(jnp.int32)
    grid_spec = pltpu.PrefetchScalarGridSpec(
        num_scalar_prefetch=1,
        grid=grid,
        in_specs=in_specs + [pl.BlockSpec(memory_space=pl.ANY)] * len(pieces),
        out_specs=out_specs,
        scratch_shapes=[
            pltpu.VMEM(scratch, jnp.bfloat16),
            pltpu.SemaphoreType.DMA((len(pieces),)),
        ],
    )
    return pl.pallas_call(
        kernel,
        grid_spec=grid_spec,
        out_shape=out_shape,
        compiler_params=pltpu.CompilerParams(vmem_limit_bytes=56 * 1024 * 1024),
    )(where, *operands, *[array for _, _, array in pieces])


def run_hidden(tokens, pieces, width, ff):
    total = tokens.shape[0]
    tile = 256 if total % 256 == 0 else total
    return call_local(
        functools.partial(hidden_kernel, [p[:2] for p in pieces]),
        (total // tile,),
        [pl.BlockSpec((tile, width), lambda i, w: (i, 0))],
        pl.BlockSpec((tile, ff), lambda i, w: (i, 0)),
        jax.ShapeDtypeStruct((total, ff), jnp.bfloat16),
        (2, width, ff),
        [tokens],
        pieces,
    )


def run_down(hidden, tokens, pieces, shape, columns, experts):
    total, ff = hidden.shape
    tile = 256 if total % 256 == 0 else total
    width = sum(columns)
    extra = tokens.shape[1] - width
    return call_local(
        functools.partial(down_kernel, [p[:2] for p in pieces], experts),
        (total // tile,),
        [
            pl.BlockSpec((tile, ff), lambda i, w: (i, 0)),
            pl.BlockSpec((tile, extra), lambda i, w: (i, width // extra)),
        ],
        [pl.BlockSpec((tile, c), lambda i, w: (i, 0)) for c in columns],
        [jax.ShapeDtypeStruct((total, c), jnp.bfloat16) for c in columns],
        shape,
        [hidden, tokens],
        pieces,
    )


def fold(terms, axis, bits):
    keep = lax.index_in_dim(terms, 0, axis, keepdims=False)
    give = lax.index_in_dim(terms, 1, axis, keepdims=False)
    other = swap_ep(give, bits)
    return (keep.astype(jnp.float32) + other.astype(jnp.float32)).astype(jnp.bfloat16)


def reduce_blocks(terms, stages, order, seq_count):
    left = list(reversed(stages))
    terms = terms.reshape((2,) * len(left) + (seq_count, terms.shape[1]))
    for bits in order:
        axis = left.index(bits)
        left.pop(axis)
        terms = fold(terms, axis, bits)
    return terms


def shards(
    queries,
    new_keys,
    new_values,
    cache_keys,
    cache_values,
    cache_lengths,
    residual,
    out_weight,
    norm_gain,
    expert_ids,
    route_weights,
    learner_weights,
):
    seq_count, width = residual.shape
    experts, _, rows, ff = learner_weights.shape
    count = lax.axis_size("ep")
    parts = lax.axis_size("tp")
    grp = lax.axis_index("grp")
    stages = [1 << b for b in range(count.bit_length() - 2, -1, -1)]
    split = ff % (2 * LANES) == 0 and lax.axis_size("grp") == 2
    half = ff // 2

    def bring(matrix, low, high, halved, deps):
        start, size = (grp * half, half) if halved else (0, ff)
        block = lax.dynamic_slice(
            learner_weights, (0, matrix, low, start), (experts, 1, high - low, size)
        )[:, 0]
        (block,) = after([block], deps)
        return lax.all_to_all(block, "ep", split_axis=0, concat_axis=0, tiled=True)

    def both(lead, mine):
        if not split:
            return [(lead, None, mine)]
        return [(lead, 0, mine), (lead, 1, swap_grp(mine))]

    def arrays(pieces):
        return [array for _, _, array in pieces]

    cut = rows * 3 // 4 // 16 * 16
    size = half if split else ff
    gate = bring(0, 0, rows, split, [])

    context = attend(queries, new_keys, new_values, cache_keys, cache_values, cache_lengths)
    attn = jnp.dot(context, out_weight, preferred_element_type=jnp.float32)
    if parts > 1:
        attn = lax.psum(attn, "tp")
    stream = residual.astype(jnp.float32) + attn
    mean_square = jnp.mean(stream * stream, axis=1, keepdims=True)
    normed = (stream * lax.rsqrt(mean_square + 1e-06) * norm_gain).astype(jnp.bfloat16)

    hit = expert_ids[:, :, None] == jnp.arange(experts, dtype=jnp.int32)[None, None, :]
    coefs = jnp.sum(jnp.where(hit, route_weights[:, :, None], 0.0), axis=1)
    coarse = coefs.astype(jnp.bfloat16)
    fine = (coefs - coarse.astype(jnp.float32)).astype(jnp.bfloat16)
    pad = -(2 * experts) % LANES
    tokens = jnp.concatenate(
        [normed, coarse, fine, jnp.zeros((seq_count, pad), jnp.bfloat16)], axis=1
    )

    def gather(tokens, bits):
        return jnp.concatenate([tokens, swap_ep(tokens, bits)], axis=0)

    def gathers(tokens, todo):
        for bits in todo:
            tokens = gather(tokens, bits)
        return tokens

    rest = len(stages) - 3
    tokens = gathers(tokens, stages[:rest])
    up = bring(1, 0, rows, split, [gate, tokens])
    gate = both((0,), gate.reshape(width, size))
    tokens = gathers(tokens, stages[rest : rest + 1])
    down_a = bring(2, 0, cut, split, [up, tokens] + arrays(gate))
    up = both((1,), up.reshape(width, size))
    tokens = gathers(tokens, stages[rest + 1 : rest + 2])
    down_b = bring(2, cut, rows, False, [down_a, tokens] + arrays(up))
    down_a = both((slice(None), pl.ds(0, cut)), down_a)
    tokens = gathers(tokens, stages[rest + 2 :])

    hidden = run_hidden(tokens, gate + up, width, ff)
    near_first = stages[::-1]
    far_first = [1] + stages[-3::-1] + [2] if len(stages) > 2 else near_first
    pieces = down_a + [((slice(None), pl.ds(cut, rows - cut)), None, down_b)]
    columns = [width // 2, width - width // 2]
    terms = run_down(hidden, tokens, pieces, (count, rows, ff), columns, experts)
    totals = [
        reduce_blocks(term, stages, order, seq_count)
        for term, order in zip(terms, (near_first, far_first))
    ]
    terms = jnp.concatenate(totals, axis=1).astype(jnp.float32)
    if parts > 1:
        terms = lax.psum_scatter(terms, "tp", scatter_dimension=1, tiled=True)
        own = width // parts
        stream = lax.dynamic_slice_in_dim(stream, lax.axis_index("tp") * own, own, 1)
    return (stream + terms).astype(jnp.bfloat16)


def solution(mesh):
    return jax.shard_map(
        shards,
        mesh=mesh,
        in_specs=(
            P(("grp", "ep"), "tp", None),
            P(("grp", "ep"), "tp", None),
            P(("grp", "ep"), "tp", None),
            P(("grp", "ep"), "tp", None, None),
            P(("grp", "ep"), "tp", None, None),
            P(("grp", "ep")),
            P(("grp", "ep"), None),
            P("tp", None),
            P(),
            P(("grp", "ep"), None),
            P(("grp", "ep"), None),
            P(None, None, "ep", "tp"),
        ),
        out_specs=P(("grp", "ep"), "tp"),
        check_vma=False,
    )
```

time: 329 us -> 243 us (0.74)
  waiting for transfers between devices: 230 us -> 132 us
  starting transfers between devices: 56.5 us -> 42.3 us
  local copies, waits for them, and re-layouts: 10.2 us -> 22.7 us
  Pallas kernels: 13.8 us -> 21.5 us
    ppermute x12 -> x3, waiting for transfers between devices: 62.2 us -> 8.63 us  [swap_grp(): return lax.ppermute(x, 'grp', [(0, 1), (1, 0)])]
    ppermute x23 -> x12, waiting for transfers between devices: 168 us -> 124 us  [swap_ep(): return lax.ppermute(x, 'ep', [(i, i ^ bits) for i in range(count)])]
    ppermute x23 -> x12, starting transfers between devices: 41.2 us -> 16.1 us  [swap_ep(): return lax.ppermute(x, 'ep', [(i, i ^ bits) for i in range(count)])]
    all_to_all x0 -> x4, starting transfers between devices: none -> 21.5 us  [bring(): return lax.all_to_all(block, 'ep', split_axis=0, concat_axis=0, tiled=True)]
    ppermute x12 -> x3, starting transfers between devices: 15.3 us -> 4.75 us  [swap_grp(): return lax.ppermute(x, 'grp', [(0, 1), (1, 0)])]
    pallas_call x1 -> x2, Pallas kernels: 13.8 us -> 21.5 us  [call_local(): pl.pallas_call(kernel, grid_spec=grid_spec, out_shape=out_shape, compiler...]
    unnamed x40 -> x30, local copies, waits for them, and re-layouts: 1.66 us -> 6.28 us
    squeeze x2 -> x10, local copies, waits for them, and re-layouts: 5.36 us -> 9.07 us  [the longest x3 8.83 us: bring(): lax.dynamic_slice(learner_weights, (0, matrix, low, start), (experts, 1,...]
  transfers between devices with their start and end apart: 35 -> 19, of which waited for: 27 -> 10; matrix products, arithmetic and copies ran while one was open for 3% -> 15% of each run, Pallas kernels for 0% -> 5%
where the time goes in v2:
time: 243 us; the launch traced here: 242 us
  waiting for transfers between devices  132 us (54%)
  starting transfers between devices  42.3 us (17%)
  local copies, waits for them, and re-layouts  22.7 us (9%)
  Pallas kernels  21.5 us (9%)
  matrix products  12.7 us (5%)
  other arithmetic  9.82 us (4%)
    ppermute x12, waiting for transfers between devices, swap_ep(): return lax.ppermute(x, 'ep', [(i, i ^ bits) for i in range(count)])  124 us
    pallas_call x2, Pallas kernels, call_local(): pl.pallas_call(kernel, grid_spec=grid_spec, out_shape=out_shape, compiler...  21.5 us
    all_to_all x4, starting transfers between devices, bring(): return lax.all_to_all(block, 'ep', split_axis=0, concat_axis=0, tiled=True)  21.5 us
    ppermute x12, starting transfers between devices, swap_ep(): return lax.ppermute(x, 'ep', [(i, i ^ bits) for i in range(count)])  16.1 us
    squeeze x3, local copies, waits for them, and re-layouts, bring(): lax.dynamic_slice(learner_weights, (0, matrix, low, start), (experts, 1,...  8.83 us
    ppermute x3, waiting for transfers between devices, swap_grp(): return lax.ppermute(x, 'grp', [(0, 1), (1, 0)])  8.63 us
    unnamed x30, local copies, waits for them, and re-layouts  6.28 us
    dot_general x1, matrix products, shards(): attn = jnp.dot(context, out_weight, preferred_element_type=jnp.float32)  5.09 us
  transfers between devices with their start and end apart: 19, of which 10 were waited for; matrix products, arithmetic and copies ran while one was open for 15% of the time, Pallas kernels for 5%

profile of v2, /device:TPU:0, one launch (start us, length us, event | category | flops | bytes accessed | tf_op | source)
XLA Modules:
  0.0 241.9 jit_solution(9602173390323338202)
XLA Ops:
  0.0 4.3 %dynamic-slice_bitcast_fusion = (bf16[16,128,384]{2,1,0:T(8,128)(2,1)}, bf16[16,128,384]{2,1,0:T(8,128)(2,1)}) fusion(bf16[16,3,128,768]{3,2,1,0:T(8,128)(2,1)} %param.23, s32[]{:T(128)S(6)} %select_n.19), kind=kLoop, calls=%fused_computation.6 | loop fusion | bytes 6291460 | tf_op jit(solution)/shard_map/squeeze | solution.py:219
  4.3 7.5 %all-to-all-start = ((bf16[16,128,384]{2,1,0:T(8,128)(2,1)}), bf16[16,128,384]{2,1,0:T(8,128)(2,1)}, u32[]{:S(2)}, u32[]{:S(2)}) async-start(bf16[16,128,384]{2,1,0:T(8,128)(2,1)} %get-tuple-element.16), calls=%async_computation | async-start | bytes 3145728 | tf_op jit(solution)/shard_map/all_to_all | solution.py:223
  11.8 0.1 iota_compare_fusion.1
  12.0 4.5 %fusion.27 = (f32[64,2,8]{2,1,0:T(2,128)S(1)}, f32[64,2,8,96]{3,2,1,0:T(8,128)}) fusion(bf16[64,2,96,128]{3,2,1,0:T(8,128)(2,1)} %param.15, bf16[64,16,128]{2,1,0:T(8,128)(2,1)S(1)} %copy-done.7, pred[64,96]{1,0:T(8,128)(4,1)S(1)} %iota_compare_fusion.1), kind=kOutput, calls=%fused_computation.76 | convolution fusion | flops 25459712 | bytes 3811328 | tf_op jit(solution)/shard_map/skgd,skld->skgl/dot_general | solution.py:21
  16.5 1.0 fusion.13
  17.6 0.1 copy.36
  17.8 1.4 fusion.8
  19.3 0.6 convert_element_type.139
  19.9 0.1 copy.41
  20.1 0.1 copy.39
  20.2 0.1 copy.38
  20.3 0.8 copy.42
  21.1 2.1 fusion.3
  23.2 5.1 %multiply_reduce_fusion = (f32[64]{0:T(128)S(1)}, f32[64,2048]{1,0:T(8,128)S(1)}) fusion(bf16[2048,2048]{1,0:T(8,128)(2,1)} %param.19, bf16[8,8,16,128]{3,2,1,0:T(8,128)(2,1)S(1)} %bitcast.102, bf16[64,2048]{1,0:T(8,128)(2,1)S(1)} %copy-done.6), kind=kOutput, calls=%fused_computation.30 | convolution fusion | flops 537395136 | bytes 9437440 | tf_op jit(solution)/shard_map/dot_general | solution.py:238
  28.3 0.1 multiply_convert_fusion
  28.5 0.7 copy-done.3
  29.1 0.1 concatenate.21
  29.2 2.8 %collective-permute-start = (bf16[64,2176]{1,0:T(8,128)(2,1)S(1)}, bf16[64,2176]{1,0:T(8,128)(2,1)S(1)}, u32[]{:S(2)}, u32[]{:S(2)}) collective-permute-start(bf16[64,2176]{1,0:T(8,128)(2,1)S(1)} %concatenate.21), channel_id=1, source_target_pairs={{0,8},{1,9},{2,10},{3,11},{4,12},{5,13},{6,14},{7,15},{8,0},{9,1},... | collective-permute-start | bytes 835592 | tf_op jit(solution)/shard_map/ppermute | solution.py:51
  32.1 29.5 %collective-permute-done = bf16[64,2176]{1,0:T(8,128)(2,1)S(1)} collective-permute-done((bf16[64,2176]{1,0:T(8,128)(2,1)S(1)}, bf16[64,2176]{1,0:T(8,128)(2,1)S(1)}, u32[]{:S(2)}, u32[]{:S(2)}) %collective-permute-start) | collective-permute-done | bytes 278560 | tf_op jit(solution)/shard_map/ppermute | solution.py:51
  61.6 0.8 pad_maximum_fusion.2
  62.4 3.7 %all-to-all-start.1 = ((bf16[16,128,384]{2,1,0:T(8,128)(2,1)}), bf16[16,128,384]{2,1,0:T(8,128)(2,1)S(1)}, u32[]{:S(2)}, u32[]{:S(2)}) async-start(bf16[16,128,384]{2,1,0:T(8,128)(2,1)} %get-tuple-element.10), calls=%async_computation.1 | async-start | bytes 3145728 | tf_op jit(solution)/shard_map/all_to_all | solution.py:223
  66.1 1.6 collective-permute-start.4
  67.7 1.8 collective-permute-start.1
  69.5 36.9 %collective-permute-done.1 = bf16[128,2176]{1,0:T(8,128)(2,1)S(1)} collective-permute-done((bf16[128,2176]{1,0:T(8,128)(2,1)}, bf16[128,2176]{1,0:T(8,128)(2,1)S(1)}, u32[]{:S(2)}, u32[]{:S(2)}) %collective-permute-start.1) | collective-permute-done | bytes 557088 | tf_op jit(solution)/shard_map/ppermute | solution.py:51
  106.4 1.1 pad_maximum_fusion.1
  107.5 1.5 collective-permute-start.2
  109.1 2.5 %dynamic-slice_bitcast_fusion.2 = bf16[16,96,384]{2,1,0:T(8,128)(2,1)} fusion(bf16[16,3,128,768]{3,2,1,0:T(8,128)(2,1)} %param.23, s32[]{:T(128)S(6)} %select_n.19), kind=kLoop, calls=%fused_computation.12 | loop fusion | bytes 2359300 | tf_op jit(solution)/shard_map/squeeze | solution.py:219
  111.5 4.4 %all-to-all-start.2 = ((bf16[16,96,384]{2,1,0:T(8,128)(2,1)}), bf16[16,96,384]{2,1,0:T(8,128)(2,1)}, u32[]{:S(2)}, u32[]{:S(2)}) async-start(bf16[16,96,384]{2,1,0:T(8,128)(2,1)} %dynamic-slice_bitcast_fusion.2), calls=%async_computation.2 | async-start | bytes 2359296 | tf_op jit(solution)/shard_map/all_to_all | solution.py:223
  115.9 1.6 collective-permute-start.5
  117.5 27.3 %collective-permute-done.2 = bf16[256,2176]{1,0:T(8,128)(2,1)} collective-permute-done((bf16[256,2176]{1,0:T(8,128)(2,1)}, bf16[256,2176]{1,0:T(8,128)(2,1)}, u32[]{:S(2)}, u32[]{:S(2)}) %collective-permute-start.2) | collective-permute-done | bytes 1114144 | tf_op jit(solution)/shard_map/ppermute | solution.py:51
  144.8 2.8 %pad_maximum_fusion = bf16[512,2176]{1,0:T(8,128)(2,1)} fusion(bf16[256,2176]{1,0:T(8,128)(2,1)} %collective-permute-done.2, bf16[128,2176]{1,0:T(8,128)(2,1)S(1)} %collective-permute-done.1, bf16[64,2176]{1,0:T(8,128)(2,1)S(1)} %collective-permute-done, bf16[64,2176]{1,0:T(8,128)(2,1)S(1)} %concatenate.21), kind=kLoop, calls=%fused_computation.1 | loop fusion | flops 8912896 | bytes 4456448 | tf_op jit(solution)/shard_map/concatenate | solution.py:255
  147.6 0.7 pad_add_fusion.where_ref
  148.2 2.1 slice_bitcast_fusion
  150.3 0.8 constant_dynamic-update-slice_fusion.4
  151.1 1.5 collective-permute-done.5.refs_3_
  152.6 5.8 %all-to-all-start.3 = ((bf16[16,32,768]{2,1,0:T(8,128)(2,1)}), bf16[16,32,768]{2,1,0:T(8,128)(2,1)S(1)}, u32[]{:S(2)}, u32[]{:S(2)}) async-start(bf16[16,32,768]{2,1,0:T(8,128)(2,1)} %slice_bitcast_fusion), calls=%async_computation.3 | async-start | bytes 1572864 | tf_op jit(solution)/shard_map/all_to_all | solution.py:223
  158.4 1.6 collective-permute-start.6
  160.0 0.7 constant_dynamic-update-slice_fusion.3
  160.8 0.8 constant_dynamic-update-slice_fusion.2
  161.6 2.4 constant_dynamic-update-slice_fusion.1
  163.9 3.2 %constant_dynamic-update-slice_fusion.x_ref.extra_ref = bf16[1024,2176]{1,0:T(8,128)(2,1)} fusion(bf16[1024,2176]{1,0:T(8,128)(2,1)} %constant_dynamic-update-slice_fusion.1, bf16[512,2176]{1,0:T(8,128)(2,1)} %collective-permute-done.3), kind=kLoop, calls=%fused_computation.60 | loop fusion | bytes 4456448 | tf_op jit(solution)/shard_map/concatenate | solution.py:255
  167.2 12.8 %shard_map.118.hidden_ref = bf16[1024,768]{1,0:T(8,128)(2,1)} custom-call(s32[2]{0:T(128)} %pad_add_fusion.where_ref, bf16[1024,2176]{1,0:T(8,128)(2,1)} %constant_dynamic-update-slice_fusion.x_ref.extra_ref, bf16[2048,384]{1,0:T(8,128)(2,1)} %bitcast.6.refs_0_, bf16[2048,384]{1,0:T(8,128)(2,1)} %collective-permute-done.4.refs_1_, ...), custom_call_target="tpu_custom_call" | custom-call | tf_op jit(solution)/shard_map/pallas_call | solution.py:134
  180.0 7.1 %collective-permute-done.6.refs_1_ = bf16[16,96,384]{2,1,0:T(8,128)(2,1)} collective-permute-done((bf16[16,96,384]{2,1,0:T(8,128)(2,1)}, bf16[16,96,384]{2,1,0:T(8,128)(2,1)}, u32[]{:S(2)}, u32[]{:S(2)}) %collective-permute-start.6) | collective-permute-done | bytes 1179680 | tf_op jit(solution)/shard_map/ppermute | solution.py:55
  187.1 0.9 copy-done.5
  188.0 8.7 %shard_map.119 = (bf16[1024,1024]{1,0:T(8,128)(2,1)}, bf16[1024,1024]{1,0:T(8,128)(2,1)}) custom-call(s32[2]{0:T(128)} %pad_add_fusion.where_ref, bf16[1024,768]{1,0:T(8,128)(2,1)} %shard_map.118.hidden_ref, bf16[1024,2176]{1,0:T(8,128)(2,1)} %constant_dynamic-update-slice_fusion.x_ref.extra_ref, bf16[16,96,384]{2,1,0:T(8,128)(2,1)} %all-to-all-done.2.refs_0_, ...), custom_call_target="tpu_custom_call" | custom-call | tf_op jit(solution)/shard_map/pallas_call | solution.py:134
  196.7 2.6 %fusion.25 = (bf16[512,1024]{1,0:T(8,128)(2,1)S(1)}, bf16[512,1024]{1,0:T(8,128)(2,1)S(1)}, bf16[512,1024]{1,0:T(8,128)(2,1)S(1)}, bf16[512,1024]{1,0:T(8,128)(2,1)S(1)}) fusion(bf16[1024,1024]{1,0:T(8,128)(2,1)} %get-tuple-element.13, bf16[1024,1024]{1,0:T(8,128)(2,1)} %get-tuple-element.14), kind=kLoop, calls=%fused_computation.74 | loop fusion | bytes 8388608 | tf_op jit(solution)/shard_map/slice | solution.py:179
  199.3 0.1 copy.44
  199.5 0.5 collective-permute-start.7
  200.0 2.1 collective-permute-done.11
  202.2 0.4 fusion.1
  202.6 1.7 collective-permute-start.12
  204.3 0.4 fusion
  204.8 1.5 collective-permute-start.8
  206.3 10.3 %collective-permute-done.12 = bf16[2,2,64,1024]{3,2,0,1:T(8,128)(2,1)S(1)} collective-permute-done((bf16[2,2,64,1024]{3,2,0,1:T(8,128)(2,1)S(1)}, bf16[2,2,64,1024]{3,2,0,1:T(8,128)(2,1)S(1)}, u32[]{:S(2)}, u32[]{:S(2)}) %collective-permute-start.12) | collective-permute-done | bytes 524320 | tf_op jit(solution)/shard_map/ppermute | solution.py:51
  216.7 0.2 fusion.4
  216.9 2.6 %collective-permute-start.13 = (bf16[2,64,1024]{2,1,0:T(8,128)(2,1)S(1)}, bf16[2,64,1024]{2,1,0:T(8,128)(2,1)S(1)}, u32[]{:S(2)}, u32[]{:S(2)}) collective-permute-start(bf16[2,64,1024]{2,1,0:T(8,128)(2,1)S(1)} %slice_bitcast_fusion.5), channel_id=1, source_target_pairs={{0,8},{1,9},{2,10},{3,11},{4,12},{5,13},{6,14},{7,15},{8,0},{9,1},... | collective-permute-start | bytes 786440 | tf_op jit(solution)/shard_map/ppermute | solution.py:51
  219.5 0.2 fusion.5
  219.7 1.5 collective-permute-start.9
  221.3 9.8 %collective-permute-done.13 = bf16[2,64,1024]{2,1,0:T(8,128)(2,1)S(1)} collective-permute-done((bf16[2,64,1024]{2,1,0:T(8,128)(2,1)S(1)}, bf16[2,64,1024]{2,1,0:T(8,128)(2,1)S(1)}, u32[]{:S(2)}, u32[]{:S(2)}) %collective-permute-start.13) | collective-permute-done | bytes 262176 | tf_op jit(solution)/shard_map/ppermute | solution.py:51
  231.2 1.7 collective-permute-start.14
  233.0 0.3 collective-permute-start.10
  233.2 3.0 %collective-permute-done.14 = bf16[64,1024]{1,0:T(8,128)(2,1)S(1)} collective-permute-done((bf16[64,1024]{1,0:T(8,128)(2,1)S(1)}, bf16[64,1024]{1,0:T(8,128)(2,1)S(1)}, u32[]{:S(2)}, u32[]{:S(2)}) %collective-permute-start.14) | collective-permute-done | bytes 131104 | tf_op jit(solution)/shard_map/ppermute | solution.py:51
  236.3 4.8 %collective-permute-done.10 = bf16[64,1024]{1,0:T(8,128)(2,1)S(1)} collective-permute-done((bf16[64,1024]{1,0:T(8,128)(2,1)S(1)}, bf16[64,1024]{1,0:T(8,128)(2,1)S(1)}, u32[]{:S(2)}, u32[]{:S(2)}) %collective-permute-start.10) | collective-permute-done | bytes 131104 | tf_op jit(solution)/shard_map/ppermute | solution.py:51
  241.1 0.8 add_convert_fusion
  (55 shorter events, 0.8 us)
Async XLA Ops:
  0.0 21.1 %copy-start = (bf16[64,2,96,128]{3,2,1,0:T(8,128)(2,1)S(1)}, bf16[64,2,96,128]{3,2,1,0:T(8,128)(2,1)}, u32[]{:S(2)}) copy-start(bf16[64,2,96,128]{3,2,1,0:T(8,128)(2,1)} %param.16) | copy-start | bytes 9437188
  4.3 7.5 %copy-start.12 = (s32[64]{0:T(128)S(1)}, s32[64]{0:T(128)}, u32[]{:S(2)}) copy-start(s32[64]{0:T(128)} %param.17) | copy-start | bytes 772
  4.3 7.6 %copy-start.7 = (bf16[64,16,128]{2,1,0:T(8,128)(2,1)S(1)}, bf16[64,16,128]{2,1,0:T(8,128)(2,1)}, u32[]{:S(2)}) copy-start(bf16[64,16,128]{2,1,0:T(8,128)(2,1)} %param.12) | copy-start | bytes 786436
  4.3 58.1 %all-to-all-start = ((bf16[16,128,384]{2,1,0:T(8,128)(2,1)}), bf16[16,128,384]{2,1,0:T(8,128)(2,1)}, u32[]{:S(2)}, u32[]{:S(2)}) async-start(bf16[16,128,384]{2,1,0:T(8,128)(2,1)} %get-tuple-element.16), calls=%async_computation | async-start | bytes 3145728 | tf_op jit(solution)/shard_map/all_to_all | solution.py:223
  11.9 7.3 %copy-start.10 = (f32[64,8]{0,1:T(8,128)S(1)}, f32[64,8]{0,1:T(8,128)}, u32[]{:S(2)}) copy-start(f32[64,8]{0,1:T(8,128)} %param.22) | copy-start | bytes 6148
  11.9 7.3 %copy-start.11 = (s32[64,8]{0,1:T(8,128)S(1)}, s32[64,8]{0,1:T(8,128)}, u32[]{:S(2)}) copy-start(s32[64,8]{0,1:T(8,128)} %param.21) | copy-start | bytes 6148
  12.0 8.0 %copy-start.8 = (bf16[64,2,128]{2,1,0:T(2,128)(2,1)S(1)}, bf16[64,2,128]{2,1,0:T(2,128)(2,1)}, u32[]{:S(2)}) copy-start(bf16[64,2,128]{2,1,0:T(2,128)(2,1)} %param.14) | copy-start | bytes 98308
  21.1 2.1 copy-start.6
  23.2 5.1 %copy-start.9 = (f32[2048]{0:T(1024)S(1)}, f32[2048]{0:T(1024)}, u32[]{:S(2)}) copy-start(f32[2048]{0:T(1024)} %param.20) | copy-start | bytes 24580
  28.3 0.8 copy-start.3
  29.2 32.3 %collective-permute-start = (bf16[64,2176]{1,0:T(8,128)(2,1)S(1)}, bf16[64,2176]{1,0:T(8,128)(2,1)S(1)}, u32[]{:S(2)}, u32[]{:S(2)}) collective-permute-start(bf16[64,2176]{1,0:T(8,128)(2,1)S(1)} %concatenate.21), channel_id=1, source_target_pairs={{0,8},{1,9},{2,10},{3,11},{4,12},{5,13},{6,14},{7,15},{8,0},{9,1},... | collective-permute-start | bytes 835592 | tf_op jit(solution)/shard_map/ppermute | solution.py:51
  62.4 49.1 %all-to-all-start.1 = ((bf16[16,128,384]{2,1,0:T(8,128)(2,1)}), bf16[16,128,384]{2,1,0:T(8,128)(2,1)S(1)}, u32[]{:S(2)}, u32[]{:S(2)}) async-start(bf16[16,128,384]{2,1,0:T(8,128)(2,1)} %get-tuple-element.10), calls=%async_computation.1 | async-start | bytes 3145728 | tf_op jit(solution)/shard_map/all_to_all | solution.py:223
  66.1 45.4 %collective-permute-start.4 = (bf16[2048,384]{1,0:T(8,128)(2,1)}, bf16[2048,384]{1,0:T(8,128)(2,1)}, u32[]{:S(2)}, u32[]{:S(2)}) collective-permute-start(bf16[2048,384]{1,0:T(8,128)(2,1)} %bitcast.6.refs_0_), channel_id=1, source_target_pairs={{0,16},{16,0},{1,17},{17,1},{2,18},{18,2},{3,19},{19,3},{4,20},{20... | collective-permute-start | bytes 4718600 | tf_op jit(solution)/shard_map/ppermute | solution.py:55
  67.7 38.7 %collective-permute-start.1 = (bf16[128,2176]{1,0:T(8,128)(2,1)}, bf16[128,2176]{1,0:T(8,128)(2,1)S(1)}, u32[]{:S(2)}, u32[]{:S(2)}) collective-permute-start(bf16[128,2176]{1,0:T(8,128)(2,1)} %pad_maximum_fusion.2), channel_id=1, source_target_pairs={{0,4},{1,5},{2,6},{3,7},{4,0},{5,1},{6,2},{7,3},{8,12},{9,13},{10,... | collective-permute-start | bytes 1671176 | tf_op jit(solution)/shard_map/ppermute | solution.py:51
  107.5 37.3 %collective-permute-start.2 = (bf16[256,2176]{1,0:T(8,128)(2,1)}, bf16[256,2176]{1,0:T(8,128)(2,1)}, u32[]{:S(2)}, u32[]{:S(2)}) collective-permute-start(bf16[256,2176]{1,0:T(8,128)(2,1)} %pad_maximum_fusion.1), channel_id=1, source_target_pairs={{0,2},{1,3},{2,0},{3,1},{4,6},{5,7},{6,4},{7,5},{8,10},{9,11},{10,... | collective-permute-start | bytes 3342344 | tf_op jit(solution)/shard_map/ppermute | solution.py:51
  111.5 36.1 %copy-start.2 = (bf16[16,128,384]{2,1,0:T(8,128)(2,1)}, bf16[16,128,384]{2,1,0:T(8,128)(2,1)S(1)}, u32[]{:S(2)}) copy-start(bf16[16,128,384]{2,1,0:T(8,128)(2,1)S(1)} %all-to-all-done.1) | copy-start | bytes 4718596
  111.5 41.1 %all-to-all-start.2 = ((bf16[16,96,384]{2,1,0:T(8,128)(2,1)}), bf16[16,96,384]{2,1,0:T(8,128)(2,1)}, u32[]{:S(2)}, u32[]{:S(2)}) async-start(bf16[16,96,384]{2,1,0:T(8,128)(2,1)} %dynamic-slice_bitcast_fusion.2), calls=%async_computation.2 | async-start | bytes 2359296 | tf_op jit(solution)/shard_map/all_to_all | solution.py:223
  115.9 36.6 %collective-permute-start.5 = (bf16[2048,384]{1,0:T(8,128)(2,1)S(1)}, bf16[2048,384]{1,0:T(8,128)(2,1)}, u32[]{:S(2)}, u32[]{:S(2)}) collective-permute-start(bf16[2048,384]{1,0:T(8,128)(2,1)S(1)} %bitcast.96), channel_id=1, source_target_pairs={{0,16},{16,0},{1,17},{17,1},{2,18},{18,2},{3,19},{19,3},{4,20},{20... | collective-permute-start | bytes 4718600 | tf_op jit(solution)/shard_map/ppermute | solution.py:55
  147.6 16.4 %collective-permute-start.3 = (bf16[512,2176]{1,0:T(8,128)(2,1)}, bf16[512,2176]{1,0:T(8,128)(2,1)}, u32[]{:S(2)}, u32[]{:S(2)}) collective-permute-start(bf16[512,2176]{1,0:T(8,128)(2,1)} %pad_maximum_fusion), channel_id=1, source_target_pairs={{0,1},{1,0},{2,3},{3,2},{4,5},{5,4},{6,7},{7,6},{8,9},{9,8},{10,11... | collective-permute-start | bytes 6684680 | tf_op jit(solution)/shard_map/ppermute | solution.py:51
  152.6 34.5 %all-to-all-start.3 = ((bf16[16,32,768]{2,1,0:T(8,128)(2,1)}), bf16[16,32,768]{2,1,0:T(8,128)(2,1)S(1)}, u32[]{:S(2)}, u32[]{:S(2)}) async-start(bf16[16,32,768]{2,1,0:T(8,128)(2,1)} %slice_bitcast_fusion), calls=%async_computation.3 | async-start | bytes 1572864 | tf_op jit(solution)/shard_map/all_to_all | solution.py:223
  158.4 28.7 %collective-permute-start.6 = (bf16[16,96,384]{2,1,0:T(8,128)(2,1)}, bf16[16,96,384]{2,1,0:T(8,128)(2,1)}, u32[]{:S(2)}, u32[]{:S(2)}) collective-permute-start(bf16[16,96,384]{2,1,0:T(8,128)(2,1)} %all-to-all-done.2.refs_0_), channel_id=1, source_target_pairs={{0,16},{16,0},{1,17},{17,1},{2,18},{18,2},{3,19},{19,3},{4,20},{20... | collective-permute-start | bytes 3538952 | tf_op jit(solution)/shard_map/ppermute | solution.py:55
  187.1 0.9 copy-start.5
  199.5 2.7 %collective-permute-start.11 = (bf16[2,2,2,64,1024]{4,3,0,2,1:T(8,128)(2,1)S(1)}, bf16[2,2,2,64,1024]{4,3,0,2,1:T(8,128)(2,1)S(1)}, u32[]{:S(2)}, u32[]{:S(2)}) collective-permute-start(bf16[2,2,2,64,1024]{4,3,0,2,1:T(8,128)(2,1)S(1)} %copy.44), channel_id=1, source_target_pairs={{0,1},{1,0},{2,3},{3,2},{4,5},{5,4},{6,7},{7,6},{8,9},{9,8},{10,11... | collective-permute-start | bytes 3145736 | tf_op jit(solution)/shard_map/ppermute | solution.py:51
  199.5 4.8 %collective-permute-start.7 = (bf16[2,2,2,64,1024]{4,3,2,1,0:T(8,128)(2,1)S(1)}, bf16[2,2,2,64,1024]{4,3,2,1,0:T(8,128)(2,1)S(1)}, u32[]{:S(2)}, u32[]{:S(2)}) collective-permute-start(bf16[2,2,2,64,1024]{4,3,2,1,0:T(8,128)(2,1)S(1)} %bitcast.101), channel_id=1, source_target_pairs={{0,1},{1,0},{2,3},{3,2},{4,5},{5,4},{6,7},{7,6},{8,9},{9,8},{10,11... | collective-permute-start | bytes 3145736 | tf_op jit(solution)/shard_map/ppermute | solution.py:51
  202.6 14.0 %collective-permute-start.12 = (bf16[2,2,64,1024]{3,2,0,1:T(8,128)(2,1)S(1)}, bf16[2,2,64,1024]{3,2,0,1:T(8,128)(2,1)S(1)}, u32[]{:S(2)}, u32[]{:S(2)}) collective-permute-start(bf16[2,2,64,1024]{3,2,0,1:T(8,128)(2,1)S(1)} %slice_bitcast_fusion.1), channel_id=1, source_target_pairs={{0,4},{1,5},{2,6},{3,7},{4,0},{5,1},{6,2},{7,3},{8,12},{9,13},{10,... | collective-permute-start | bytes 1572872 | tf_op jit(solution)/shard_map/ppermute | solution.py:51
  204.8 14.7 %collective-permute-start.8 = (bf16[2,2,64,1024]{3,2,1,0:T(8,128)(2,1)S(1)}, bf16[2,2,64,1024]{3,2,1,0:T(8,128)(2,1)S(1)}, u32[]{:S(2)}, u32[]{:S(2)}) collective-permute-start(bf16[2,2,64,1024]{3,2,1,0:T(8,128)(2,1)S(1)} %slice_bitcast_fusion.3), channel_id=1, source_target_pairs={{0,2},{1,3},{2,0},{3,1},{4,6},{5,7},{6,4},{7,5},{8,10},{9,11},{10,... | collective-permute-start | bytes 1572872 | tf_op jit(solution)/shard_map/ppermute | solution.py:51
  216.9 24.2 %copy-start.4 = (f32[64,2048]{1,0:T(8,128)S(1)}, f32[64,2048]{1,0:T(8,128)}, u32[]{:S(2)}) copy-start(f32[64,2048]{1,0:T(8,128)} %copy-done.3) | copy-start | bytes 1572868
  216.9 14.2 %collective-permute-start.13 = (bf16[2,64,1024]{2,1,0:T(8,128)(2,1)S(1)}, bf16[2,64,1024]{2,1,0:T(8,128)(2,1)S(1)}, u32[]{:S(2)}, u32[]{:S(2)}) collective-permute-start(bf16[2,64,1024]{2,1,0:T(8,128)(2,1)S(1)} %slice_bitcast_fusion.5), channel_id=1, source_target_pairs={{0,8},{1,9},{2,10},{3,11},{4,12},{5,13},{6,14},{7,15},{8,0},{9,1},... | collective-permute-start | bytes 786440 | tf_op jit(solution)/shard_map/ppermute | solution.py:51
  219.5 22.4 %copy-start.1 = (bf16[64,2,96,128]{3,2,1,0:T(8,128)(2,1)S(1)}, bf16[64,2,96,128]{3,2,1,0:T(8,128)(2,1)}, u32[]{:S(2)}) copy-start(bf16[64,2,96,128]{3,2,1,0:T(8,128)(2,1)} %param.16) | copy-start | bytes 9437188
  219.7 13.2 %collective-permute-start.9 = (bf16[2,64,1024]{2,1,0:T(8,128)(2,1)S(1)}, bf16[2,64,1024]{2,1,0:T(8,128)(2,1)S(1)}, u32[]{:S(2)}, u32[]{:S(2)}) collective-permute-start(bf16[2,64,1024]{2,1,0:T(8,128)(2,1)S(1)} %slice_bitcast_fusion.7), channel_id=1, source_target_pairs={{0,4},{1,5},{2,6},{3,7},{4,0},{5,1},{6,2},{7,3},{8,12},{9,13},{10,... | collective-permute-start | bytes 786440 | tf_op jit(solution)/shard_map/ppermute | solution.py:51
  231.2 5.0 %collective-permute-start.14 = (bf16[64,1024]{1,0:T(8,128)(2,1)S(1)}, bf16[64,1024]{1,0:T(8,128)(2,1)S(1)}, u32[]{:S(2)}, u32[]{:S(2)}) collective-permute-start(bf16[64,1024]{1,0:T(8,128)(2,1)S(1)} %slice_bitcast_fusion.9), channel_id=1, source_target_pairs={{0,2},{1,3},{2,0},{3,1},{4,6},{5,7},{6,4},{7,5},{8,10},{9,11},{10,... | collective-permute-start | bytes 393224 | tf_op jit(solution)/shard_map/ppermute | solution.py:51
  233.0 8.1 %collective-permute-start.10 = (bf16[64,1024]{1,0:T(8,128)(2,1)S(1)}, bf16[64,1024]{1,0:T(8,128)(2,1)S(1)}, u32[]{:S(2)}, u32[]{:S(2)}) collective-permute-start(bf16[64,1024]{1,0:T(8,128)(2,1)S(1)} %slice_bitcast_fusion.11), channel_id=1, source_target_pairs={{0,8},{1,9},{2,10},{3,11},{4,12},{5,13},{6,14},{7,15},{8,0},{9,1},... | collective-permute-start | bytes 393224 | tf_op jit(solution)/shard_map/ppermute | solution.py:51

commit v3 on v2

--- a/solution.py
+++ b/solution.py
@@ -64,47 +64,56 @@
 def load_weights(places, piece_refs, weights, sems, grp):
     half = weights.shape[-1] // 2
     copies = []
-    for index, (lead, part) in enumerate(places):
+    for index, (source, lead, part) in enumerate(places):
+        piece = piece_refs[index]
+        if source is not None:
+            piece = piece.at[source]
         tail = (slice(None),) * (len(weights.shape) - 1 - len(lead))
         if part is None:
             target = weights.at[lead + tail]
         else:
             start = pl.multiple_of((grp ^ part) * half, LANES)
             target = weights.at[lead + tail + (pl.ds(start, half),)]
-        copies.append(pltpu.make_async_copy(piece_refs[index], target, sems.at[index]))
+        copies.append(pltpu.make_async_copy(piece, target, sems.at[index]))
     for copy in copies:
         copy.start()
     for copy in copies:
         copy.wait()
 
 
-def hidden_kernel(places, where_ref, x_ref, *refs):
+def hidden_kernel(places, experts, where_ref, x_ref, *refs):
     piece_refs = refs[: len(places)]
     out_ref, weights, sems = refs[len(places) :]
+    me = where_ref[0]
 
     @pl.when(pl.program_id(0) == 0)
     def load():
         load_weights(places, piece_refs, weights, sems, where_ref[1])
 
-    x = x_ref[...]
-    gate = jnp.dot(x, weights[0], preferred_element_type=jnp.float32)
-    up = jnp.dot(x, weights[1], preferred_element_type=jnp.float32)
-    out_ref[...] = (gate / (1.0 + jnp.exp(-gate)) * up).astype(jnp.bfloat16)
-
-
-def down_kernel(places, experts, where_ref, hidden_ref, extra_ref, *refs):
-    piece_refs = refs[: len(places)]
-    out_refs, (weights, sems) = refs[len(places) : -2], refs[-2:]
-    me = where_ref[0]
-
-    @pl.when(pl.program_id(0) == 0)
-    def load():
-        load_weights(places, piece_refs, weights, sems, where_ref[1])
-
-    extra = extra_ref[...].astype(jnp.float32)
+    width = weights.shape[1]
+    extra = x_ref[:, width:].astype(jnp.float32)
     lane = lax.broadcasted_iota(jnp.int32, extra.shape, 1)
     picked = jnp.where((lane == me) | (lane == me + experts), extra, 0.0)
     coef = jnp.sum(picked, axis=1, keepdims=True)
+    x = x_ref[:, :width]
+    gate = jnp.dot(x, weights[0], preferred_element_type=jnp.float32)
+    up = jnp.dot(x, weights[1], preferred_element_type=jnp.float32)
+    out_ref[...] = (gate / (1.0 + jnp.exp(-gate)) * up * coef).astype(jnp.bfloat16)
+
+
+def down_kernel(places, where_ref, hidden_ref, *refs):
+    piece_refs = refs[: len(places)]
+    out_refs, weights = refs[len(places) : -1], refs[-1]
+    grp = where_ref[1]
+    step = pl.program_id(0)
+    half = weights.shape[-1] // 2
+    for ref, (low, part) in zip(piece_refs, places):
+        span = slice(low, low + ref.shape[1])
+        if part is None:
+            weights[:, span, :] = ref[...]
+        else:
+            start = pl.multiple_of((grp ^ part) * half, LANES)
+            weights[:, span, pl.ds(start, half)] = ref[...]
     matrix = weights[...]
     down = lax.dot_general(
         hidden_ref[...],
@@ -112,11 +121,15 @@
         (((1,), (1,)), ((), ())),
         preferred_element_type=jnp.float32,
     )
-    down = (down * coef).astype(jnp.bfloat16)
-    start = 0
-    for out_ref in out_refs:
-        out_ref[...] = down[:, start : start + out_ref.shape[1]]
-        start += out_ref.shape[1]
+    down = down.astype(jnp.bfloat16)
+    size = out_refs[0].shape[0]
+    turn = pl.num_programs(0) // 2
+    for column in range(2):
+
+        @pl.when((step >= turn) == (column == 1))
+        def store(column=column):
+            out_refs[2 * column][...] = down[:size]
+            out_refs[2 * column + 1][...] = down[size:]
 
 
 def call_local(kernel, grid, in_specs, out_specs, out_shape, scratch, operands, pieces):
@@ -136,16 +149,16 @@
         grid_spec=grid_spec,
         out_shape=out_shape,
         compiler_params=pltpu.CompilerParams(vmem_limit_bytes=56 * 1024 * 1024),
-    )(where, *operands, *[array for _, _, array in pieces])
-
-
-def run_hidden(tokens, pieces, width, ff):
+    )(where, *operands, *[piece[3] for piece in pieces])
+
+
+def run_hidden(tokens, pieces, width, ff, experts):
     total = tokens.shape[0]
     tile = 256 if total % 256 == 0 else total
     return call_local(
-        functools.partial(hidden_kernel, [p[:2] for p in pieces]),
+        functools.partial(hidden_kernel, [p[:3] for p in pieces], experts),
         (total // tile,),
-        [pl.BlockSpec((tile, width), lambda i, w: (i, 0))],
+        [pl.BlockSpec((tile, tokens.shape[1]), lambda i, w: (i, 0))],
         pl.BlockSpec((tile, ff), lambda i, w: (i, 0)),
         jax.ShapeDtypeStruct((total, ff), jnp.bfloat16),
         (2, width, ff),
@@ -154,35 +167,42 @@
     )
 
 
-def run_down(hidden, tokens, pieces, shape, columns, experts):
+def run_down(hidden, pieces, count, rows, width):
     total, ff = hidden.shape
-    tile = 256 if total % 256 == 0 else total
-    width = sum(columns)
-    extra = tokens.shape[1] - width
-    return call_local(
-        functools.partial(down_kernel, [p[:2] for p in pieces], experts),
-        (total // tile,),
-        [
-            pl.BlockSpec((tile, ff), lambda i, w: (i, 0)),
-            pl.BlockSpec((tile, extra), lambda i, w: (i, width // extra)),
-        ],
-        [pl.BlockSpec((tile, c), lambda i, w: (i, 0)) for c in columns],
-        [jax.ShapeDtypeStruct((total, c), jnp.bfloat16) for c in columns],
-        shape,
-        [hidden, tokens],
-        pieces,
-    )
+    block = min(max(4, 4 * LANES // rows), count // 2)
+    steps = count // block
+    where = jnp.stack([lax.axis_index("ep"), lax.axis_index("grp")]).astype(jnp.int32)
+    spec = (total // 2, block * rows)
+    low = pl.BlockSpec(spec, lambda i, w: (0, jnp.minimum(i, steps // 2 - 1)))
+    high = pl.BlockSpec(spec, lambda i, w: (0, jnp.maximum(i - steps // 2, 0)))
+    grid_spec = pltpu.PrefetchScalarGridSpec(
+        num_scalar_prefetch=1,
+        grid=(steps,),
+        in_specs=[pl.BlockSpec((total, ff), lambda i, w: (0, 0))]
+        + [pl.BlockSpec((block,) + p[3].shape[1:], lambda i, w: (i, 0, 0)) for p in pieces],
+        out_specs=[low, low, high, high],
+        scratch_shapes=[pltpu.VMEM((block, rows, ff), jnp.bfloat16)],
+    )
+    return pl.pallas_call(
+        functools.partial(down_kernel, [p[1:3] for p in pieces]),
+        grid_spec=grid_spec,
+        out_shape=[jax.ShapeDtypeStruct((total // 2, width // 2), jnp.bfloat16)] * 4,
+        compiler_params=pltpu.CompilerParams(vmem_limit_bytes=56 * 1024 * 1024),
+    )(where, hidden, *[piece[3] for piece in pieces])
+
+
+def add_terms(mine, other):
+    return (mine.astype(jnp.float32) + other.astype(jnp.float32)).astype(jnp.bfloat16)
 
 
 def fold(terms, axis, bits):
     keep = lax.index_in_dim(terms, 0, axis, keepdims=False)
     give = lax.index_in_dim(terms, 1, axis, keepdims=False)
-    other = swap_ep(give, bits)
-    return (keep.astype(jnp.float32) + other.astype(jnp.float32)).astype(jnp.bfloat16)
-
-
-def reduce_blocks(terms, stages, order, seq_count):
-    left = list(reversed(stages))
+    return add_terms(keep, swap_ep(give, bits))
+
+
+def reduce_blocks(terms, left, order, seq_count):
+    left = list(left)
     terms = terms.reshape((2,) * len(left) + (seq_count, terms.shape[1]))
     for bits in order:
         axis = left.index(bits)
@@ -214,25 +234,33 @@
     split = ff % (2 * LANES) == 0 and lax.axis_size("grp") == 2
     half = ff // 2
 
-    def bring(matrix, low, high, halved, deps):
-        start, size = (grp * half, half) if halved else (0, ff)
-        block = lax.dynamic_slice(
+    def cut_out(matrix, low, high, halved, start):
+        start, size = (start, half) if halved else (0, ff)
+        return lax.dynamic_slice(
             learner_weights, (0, matrix, low, start), (experts, 1, high - low, size)
         )[:, 0]
+
+    def bring(block, deps):
         (block,) = after([block], deps)
         return lax.all_to_all(block, "ep", split_axis=0, concat_axis=0, tiled=True)
 
     def both(lead, mine):
         if not split:
-            return [(lead, None, mine)]
-        return [(lead, 0, mine), (lead, 1, swap_grp(mine))]
+            return [(None, lead, None, mine)]
+        return [(None, lead, 0, mine), (None, lead, 1, swap_grp(mine))]
 
     def arrays(pieces):
-        return [array for _, _, array in pieces]
+        return [piece[3] for piece in pieces]
 
     cut = rows * 3 // 4 // 16 * 16
     size = half if split else ff
-    gate = bring(0, 0, rows, split, [])
+    gate_block = cut_out(0, 0, rows, split, grp * half)
+    (start,) = after([grp * half], [gate_block])
+    up_block = cut_out(1, 0, rows, split, start)
+    down_a_block = cut_out(2, 0, cut, split, start)
+    down_b_block = cut_out(2, cut, rows, False, start)
+    gate = bring(gate_block, [])
+    (gate,) = after([gate], [up_block, down_a_block, down_b_block])
 
     context = attend(queries, new_keys, new_values, cache_keys, cache_values, cache_lengths)
     attn = jnp.dot(context, out_weight, preferred_element_type=jnp.float32)
@@ -252,34 +280,32 @@
     )
 
     def gather(tokens, bits):
-        return jnp.concatenate([tokens, swap_ep(tokens, bits)], axis=0)
-
-    def gathers(tokens, todo):
-        for bits in todo:
-            tokens = gather(tokens, bits)
-        return tokens
+        other = swap_ep(tokens, bits)
+        return jnp.concatenate([tokens, other], axis=0), other
 
     rest = len(stages) - 3
-    tokens = gathers(tokens, stages[:rest])
-    up = bring(1, 0, rows, split, [gate, tokens])
+    for bits in stages[:rest]:
+        tokens, other = gather(tokens, bits)
+    up = bring(up_block, [gate, other])
     gate = both((0,), gate.reshape(width, size))
-    tokens = gathers(tokens, stages[rest : rest + 1])
-    down_a = bring(2, 0, cut, split, [up, tokens] + arrays(gate))
+    tokens, other = gather(tokens, stages[rest])
+    down_a = bring(down_a_block, [up, other] + arrays(gate))
     up = both((1,), up.reshape(width, size))
-    tokens = gathers(tokens, stages[rest + 1 : rest + 2])
-    down_b = bring(2, cut, rows, False, [down_a, tokens] + arrays(up))
-    down_a = both((slice(None), pl.ds(0, cut)), down_a)
-    tokens = gathers(tokens, stages[rest + 2 :])
-
-    hidden = run_hidden(tokens, gate + up, width, ff)
-    near_first = stages[::-1]
-    far_first = [1] + stages[-3::-1] + [2] if len(stages) > 2 else near_first
-    pieces = down_a + [((slice(None), pl.ds(cut, rows - cut)), None, down_b)]
-    columns = [width // 2, width - width // 2]
-    terms = run_down(hidden, tokens, pieces, (count, rows, ff), columns, experts)
+    tokens, other = gather(tokens, stages[rest + 1])
+    down_b = bring(down_b_block, [down_a, other] + arrays(up))
+    down_a = both(0, down_a)
+    tokens, _ = gather(tokens, stages[rest + 2])
+
+    hidden = run_hidden(tokens, gate + up, width, ff, experts)
+    lower = stages[-2::-1]
+    orders = (lower, lower[1:] + lower[:1])
+    pieces = down_a + [(None, cut, None, down_b)]
+    products = run_down(hidden, pieces, count, rows, width)
+    kept = products[0::2]
+    given = [swap_ep(give, 1) for give in products[1::2]]
     totals = [
-        reduce_blocks(term, stages, order, seq_count)
-        for term, order in zip(terms, (near_first, far_first))
+        reduce_blocks(add_terms(terms, other), lower, order, seq_count)
+        for terms, other, order in zip(kept, given, orders)
     ]
     terms = jnp.concatenate(totals, axis=1).astype(jnp.float32)
     if parts > 1:

time: 243 us -> 237 us (0.975)
  waiting for transfers between devices: 132 us -> 127 us
    ppermute x12, waiting for transfers between devices: 124 us -> 108 us  [swap_ep(): return lax.ppermute(x, 'ep', [(i, i ^ bits) for i in range(count)])]
    all_to_all x4, waiting for transfers between devices: 0.01 us -> 9.97 us  [bring(): return lax.all_to_all(block, 'ep', split_axis=0, concat_axis=0, tiled=True)]
    pallas_call x0 -> x1, Pallas kernels: none -> 8.97 us  [run_down(): pl.pallas_call(functools.partial(down_kernel, [p[1:3] for p in pieces]),...]
    pallas_call x2 -> x1, Pallas kernels: 21.5 us -> 12.9 us  [call_local(): pl.pallas_call(kernel, grid_spec=grid_spec, out_shape=out_shape, compiler...]
    squeeze x3 -> x4, local copies, waits for them, and re-layouts: 8.83 us -> 11.5 us  [cut_out(): lax.dynamic_slice(learner_weights, (0, matrix, low, start), (experts, 1,...]
    slice x1, local copies, waits for them, and re-layouts: 2.62 us -> 0.07 us  [fold(): give = lax.index_in_dim(terms, 1, axis, keepdims=False)]
    unnamed x30 -> x33, local copies, waits for them, and re-layouts: 6.28 us -> 6.26 us
  transfers between devices with their start and end apart: 19 -> 19, of which waited for: 10 -> 11; matrix products, arithmetic and copies ran while one was open for 15% -> 17% of each run, Pallas kernels for 5% -> 5%
where the time goes in v3:
time: 237 us; the launch traced here: 236 us
  waiting for transfers between devices  127 us (54%)
  starting transfers between devices  42.4 us (18%)
  local copies, waits for them, and re-layouts  22 us (9%)
  Pallas kernels  21.8 us (9%)
  matrix products  12.7 us (5%)
  other arithmetic  10.3 us (4%)
    ppermute x12, waiting for transfers between devices, swap_ep(): return lax.ppermute(x, 'ep', [(i, i ^ bits) for i in range(count)])  108 us
    all_to_all x4, starting transfers between devices, bring(): return lax.all_to_all(block, 'ep', split_axis=0, concat_axis=0, tiled=True)  21.5 us
    ppermute x12, starting transfers between devices, swap_ep(): return lax.ppermute(x, 'ep', [(i, i ^ bits) for i in range(count)])  16.2 us
    pallas_call x1, Pallas kernels, call_local(): pl.pallas_call(kernel, grid_spec=grid_spec, out_shape=out_shape, compiler...  12.9 us
    squeeze x4, local copies, waits for them, and re-layouts, cut_out(): lax.dynamic_slice(learner_weights, (0, matrix, low, start), (experts, 1,...  11.5 us
    all_to_all x4, waiting for transfers between devices, bring(): return lax.all_to_all(block, 'ep', split_axis=0, concat_axis=0, tiled=True)  9.97 us
    pallas_call x1, Pallas kernels, run_down(): pl.pallas_call(functools.partial(down_kernel, [p[1:3] for p in pieces]),...  8.97 us
    ppermute x3, waiting for transfers between devices, swap_grp(): return lax.ppermute(x, 'grp', [(0, 1), (1, 0)])  8.21 us
  transfers between devices with their start and end apart: 19, of which 11 were waited for; matrix products, arithmetic and copies ran while one was open for 17% of the time, Pallas kernels for 5%

profile of v3, /device:TPU:0, one launch (start us, length us, event | category | flops | bytes accessed | tf_op | source)
XLA Modules:
  0.0 236.3 jit_solution(8402958120058191640)
XLA Ops:
  0.0 3.0 %dynamic-slice_bitcast_fusion.1 = bf16[16,128,384]{2,1,0:T(8,128)(2,1)} fusion(bf16[16,3,128,768]{3,2,1,0:T(8,128)(2,1)} %param.23, s32[]{:T(128)S(6)} %select_n.21), kind=kLoop, calls=%fused_computation.5 | loop fusion | bytes 3145732 | tf_op jit(solution)/shard_map/squeeze | solution.py:239
  3.0 7.5 %all-to-all-start = ((bf16[16,128,384]{2,1,0:T(8,128)(2,1)}), bf16[16,128,384]{2,1,0:T(8,128)(2,1)}, u32[]{:S(2)}, u32[]{:S(2)}) async-start(bf16[16,128,384]{2,1,0:T(8,128)(2,1)} %dynamic-slice_bitcast_fusion.1), calls=%async_computation | async-start | bytes 3145728 | tf_op jit(solution)/shard_map/all_to_all | solution.py:245
  10.6 0.1 copy.38
  10.7 0.1 iota_compare_fusion.1
  10.8 0.7 convert_element_type.130
  11.5 4.5 %fusion.25 = (f32[64,2,8]{2,1,0:T(2,128)S(1)}, f32[64,2,8,96]{3,2,1,0:T(8,128)}) fusion(bf16[64,2,96,128]{3,2,1,0:T(8,128)(2,1)} %param.15, bf16[64,16,128]{2,1,0:T(8,128)(2,1)S(1)} %copy-done.8, pred[64,96]{1,0:T(8,128)(4,1)S(1)} %iota_compare_fusion.1), kind=kOutput, calls=%fused_computation.72 | convolution fusion | flops 25459712 | bytes 3811328 | tf_op jit(solution)/shard_map/skgd,skld->skgl/dot_general | solution.py:21
  16.0 1.0 fusion.11
  17.1 0.1 copy.33
  17.2 1.4 fusion.6
  18.8 0.1 copy.36
  18.9 0.1 copy.35
  19.0 0.1 copy.39
  19.1 2.1 fusion.1
  21.2 5.1 %multiply_reduce_fusion = (f32[64]{0:T(128)S(1)}, f32[64,2048]{1,0:T(8,128)S(1)}) fusion(bf16[2048,2048]{1,0:T(8,128)(2,1)} %param.19, bf16[8,8,16,128]{3,2,1,0:T(8,128)(2,1)S(1)} %bitcast.92, bf16[64,2048]{1,0:T(8,128)(2,1)S(1)} %copy-done.7), kind=kOutput, calls=%fused_computation.26 | convolution fusion | flops 537395136 | bytes 9437440 | tf_op jit(solution)/shard_map/dot_general | solution.py:266
  26.4 0.1 multiply_convert_fusion
  26.5 0.6 copy-done.3
  27.1 0.1 concatenate.21
  27.2 2.8 %collective-permute-start = (bf16[64,2176]{1,0:T(8,128)(2,1)S(1)}, bf16[64,2176]{1,0:T(8,128)(2,1)S(1)}, u32[]{:S(2)}, u32[]{:S(2)}) collective-permute-start(bf16[64,2176]{1,0:T(8,128)(2,1)S(1)} %concatenate.21), channel_id=1, source_target_pairs={{0,8},{1,9},{2,10},{3,11},{4,12},{5,13},{6,14},{7,15},{8,0},{9,1},... | collective-permute-start | bytes 835592 | tf_op jit(solution)/shard_map/ppermute | solution.py:51
  30.1 3.5 %dynamic-slice_bitcast_fusion = bf16[16,128,384]{2,1,0:T(8,128)(2,1)} fusion(bf16[16,3,128,768]{3,2,1,0:T(8,128)(2,1)} %param.23, s32[]{:T(128)S(6)} %select_n.22), kind=kLoop, calls=%fused_computation.4 | loop fusion | bytes 3145732 | tf_op jit(solution)/shard_map/squeeze | solution.py:239
  33.6 3.0 %dynamic-slice_bitcast_fusion.2 = bf16[16,96,384]{2,1,0:T(8,128)(2,1)} fusion(bf16[16,3,128,768]{3,2,1,0:T(8,128)(2,1)} %param.23, s32[]{:T(128)S(6)} %select_n.22), kind=kLoop, calls=%fused_computation.10 | loop fusion | bytes 2359300 | tf_op jit(solution)/shard_map/squeeze | solution.py:239
  36.5 2.1 slice_bitcast_fusion
  38.6 10.0 %all-to-all-done = bf16[16,128,384]{2,1,0:T(8,128)(2,1)} async-done(((bf16[16,128,384]{2,1,0:T(8,128)(2,1)}), bf16[16,128,384]{2,1,0:T(8,128)(2,1)}, u32[]{:S(2)}, u32[]{:S(2)}) %all-to-all-start) | async-done | bytes 1572896 | tf_op jit(solution)/shard_map/all_to_all | solution.py:245
  48.6 11.7 %collective-permute-done = bf16[64,2176]{1,0:T(8,128)(2,1)S(1)} collective-permute-done((bf16[64,2176]{1,0:T(8,128)(2,1)S(1)}, bf16[64,2176]{1,0:T(8,128)(2,1)S(1)}, u32[]{:S(2)}, u32[]{:S(2)}) %collective-permute-start) | collective-permute-done | bytes 278560 | tf_op jit(solution)/shard_map/ppermute | solution.py:51
  60.3 3.7 %all-to-all-start.1 = ((bf16[16,128,384]{2,1,0:T(8,128)(2,1)}), bf16[16,128,384]{2,1,0:T(8,128)(2,1)S(1)}, u32[]{:S(2)}, u32[]{:S(2)}) async-start(bf16[16,128,384]{2,1,0:T(8,128)(2,1)} %dynamic-slice_bitcast_fusion), calls=%async_computation.1 | async-start | bytes 3145728 | tf_op jit(solution)/shard_map/all_to_all | solution.py:245
  64.0 1.6 collective-permute-start.4
  65.6 1.9 collective-permute-start.1
  67.6 36.8 %collective-permute-done.1 = bf16[128,2176]{1,0:T(8,128)(2,1)S(1)} collective-permute-done((bf16[128,2176]{1,0:T(8,128)(2,1)S(1)}, bf16[128,2176]{1,0:T(8,128)(2,1)S(1)}, u32[]{:S(2)}, u32[]{:S(2)}) %collective-permute-start.1) | collective-permute-done | bytes 557088 | tf_op jit(solution)/shard_map/ppermute | solution.py:51
  104.3 1.1 pad_maximum_fusion.1
  105.4 1.5 collective-permute-start.2
  107.0 4.4 %all-to-all-start.2 = ((bf16[16,96,384]{2,1,0:T(8,128)(2,1)}), bf16[16,96,384]{2,1,0:T(8,128)(2,1)}, u32[]{:S(2)}, u32[]{:S(2)}) async-start(bf16[16,96,384]{2,1,0:T(8,128)(2,1)} %dynamic-slice_bitcast_fusion.2), calls=%async_computation.2 | async-start | bytes 2359296 | tf_op jit(solution)/shard_map/all_to_all | solution.py:245
  111.4 1.6 collective-permute-start.5
  113.0 29.8 %collective-permute-done.2 = bf16[256,2176]{1,0:T(8,128)(2,1)} collective-permute-done((bf16[256,2176]{1,0:T(8,128)(2,1)}, bf16[256,2176]{1,0:T(8,128)(2,1)}, u32[]{:S(2)}, u32[]{:S(2)}) %collective-permute-start.2) | collective-permute-done | bytes 1114144 | tf_op jit(solution)/shard_map/ppermute | solution.py:51
  142.7 2.8 %pad_maximum_fusion = bf16[512,2176]{1,0:T(8,128)(2,1)} fusion(bf16[256,2176]{1,0:T(8,128)(2,1)} %collective-permute-done.2, bf16[128,2176]{1,0:T(8,128)(2,1)S(1)} %collective-permute-done.1, bf16[64,2176]{1,0:T(8,128)(2,1)S(1)} %collective-permute-done, bf16[64,2176]{1,0:T(8,128)(2,1)S(1)} %concatenate.21), kind=kLoop, calls=%fused_computation.1 | loop fusion | flops 8912896 | bytes 4456448 | tf_op jit(solution)/shard_map/concatenate | solution.py:284
  145.5 0.7 pad_add_fusion.where_ref
  146.2 0.7 constant_dynamic-update-slice_fusion.4
  146.9 1.1 collective-permute-done.5.refs_3_
  148.0 5.8 %all-to-all-start.3 = ((bf16[16,32,768]{2,1,0:T(8,128)(2,1)}), bf16[16,32,768]{2,1,0:T(8,128)(2,1)S(1)}, u32[]{:S(2)}, u32[]{:S(2)}) async-start(bf16[16,32,768]{2,1,0:T(8,128)(2,1)} %slice_bitcast_fusion), calls=%async_computation.3 | async-start | bytes 1572864 | tf_op jit(solution)/shard_map/all_to_all | solution.py:245
  153.9 1.6 collective-permute-start.6
  155.4 0.7 constant_dynamic-update-slice_fusion.3
  156.2 0.9 constant_dynamic-update-slice_fusion.2
  157.0 2.3 constant_dynamic-update-slice_fusion.1
  159.4 3.2 %constant_dynamic-update-slice_fusion.x_ref = bf16[1024,2176]{1,0:T(8,128)(2,1)} fusion(bf16[1024,2176]{1,0:T(8,128)(2,1)} %constant_dynamic-update-slice_fusion.1, bf16[512,2176]{1,0:T(8,128)(2,1)} %collective-permute-done.3), kind=kLoop, calls=%fused_computation.56 | loop fusion | bytes 4456448 | tf_op jit(solution)/shard_map/concatenate | solution.py:284
  162.5 12.9 %shard_map.118.hidden_ref = bf16[1024,768]{1,0:T(8,128)(2,1)} custom-call(s32[2]{0:T(128)} %pad_add_fusion.where_ref, bf16[1024,2176]{1,0:T(8,128)(2,1)} %constant_dynamic-update-slice_fusion.x_ref, bf16[2048,384]{1,0:T(8,128)(2,1)} %bitcast.9.refs_0_, bf16[2048,384]{1,0:T(8,128)(2,1)} %collective-permute-done.4.refs_1_, bf16[2048,384]{1,0:T(8,128)(2,1)} %bitcast.89, ...), custom_call_target="tpu_custom_call" | custom-call | tf_op jit(solution)/shard_map/pallas_call | solution.py:147
  175.4 7.1 %collective-permute-done.6.refs_1_ = bf16[16,96,384]{2,1,0:T(8,128)(2,1)} collective-permute-done((bf16[16,96,384]{2,1,0:T(8,128)(2,1)}, bf16[16,96,384]{2,1,0:T(8,128)(2,1)}, u32[]{:S(2)}, u32[]{:S(2)}) %collective-permute-start.6) | collective-permute-done | bytes 1179680 | tf_op jit(solution)/shard_map/ppermute | solution.py:55
  182.5 0.9 copy-done.5
  183.5 9.0 %shard_map.119 = (bf16[512,1024]{1,0:T(8,128)(2,1)}, bf16[512,1024]{1,0:T(8,128)(2,1)}, bf16[512,1024]{1,0:T(8,128)(2,1)}, bf16[512,1024]{1,0:T(8,128)(2,1)}) custom-call(s32[2]{0:T(128)} %pad_add_fusion.where_ref, bf16[1024,768]{1,0:T(8,128)(2,1)} %shard_map.118.hidden_ref, bf16[16,96,384]{2,1,0:T(8,128)(2,1)} %all-to-all-done.2.refs_0_, ...), custom_call_target="tpu_custom_call" | custom-call | tf_op jit(solution)/shard_map/pallas_call | solution.py:186
  192.4 0.5 collective-permute-start.7
  192.9 2.4 collective-permute-done.11
  195.3 1.6 add_convert_fusion
  196.9 0.1 fusion.24
  197.1 1.7 collective-permute-start.12
  198.8 0.4 add_convert_fusion.1
  199.2 1.5 collective-permute-start.8
  200.8 10.3 %collective-permute-done.12 = bf16[2,2,64,1024]{3,2,0,1:T(8,128)(2,1)S(1)} collective-permute-done((bf16[2,2,64,1024]{3,2,0,1:T(8,128)(2,1)S(1)}, bf16[2,2,64,1024]{3,2,0,1:T(8,128)(2,1)S(1)}, u32[]{:S(2)}, u32[]{:S(2)}) %collective-permute-start.12) | collective-permute-done | bytes 524320 | tf_op jit(solution)/shard_map/ppermute | solution.py:51
  211.1 0.2 fusion.2
  211.3 2.6 %collective-permute-start.13 = (bf16[2,64,1024]{2,1,0:T(8,128)(2,1)S(1)}, bf16[2,64,1024]{2,1,0:T(8,128)(2,1)S(1)}, u32[]{:S(2)}, u32[]{:S(2)}) collective-permute-start(bf16[2,64,1024]{2,1,0:T(8,128)(2,1)S(1)} %slice_bitcast_fusion.1), channel_id=1, source_target_pairs={{0,8},{1,9},{2,10},{3,11},{4,12},{5,13},{6,14},{7,15},{8,0},{9,1},... | collective-permute-start | bytes 786440 | tf_op jit(solution)/shard_map/ppermute | solution.py:51
  213.9 0.2 fusion.3
  214.1 1.5 collective-permute-start.9
  215.7 9.8 %collective-permute-done.13 = bf16[2,64,1024]{2,1,0:T(8,128)(2,1)S(1)} collective-permute-done((bf16[2,64,1024]{2,1,0:T(8,128)(2,1)S(1)}, bf16[2,64,1024]{2,1,0:T(8,128)(2,1)S(1)}, u32[]{:S(2)}, u32[]{:S(2)}) %collective-permute-start.13) | collective-permute-done | bytes 262176 | tf_op jit(solution)/shard_map/ppermute | solution.py:51
  225.6 1.7 collective-permute-start.14
  227.4 0.3 collective-permute-start.10
  227.7 2.9 %collective-permute-done.14 = bf16[64,1024]{1,0:T(8,128)(2,1)S(1)} collective-permute-done((bf16[64,1024]{1,0:T(8,128)(2,1)S(1)}, bf16[64,1024]{1,0:T(8,128)(2,1)S(1)}, u32[]{:S(2)}, u32[]{:S(2)}) %collective-permute-start.14) | collective-permute-done | bytes 131104 | tf_op jit(solution)/shard_map/ppermute | solution.py:51
  230.7 4.8 %collective-permute-done.10 = bf16[64,1024]{1,0:T(8,128)(2,1)S(1)} collective-permute-done((bf16[64,1024]{1,0:T(8,128)(2,1)S(1)}, bf16[64,1024]{1,0:T(8,128)(2,1)S(1)}, u32[]{:S(2)}, u32[]{:S(2)}) %collective-permute-start.10) | collective-permute-done | bytes 131104 | tf_op jit(solution)/shard_map/ppermute | solution.py:51
  235.5 0.8 add_convert_fusion.2
  (57 shorter events, 0.8 us)
Async XLA Ops:
  0.0 19.1 %copy-start = (bf16[64,2,96,128]{3,2,1,0:T(8,128)(2,1)S(1)}, bf16[64,2,96,128]{3,2,1,0:T(8,128)(2,1)}, u32[]{:S(2)}) copy-start(bf16[64,2,96,128]{3,2,1,0:T(8,128)(2,1)} %param.16) | copy-start | bytes 9437188
  3.0 7.6 %copy-start.11 = (f32[64,8]{0,1:T(8,128)S(1)}, f32[64,8]{0,1:T(8,128)}, u32[]{:S(2)}) copy-start(f32[64,8]{0,1:T(8,128)} %param.22) | copy-start | bytes 6148
  3.0 7.6 %copy-start.12 = (s32[64,8]{0,1:T(8,128)S(1)}, s32[64,8]{0,1:T(8,128)}, u32[]{:S(2)}) copy-start(s32[64,8]{0,1:T(8,128)} %param.21) | copy-start | bytes 6148
  3.0 7.7 %copy-start.13 = (s32[64]{0:T(128)S(1)}, s32[64]{0:T(128)}, u32[]{:S(2)}) copy-start(s32[64]{0:T(128)} %param.17) | copy-start | bytes 772
  3.0 7.8 %copy-start.9 = (bf16[64,2,128]{2,1,0:T(2,128)(2,1)S(1)}, bf16[64,2,128]{2,1,0:T(2,128)(2,1)}, u32[]{:S(2)}) copy-start(bf16[64,2,128]{2,1,0:T(2,128)(2,1)} %param.14) | copy-start | bytes 98308
  3.0 8.4 %copy-start.8 = (bf16[64,16,128]{2,1,0:T(8,128)(2,1)S(1)}, bf16[64,16,128]{2,1,0:T(8,128)(2,1)}, u32[]{:S(2)}) copy-start(bf16[64,16,128]{2,1,0:T(8,128)(2,1)} %param.12) | copy-start | bytes 786436
  3.0 45.6 %all-to-all-start = ((bf16[16,128,384]{2,1,0:T(8,128)(2,1)}), bf16[16,128,384]{2,1,0:T(8,128)(2,1)}, u32[]{:S(2)}, u32[]{:S(2)}) async-start(bf16[16,128,384]{2,1,0:T(8,128)(2,1)} %dynamic-slice_bitcast_fusion.1), calls=%async_computation | async-start | bytes 3145728 | tf_op jit(solution)/shard_map/all_to_all | solution.py:245
  19.1 2.1 copy-start.7
  21.2 5.1 %copy-start.10 = (f32[2048]{0:T(1024)S(1)}, f32[2048]{0:T(1024)}, u32[]{:S(2)}) copy-start(f32[2048]{0:T(1024)} %param.20) | copy-start | bytes 24580
  26.3 0.8 copy-start.3
  27.2 33.1 %collective-permute-start = (bf16[64,2176]{1,0:T(8,128)(2,1)S(1)}, bf16[64,2176]{1,0:T(8,128)(2,1)S(1)}, u32[]{:S(2)}, u32[]{:S(2)}) collective-permute-start(bf16[64,2176]{1,0:T(8,128)(2,1)S(1)} %concatenate.21), channel_id=1, source_target_pairs={{0,8},{1,9},{2,10},{3,11},{4,12},{5,13},{6,14},{7,15},{8,0},{9,1},... | collective-permute-start | bytes 835592 | tf_op jit(solution)/shard_map/ppermute | solution.py:51
  60.3 46.7 %all-to-all-start.1 = ((bf16[16,128,384]{2,1,0:T(8,128)(2,1)}), bf16[16,128,384]{2,1,0:T(8,128)(2,1)S(1)}, u32[]{:S(2)}, u32[]{:S(2)}) async-start(bf16[16,128,384]{2,1,0:T(8,128)(2,1)} %dynamic-slice_bitcast_fusion), calls=%async_computation.1 | async-start | bytes 3145728 | tf_op jit(solution)/shard_map/all_to_all | solution.py:245
  64.0 42.9 %collective-permute-start.4 = (bf16[2048,384]{1,0:T(8,128)(2,1)}, bf16[2048,384]{1,0:T(8,128)(2,1)}, u32[]{:S(2)}, u32[]{:S(2)}) collective-permute-start(bf16[2048,384]{1,0:T(8,128)(2,1)} %bitcast.9.refs_0_), channel_id=1, source_target_pairs={{0,16},{16,0},{1,17},{17,1},{2,18},{18,2},{3,19},{19,3},{4,20},{20... | collective-permute-start | bytes 4718600 | tf_op jit(solution)/shard_map/ppermute | solution.py:55
  65.6 38.7 %collective-permute-start.1 = (bf16[128,2176]{1,0:T(8,128)(2,1)S(1)}, bf16[128,2176]{1,0:T(8,128)(2,1)S(1)}, u32[]{:S(2)}, u32[]{:S(2)}) collective-permute-start(bf16[128,2176]{1,0:T(8,128)(2,1)S(1)} %pad_maximum_fusion.2), channel_id=1, source_target_pairs={{0,4},{1,5},{2,6},{3,7},{4,0},{5,1},{6,2},{7,3},{8,12},{9,13},{10,... | collective-permute-start | bytes 1671176 | tf_op jit(solution)/shard_map/ppermute | solution.py:51
  105.4 37.3 %collective-permute-start.2 = (bf16[256,2176]{1,0:T(8,128)(2,1)}, bf16[256,2176]{1,0:T(8,128)(2,1)}, u32[]{:S(2)}, u32[]{:S(2)}) collective-permute-start(bf16[256,2176]{1,0:T(8,128)(2,1)} %pad_maximum_fusion.1), channel_id=1, source_target_pairs={{0,2},{1,3},{2,0},{3,1},{4,6},{5,7},{6,4},{7,5},{8,10},{9,11},{10,... | collective-permute-start | bytes 3342344 | tf_op jit(solution)/shard_map/ppermute | solution.py:51
  107.0 38.6 %copy-start.2 = (bf16[16,128,384]{2,1,0:T(8,128)(2,1)}, bf16[16,128,384]{2,1,0:T(8,128)(2,1)S(1)}, u32[]{:S(2)}) copy-start(bf16[16,128,384]{2,1,0:T(8,128)(2,1)S(1)} %all-to-all-done.1) | copy-start | bytes 4718596
  107.0 41.1 %all-to-all-start.2 = ((bf16[16,96,384]{2,1,0:T(8,128)(2,1)}), bf16[16,96,384]{2,1,0:T(8,128)(2,1)}, u32[]{:S(2)}, u32[]{:S(2)}) async-start(bf16[16,96,384]{2,1,0:T(8,128)(2,1)} %dynamic-slice_bitcast_fusion.2), calls=%async_computation.2 | async-start | bytes 2359296 | tf_op jit(solution)/shard_map/all_to_all | solution.py:245
  111.4 36.6 %collective-permute-start.5 = (bf16[2048,384]{1,0:T(8,128)(2,1)S(1)}, bf16[2048,384]{1,0:T(8,128)(2,1)}, u32[]{:S(2)}, u32[]{:S(2)}) collective-permute-start(bf16[2048,384]{1,0:T(8,128)(2,1)S(1)} %bitcast.88), channel_id=1, source_target_pairs={{0,16},{16,0},{1,17},{17,1},{2,18},{18,2},{3,19},{19,3},{4,20},{20... | collective-permute-start | bytes 4718600 | tf_op jit(solution)/shard_map/ppermute | solution.py:55
  145.5 13.8 %collective-permute-start.3 = (bf16[512,2176]{1,0:T(8,128)(2,1)}, bf16[512,2176]{1,0:T(8,128)(2,1)}, u32[]{:S(2)}, u32[]{:S(2)}) collective-permute-start(bf16[512,2176]{1,0:T(8,128)(2,1)} %pad_maximum_fusion), channel_id=1, source_target_pairs={{0,1},{1,0},{2,3},{3,2},{4,5},{5,4},{6,7},{7,6},{8,9},{9,8},{10,11... | collective-permute-start | bytes 6684680 | tf_op jit(solution)/shard_map/ppermute | solution.py:51
  148.0 34.5 %all-to-all-start.3 = ((bf16[16,32,768]{2,1,0:T(8,128)(2,1)}), bf16[16,32,768]{2,1,0:T(8,128)(2,1)S(1)}, u32[]{:S(2)}, u32[]{:S(2)}) async-start(bf16[16,32,768]{2,1,0:T(8,128)(2,1)} %slice_bitcast_fusion), calls=%async_computation.3 | async-start | bytes 1572864 | tf_op jit(solution)/shard_map/all_to_all | solution.py:245
  153.9 28.7 %collective-permute-start.6 = (bf16[16,96,384]{2,1,0:T(8,128)(2,1)}, bf16[16,96,384]{2,1,0:T(8,128)(2,1)}, u32[]{:S(2)}, u32[]{:S(2)}) collective-permute-start(bf16[16,96,384]{2,1,0:T(8,128)(2,1)} %all-to-all-done.2.refs_0_), channel_id=1, source_target_pairs={{0,16},{16,0},{1,17},{17,1},{2,18},{18,2},{3,19},{19,3},{4,20},{20... | collective-permute-start | bytes 3538952 | tf_op jit(solution)/shard_map/ppermute | solution.py:55
  182.5 0.9 copy-start.5
  192.4 2.9 %collective-permute-start.11 = (bf16[512,1024]{1,0:T(8,128)(2,1)}, bf16[512,1024]{1,0:T(8,128)(2,1)S(1)}, u32[]{:S(2)}, u32[]{:S(2)}) collective-permute-start(bf16[512,1024]{1,0:T(8,128)(2,1)} %get-tuple-element.22), channel_id=1, source_target_pairs={{0,1},{1,0},{2,3},{3,2},{4,5},{5,4},{6,7},{7,6},{8,9},{9,8},{10,11... | collective-permute-start | bytes 3145736 | tf_op jit(solution)/shard_map/ppermute | solution.py:51
  192.4 6.3 %collective-permute-start.7 = (bf16[512,1024]{1,0:T(8,128)(2,1)}, bf16[512,1024]{1,0:T(8,128)(2,1)S(1)}, u32[]{:S(2)}, u32[]{:S(2)}) collective-permute-start(bf16[512,1024]{1,0:T(8,128)(2,1)} %get-tuple-element.20), channel_id=1, source_target_pairs={{0,1},{1,0},{2,3},{3,2},{4,5},{5,4},{6,7},{7,6},{8,9},{9,8},{10,11... | collective-permute-start | bytes 3145736 | tf_op jit(solution)/shard_map/ppermute | solution.py:51
  196.9 1.8 copy-start.6
  197.1 14.0 %collective-permute-start.12 = (bf16[2,2,64,1024]{3,2,0,1:T(8,128)(2,1)S(1)}, bf16[2,2,64,1024]{3,2,0,1:T(8,128)(2,1)S(1)}, u32[]{:S(2)}, u32[]{:S(2)}) collective-permute-start(bf16[2,2,64,1024]{3,2,0,1:T(8,128)(2,1)S(1)} %bitcast.93), channel_id=1, source_target_pairs={{0,4},{1,5},{2,6},{3,7},{4,0},{5,1},{6,2},{7,3},{8,12},{9,13},{10,... | collective-permute-start | bytes 1572872 | tf_op jit(solution)/shard_map/ppermute | solution.py:51
  199.2 14.7 %collective-permute-start.8 = (bf16[2,2,64,1024]{3,2,1,0:T(8,128)(2,1)S(1)}, bf16[2,2,64,1024]{3,2,1,0:T(8,128)(2,1)S(1)}, u32[]{:S(2)}, u32[]{:S(2)}) collective-permute-start(bf16[2,2,64,1024]{3,2,1,0:T(8,128)(2,1)S(1)} %bitcast.94), channel_id=1, source_target_pairs={{0,2},{1,3},{2,0},{3,1},{4,6},{5,7},{6,4},{7,5},{8,10},{9,11},{10,... | collective-permute-start | bytes 1572872 | tf_op jit(solution)/shard_map/ppermute | solution.py:51
  211.3 14.2 %collective-permute-start.13 = (bf16[2,64,1024]{2,1,0:T(8,128)(2,1)S(1)}, bf16[2,64,1024]{2,1,0:T(8,128)(2,1)S(1)}, u32[]{:S(2)}, u32[]{:S(2)}) collective-permute-start(bf16[2,64,1024]{2,1,0:T(8,128)(2,1)S(1)} %slice_bitcast_fusion.1), channel_id=1, source_target_pairs={{0,8},{1,9},{2,10},{3,11},{4,12},{5,13},{6,14},{7,15},{8,0},{9,1},... | collective-permute-start | bytes 786440 | tf_op jit(solution)/shard_map/ppermute | solution.py:51
  213.9 21.6 %copy-start.4 = (f32[64,2048]{1,0:T(8,128)S(1)}, f32[64,2048]{1,0:T(8,128)}, u32[]{:S(2)}) copy-start(f32[64,2048]{1,0:T(8,128)} %copy-done.3) | copy-start | bytes 1572868
  213.9 22.4 %copy-start.1 = (bf16[64,2,96,128]{3,2,1,0:T(8,128)(2,1)S(1)}, bf16[64,2,96,128]{3,2,1,0:T(8,128)(2,1)}, u32[]{:S(2)}) copy-start(bf16[64,2,96,128]{3,2,1,0:T(8,128)(2,1)} %param.16) | copy-start | bytes 9437188
  214.1 13.2 %collective-permute-start.9 = (bf16[2,64,1024]{2,1,0:T(8,128)(2,1)S(1)}, bf16[2,64,1024]{2,1,0:T(8,128)(2,1)S(1)}, u32[]{:S(2)}, u32[]{:S(2)}) collective-permute-start(bf16[2,64,1024]{2,1,0:T(8,128)(2,1)S(1)} %slice_bitcast_fusion.3), channel_id=1, source_target_pairs={{0,4},{1,5},{2,6},{3,7},{4,0},{5,1},{6,2},{7,3},{8,12},{9,13},{10,... | collective-permute-start | bytes 786440 | tf_op jit(solution)/shard_map/ppermute | solution.py:51
  225.6 5.0 %collective-permute-start.14 = (bf16[64,1024]{1,0:T(8,128)(2,1)S(1)}, bf16[64,1024]{1,0:T(8,128)(2,1)S(1)}, u32[]{:S(2)}, u32[]{:S(2)}) collective-permute-start(bf16[64,1024]{1,0:T(8,128)(2,1)S(1)} %slice_bitcast_fusion.5), channel_id=1, source_target_pairs={{0,2},{1,3},{2,0},{3,1},{4,6},{5,7},{6,4},{7,5},{8,10},{9,11},{10,... | collective-permute-start | bytes 393224 | tf_op jit(solution)/shard_map/ppermute | solution.py:51
  227.4 8.1 %collective-permute-start.10 = (bf16[64,1024]{1,0:T(8,128)(2,1)S(1)}, bf16[64,1024]{1,0:T(8,128)(2,1)S(1)}, u32[]{:S(2)}, u32[]{:S(2)}) collective-permute-start(bf16[64,1024]{1,0:T(8,128)(2,1)S(1)} %slice_bitcast_fusion.7), channel_id=1, source_target_pairs={{0,8},{1,9},{2,10},{3,11},{4,12},{5,13},{6,14},{7,15},{8,0},{9,1},... | collective-permute-start | bytes 393224 | tf_op jit(solution)/shard_map/ppermute | solution.py:51

commit v4 on v3

--- a/solution.py
+++ b/solution.py
@@ -8,6 +8,7 @@
 from jax.sharding import PartitionSpec as P
 
 LANES = 128
+PLANE = 4
 
 
 def attend(queries, new_keys, new_values, cache_keys, cache_values, cache_lengths):
@@ -64,56 +65,71 @@
 def load_weights(places, piece_refs, weights, sems, grp):
     half = weights.shape[-1] // 2
     copies = []
-    for index, (source, lead, part) in enumerate(places):
-        piece = piece_refs[index]
-        if source is not None:
-            piece = piece.at[source]
-        tail = (slice(None),) * (len(weights.shape) - 1 - len(lead))
-        if part is None:
-            target = weights.at[lead + tail]
+    for number, (matrix, side) in enumerate(places):
+        if side is None:
+            lanes = pl.ds(0, 2 * half)
         else:
-            start = pl.multiple_of((grp ^ part) * half, LANES)
-            target = weights.at[lead + tail + (pl.ds(start, half),)]
-        copies.append(pltpu.make_async_copy(piece, target, sems.at[index]))
+            lanes = pl.ds(pl.multiple_of((grp ^ side) * half, LANES), half)
+        target = weights.at[matrix, :, :, lanes]
+        copies.append(pltpu.make_async_copy(piece_refs[number], target, sems.at[number]))
     for copy in copies:
         copy.start()
     for copy in copies:
         copy.wait()
 
 
-def hidden_kernel(places, experts, where_ref, x_ref, *refs):
-    piece_refs = refs[: len(places)]
-    out_ref, weights, sems = refs[len(places) :]
+def hidden_kernel(places, experts, where_ref, first_ref, second_ref, *refs):
+    piece_refs, (out_ref, x_ref, weights, sems) = refs[:-4], refs[-4:]
     me = where_ref[0]
-
-    @pl.when(pl.program_id(0) == 0)
+    step = pl.program_id(0)
+
+    @pl.when(step == 0)
     def load():
         load_weights(places, piece_refs, weights, sems, where_ref[1])
 
-    width = weights.shape[1]
+    @pl.when(step < pl.num_programs(0) // 2)
+    def early():
+        x_ref[...] = first_ref[...]
+
+    @pl.when(step >= pl.num_programs(0) // 2)
+    def late():
+        x_ref[...] = second_ref[...]
+
+    width = weights.shape[1] * weights.shape[2]
     extra = x_ref[:, width:].astype(jnp.float32)
     lane = lax.broadcasted_iota(jnp.int32, extra.shape, 1)
     picked = jnp.where((lane == me) | (lane == me + experts), extra, 0.0)
     coef = jnp.sum(picked, axis=1, keepdims=True)
     x = x_ref[:, :width]
-    gate = jnp.dot(x, weights[0], preferred_element_type=jnp.float32)
-    up = jnp.dot(x, weights[1], preferred_element_type=jnp.float32)
+    ff = weights.shape[-1]
+    gate = jnp.dot(x, weights[0].reshape(width, ff), preferred_element_type=jnp.float32)
+    up = jnp.dot(x, weights[1].reshape(width, ff), preferred_element_type=jnp.float32)
     out_ref[...] = (gate / (1.0 + jnp.exp(-gate)) * up * coef).astype(jnp.bfloat16)
 
 
-def down_kernel(places, where_ref, hidden_ref, *refs):
-    piece_refs = refs[: len(places)]
-    out_refs, weights = refs[len(places) : -1], refs[-1]
-    grp = where_ref[1]
+def down_kernel(cut, split, where_ref, hidden_ref, *refs):
+    out_refs, weights = refs[-5:-1], refs[-1]
+    mine_ref, whole_ref = refs[0], refs[1]
+    me, grp = where_ref[0], where_ref[1]
     step = pl.program_id(0)
     half = weights.shape[-1] // 2
-    for ref, (low, part) in zip(piece_refs, places):
-        span = slice(low, low + ref.shape[1])
-        if part is None:
-            weights[:, span, :] = ref[...]
-        else:
-            start = pl.multiple_of((grp ^ part) * half, LANES)
-            weights[:, span, pl.ds(start, half)] = ref[...]
+    weights[:, cut:, :] = whole_ref[...]
+    if split:
+        own = pl.ds(pl.multiple_of(grp * half, LANES), half)
+        other = pl.ds(pl.multiple_of((1 - grp) * half, LANES), half)
+        far_ref, near_refs = refs[2], refs[3:-5]
+        weights[:, :cut, own] = mine_ref[...]
+
+        @pl.when(step == me // PLANE)
+        def near():
+            for bits, ref in enumerate(near_refs):
+                weights[pl.ds((me ^ bits) % PLANE, 1), :cut, other] = ref[...]
+
+        @pl.when(step != me // PLANE)
+        def far():
+            weights[:, :cut, other] = far_ref[...]
+    else:
+        weights[:, :cut, :] = mine_ref[...]
     matrix = weights[...]
     down = lax.dot_general(
         hidden_ref[...],
@@ -132,63 +148,71 @@
             out_refs[2 * column + 1][...] = down[size:]
 
 
-def call_local(kernel, grid, in_specs, out_specs, out_shape, scratch, operands, pieces):
+def run_hidden(first, second, pieces, places, shape, experts):
+    total, ext = first.shape[0] * 2, first.shape[1]
+    tile = 256 if total % 512 == 0 else total // 2
+    steps = total // tile
+    ff = shape[-1]
     where = jnp.stack([lax.axis_index("ep"), lax.axis_index("grp")]).astype(jnp.int32)
     grid_spec = pltpu.PrefetchScalarGridSpec(
         num_scalar_prefetch=1,
-        grid=grid,
-        in_specs=in_specs + [pl.BlockSpec(memory_space=pl.ANY)] * len(pieces),
-        out_specs=out_specs,
+        grid=(steps,),
+        in_specs=[
+            pl.BlockSpec((tile, ext), lambda i, w: (jnp.minimum(i, steps // 2 - 1), 0)),
+            pl.BlockSpec((tile, ext), lambda i, w: (jnp.maximum(i - steps // 2, 0), 0)),
+        ]
+        + [pl.BlockSpec(memory_space=pl.ANY)] * len(pieces),
+        out_specs=pl.BlockSpec((tile, ff), lambda i, w: (i, 0)),
         scratch_shapes=[
-            pltpu.VMEM(scratch, jnp.bfloat16),
-            pltpu.SemaphoreType.DMA((len(pieces),)),
+            pltpu.VMEM((tile, ext), jnp.bfloat16),
+            pltpu.VMEM(shape, jnp.bfloat16),
+            pltpu.SemaphoreType.DMA((len(places),)),
         ],
     )
     return pl.pallas_call(
-        kernel,
+        functools.partial(hidden_kernel, places, experts),
         grid_spec=grid_spec,
-        out_shape=out_shape,
+        out_shape=jax.ShapeDtypeStruct((total, ff), jnp.bfloat16),
         compiler_params=pltpu.CompilerParams(vmem_limit_bytes=56 * 1024 * 1024),
-    )(where, *operands, *[piece[3] for piece in pieces])
-
-
-def run_hidden(tokens, pieces, width, ff, experts):
-    total = tokens.shape[0]
-    tile = 256 if total % 256 == 0 else total
-    return call_local(
-        functools.partial(hidden_kernel, [p[:3] for p in pieces], experts),
-        (total // tile,),
-        [pl.BlockSpec((tile, tokens.shape[1]), lambda i, w: (i, 0))],
-        pl.BlockSpec((tile, ff), lambda i, w: (i, 0)),
-        jax.ShapeDtypeStruct((total, ff), jnp.bfloat16),
-        (2, width, ff),
-        [tokens],
-        pieces,
-    )
-
-
-def run_down(hidden, pieces, count, rows, width):
+    )(where, first, second, *pieces)
+
+
+def run_down(hidden, mine, whole, far, near, rows, width):
     total, ff = hidden.shape
-    block = min(max(4, 4 * LANES // rows), count // 2)
+    count, cut, size = mine.shape
+    block = PLANE if far is not None else min(max(PLANE, PLANE * LANES // rows), count // 2)
     steps = count // block
     where = jnp.stack([lax.axis_index("ep"), lax.axis_index("grp")]).astype(jnp.int32)
     spec = (total // 2, block * rows)
     low = pl.BlockSpec(spec, lambda i, w: (0, jnp.minimum(i, steps // 2 - 1)))
     high = pl.BlockSpec(spec, lambda i, w: (0, jnp.maximum(i - steps // 2, 0)))
+    in_specs = [
+        pl.BlockSpec((total, ff), lambda i, w: (0, 0)),
+        pl.BlockSpec((block, cut, size), lambda i, w: (i, 0, 0)),
+        pl.BlockSpec((block, rows - cut, ff), lambda i, w: (i, 0, 0)),
+    ]
+    pieces = [mine, whole]
+    if far is not None:
+        in_specs.append(
+            pl.BlockSpec(
+                (block, cut, size), lambda i, w: (jnp.maximum((i ^ (w[0] // PLANE)) - 1, 0), 0, 0)
+            )
+        )
+        in_specs += [pl.BlockSpec((1, cut, size), lambda i, w: (0, 0, 0))] * len(near)
+        pieces += [far] + near
     grid_spec = pltpu.PrefetchScalarGridSpec(
         num_scalar_prefetch=1,
         grid=(steps,),
-        in_specs=[pl.BlockSpec((total, ff), lambda i, w: (0, 0))]
-        + [pl.BlockSpec((block,) + p[3].shape[1:], lambda i, w: (i, 0, 0)) for p in pieces],
+        in_specs=in_specs,
         out_specs=[low, low, high, high],
         scratch_shapes=[pltpu.VMEM((block, rows, ff), jnp.bfloat16)],
     )
     return pl.pallas_call(
-        functools.partial(down_kernel, [p[1:3] for p in pieces]),
+        functools.partial(down_kernel, cut, far is not None),
         grid_spec=grid_spec,
         out_shape=[jax.ShapeDtypeStruct((total // 2, width // 2), jnp.bfloat16)] * 4,
         compiler_params=pltpu.CompilerParams(vmem_limit_bytes=56 * 1024 * 1024),
-    )(where, hidden, *[piece[3] for piece in pieces])
+    )(where, hidden, *pieces)
 
 
 def add_terms(mine, other):
@@ -229,9 +253,11 @@
     experts, _, rows, ff = learner_weights.shape
     count = lax.axis_size("ep")
     parts = lax.axis_size("tp")
+    me = lax.axis_index("ep")
     grp = lax.axis_index("grp")
     stages = [1 << b for b in range(count.bit_length() - 2, -1, -1)]
     split = ff % (2 * LANES) == 0 and lax.axis_size("grp") == 2
+    split = split and count % (2 * PLANE) == 0 and PLANE * rows % LANES == 0
     half = ff // 2
 
     def cut_out(matrix, low, high, halved, start):
@@ -244,13 +270,22 @@
         (block,) = after([block], deps)
         return lax.all_to_all(block, "ep", split_axis=0, concat_axis=0, tiled=True)
 
-    def both(lead, mine):
+    def swapped(mine):
         if not split:
-            return [(None, lead, None, mine)]
-        return [(None, lead, 0, mine), (None, lead, 1, swap_grp(mine))]
-
-    def arrays(pieces):
-        return [piece[3] for piece in pieces]
+            return None
+        planes = [
+            lax.dynamic_slice_in_dim(mine, ((me // PLANE) ^ k) * PLANE, PLANE, 0)
+            for k in range(1, count // PLANE)
+        ]
+        return swap_grp(jnp.concatenate(planes, axis=0))
+
+    def beside(bits, deps):
+        (start,) = after([(1 - grp) * half], deps)
+        block = lax.dynamic_slice(learner_weights, (me ^ bits, 2, 0, start), (1, 1, cut, half))[0]
+        return swap_ep(block, bits) if bits else block
+
+    def arrays(*values):
+        return [value for value in values if value is not None]
 
     cut = rows * 3 // 4 // 16 * 16
     size = half if split else ff
@@ -287,20 +322,28 @@
     for bits in stages[:rest]:
         tokens, other = gather(tokens, bits)
     up = bring(up_block, [gate, other])
-    gate = both((0,), gate.reshape(width, size))
+    gate_far = swap_grp(gate) if split else None
     tokens, other = gather(tokens, stages[rest])
-    down_a = bring(down_a_block, [up, other] + arrays(gate))
-    up = both((1,), up.reshape(width, size))
+    down_a = bring(down_a_block, [up, other] + arrays(gate_far))
+    near = [beside(bits, [up]) for bits in range(PLANE)] if split else []
+    up_far = swap_grp(up) if split else None
     tokens, other = gather(tokens, stages[rest + 1])
-    down_b = bring(down_b_block, [down_a, other] + arrays(up))
-    down_a = both(0, down_a)
-    tokens, _ = gather(tokens, stages[rest + 2])
-
-    hidden = run_hidden(tokens, gate + up, width, ff, experts)
+    down_b = bring(down_b_block, [down_a, other] + arrays(up_far))
+    down_a_far = swapped(down_a)
+    other = swap_ep(tokens, stages[rest + 2])
+
+    pieces, places = [], []
+    side = 0 if split else None
+    for matrix, (mine, far) in enumerate(((gate, gate_far), (up, up_far))):
+        places.append((matrix, side))
+        pieces.append(mine)
+        if split:
+            places.append((matrix, 1))
+            pieces.append(far)
+    hidden = run_hidden(tokens, other, pieces, places, (2, count, rows, ff), experts)
     lower = stages[-2::-1]
     orders = (lower, lower[1:] + lower[:1])
-    pieces = down_a + [(None, cut, None, down_b)]
-    products = run_down(hidden, pieces, count, rows, width)
+    products = run_down(hidden, down_a, down_b, down_a_far, near, rows, width)
     kept = products[0::2]
     given = [swap_ep(give, 1) for give in products[1::2]]
     totals = [

time: 237 us -> 232 us (0.979)
  local copies, waits for them, and re-layouts: 22 us -> 15.8 us
  waiting for transfers between devices: 127 us -> 124 us
    unnamed x33 -> x39, local copies, waits for them, and re-layouts: 6.26 us -> 1.24 us
    ppermute x3, waiting for transfers between devices: 8.21 us -> 4.55 us  [swap_grp(): return lax.ppermute(x, 'grp', [(0, 1), (1, 0)])]
    concatenate x1 -> x0, local copies, waits for them, and re-layouts: 3.17 us -> none  [gather(): return (jnp.concatenate([tokens, other], axis=0), other)]
    ppermute x12 -> x15, starting transfers between devices: 16.2 us -> 17.9 us  [swap_ep(): return lax.ppermute(x, 'ep', [(i, i ^ bits) for i in range(count)])]
    ppermute x12 -> x15, waiting for transfers between devices: 108 us -> 109 us  [swap_ep(): return lax.ppermute(x, 'ep', [(i, i ^ bits) for i in range(count)])]
  transfers between devices with their start and end apart: 19 -> 22, of which waited for: 11 -> 13; matrix products, arithmetic and copies ran while one was open for 17% -> 16% of each run, Pallas kernels for 5% -> 6%
where the time goes in v4:
time: 232 us; the launch traced here: 231 us
  waiting for transfers between devices  124 us (53%)
  starting transfers between devices  43.7 us (19%)
  Pallas kernels  22.7 us (10%)
  local copies, waits for them, and re-layouts  15.8 us (7%)
  matrix products  12.7 us (5%)
  other arithmetic  12.5 us (5%)
    ppermute x15, waiting for transfers between devices, swap_ep(): return lax.ppermute(x, 'ep', [(i, i ^ bits) for i in range(count)])  109 us
    all_to_all x4, starting transfers between devices, bring(): return lax.all_to_all(block, 'ep', split_axis=0, concat_axis=0, tiled=True)  21 us
    ppermute x15, starting transfers between devices, swap_ep(): return lax.ppermute(x, 'ep', [(i, i ^ bits) for i in range(count)])  17.9 us
    pallas_call x1, Pallas kernels, run_hidden(): pl.pallas_call(functools.partial(hidden_kernel, places, experts), grid_sp...  13.6 us
    squeeze x4, local copies, waits for them, and re-layouts, cut_out(): lax.dynamic_slice(learner_weights, (0, matrix, low, start), (experts, 1,...  11.6 us
    all_to_all x4, waiting for transfers between devices, bring(): return lax.all_to_all(block, 'ep', split_axis=0, concat_axis=0, tiled=True)  9.73 us
    pallas_call x1, Pallas kernels, run_down(): pl.pallas_call(functools.partial(down_kernel, cut, far is not None), grid...  9.11 us
    dot_general x1, matrix products, shards(): attn = jnp.dot(context, out_weight, preferred_element_type=jnp.float32)  5.08 us
  transfers between devices with their start and end apart: 22, of which 13 were waited for; matrix products, arithmetic and copies ran while one was open for 16% of the time, Pallas kernels for 6%

profile of v4, /device:TPU:0, one launch (start us, length us, event | category | flops | bytes accessed | tf_op | source)
XLA Modules:
  0.0 231.3 jit_solution(6986505417747938067)
XLA Ops:
  0.0 3.0 %dynamic-slice_bitcast_fusion.1 = bf16[16,128,384]{2,1,0:T(8,128)(2,1)} fusion(bf16[16,3,128,768]{3,2,1,0:T(8,128)(2,1)} %param.23, s32[]{:T(128)S(6)} %select_n.55), kind=kLoop, calls=%fused_computation.5 | loop fusion | bytes 3145732 | tf_op jit(solution)/shard_map/squeeze | solution.py:265
  3.0 7.5 %all-to-all-start = ((bf16[16,128,384]{2,1,0:T(8,128)(2,1)}), bf16[16,128,384]{2,1,0:T(8,128)(2,1)}, u32[]{:S(2)}, u32[]{:S(2)}) async-start(bf16[16,128,384]{2,1,0:T(8,128)(2,1)} %dynamic-slice_bitcast_fusion.1), calls=%async_computation | async-start | bytes 3145728 | tf_op jit(solution)/shard_map/all_to_all | solution.py:271
  10.6 0.1 copy.38
  10.8 0.1 copy.39
  10.9 1.0 fusion.11
  12.0 1.4 convert_element_type.130
  13.4 4.5 %fusion.25 = (f32[64,2,8]{2,1,0:T(2,128)S(1)}, f32[64,2,8,96]{3,2,1,0:T(8,128)}) fusion(bf16[64,2,96,128]{3,2,1,0:T(8,128)(2,1)} %param.15, bf16[64,16,128]{2,1,0:T(8,128)(2,1)S(1)} %copy-done.11, pred[64,96]{1,0:T(8,128)(4,1)S(1)} %iota_compare_fusion.1), kind=kOutput, calls=%fused_computation.75 | convolution fusion | flops 25459712 | bytes 3811328 | tf_op jit(solution)/shard_map/skgd,skld->skgl/dot_general | solution.py:22
  18.0 0.1 copy.33
  18.1 1.4 fusion.6
  19.6 0.1 copy.35
  19.7 0.1 copy.36
  19.9 2.1 fusion.1
  22.0 5.1 %multiply_reduce_fusion = (f32[64]{0:T(128)S(1)}, f32[64,2048]{1,0:T(8,128)S(1)}) fusion(bf16[2048,2048]{1,0:T(8,128)(2,1)} %param.19, bf16[8,8,16,128]{3,2,1,0:T(8,128)(2,1)S(1)} %bitcast.96, bf16[64,2048]{1,0:T(8,128)(2,1)S(1)} %copy-done.10), kind=kOutput, calls=%fused_computation.27 | convolution fusion | flops 537395136 | bytes 9437440 | tf_op jit(solution)/shard_map/dot_general | solution.py:301
  27.1 0.1 multiply_convert_fusion
  27.2 0.1 concatenate.20
  27.3 2.8 %collective-permute-start = (bf16[64,2176]{1,0:T(8,128)(2,1)S(1)}, bf16[64,2176]{1,0:T(8,128)(2,1)S(1)}, u32[]{:S(2)}, u32[]{:S(2)}) collective-permute-start(bf16[64,2176]{1,0:T(8,128)(2,1)S(1)} %concatenate.20), channel_id=1, source_target_pairs={{0,8},{1,9},{2,10},{3,11},{4,12},{5,13},{6,14},{7,15},{8,0},{9,1},... | collective-permute-start | bytes 835592 | tf_op jit(solution)/shard_map/ppermute | solution.py:52
  30.2 3.5 %dynamic-slice_bitcast_fusion = bf16[16,128,384]{2,1,0:T(8,128)(2,1)} fusion(bf16[16,3,128,768]{3,2,1,0:T(8,128)(2,1)} %param.23, s32[]{:T(128)S(6)} %select_n.56), kind=kLoop, calls=%fused_computation.4 | loop fusion | bytes 3145732 | tf_op jit(solution)/shard_map/squeeze | solution.py:265
  33.7 3.0 %dynamic-slice_bitcast_fusion.2 = bf16[16,96,384]{2,1,0:T(8,128)(2,1)} fusion(bf16[16,3,128,768]{3,2,1,0:T(8,128)(2,1)} %param.23, s32[]{:T(128)S(6)} %select_n.56), kind=kLoop, calls=%fused_computation.10 | loop fusion | bytes 2359300 | tf_op jit(solution)/shard_map/squeeze | solution.py:265
  36.7 2.1 slice_bitcast_fusion
  38.8 9.7 %all-to-all-done.refs_0_ = bf16[16,128,384]{2,1,0:T(8,128)(2,1)} async-done(((bf16[16,128,384]{2,1,0:T(8,128)(2,1)}), bf16[16,128,384]{2,1,0:T(8,128)(2,1)}, u32[]{:S(2)}, u32[]{:S(2)}) %all-to-all-start) | async-done | bytes 1572896 | tf_op jit(solution)/shard_map/all_to_all | solution.py:271
  48.6 11.7 %collective-permute-done = bf16[64,2176]{1,0:T(8,128)(2,1)S(1)} collective-permute-done((bf16[64,2176]{1,0:T(8,128)(2,1)S(1)}, bf16[64,2176]{1,0:T(8,128)(2,1)S(1)}, u32[]{:S(2)}, u32[]{:S(2)}) %collective-permute-start) | collective-permute-done | bytes 278560 | tf_op jit(solution)/shard_map/ppermute | solution.py:52
  60.3 3.7 %all-to-all-start.1 = ((bf16[16,128,384]{2,1,0:T(8,128)(2,1)}), bf16[16,128,384]{2,1,0:T(8,128)(2,1)S(1)}, u32[]{:S(2)}, u32[]{:S(2)}) async-start(bf16[16,128,384]{2,1,0:T(8,128)(2,1)} %dynamic-slice_bitcast_fusion), calls=%async_computation.1 | async-start | bytes 3145728 | tf_op jit(solution)/shard_map/all_to_all | solution.py:271
  64.0 1.6 collective-permute-start.4
  65.6 1.9 collective-permute-start.1
  67.5 36.8 %collective-permute-done.1 = bf16[128,2176]{1,0:T(8,128)(2,1)S(1)} collective-permute-done((bf16[128,2176]{1,0:T(8,128)(2,1)S(1)}, bf16[128,2176]{1,0:T(8,128)(2,1)S(1)}, u32[]{:S(2)}, u32[]{:S(2)}) %collective-permute-start.1) | collective-permute-done | bytes 557088 | tf_op jit(solution)/shard_map/ppermute | solution.py:52
  104.3 1.2 pad_maximum_fusion.1
  105.5 1.5 collective-permute-start.2
  107.1 4.0 %all-to-all-start.2 = ((bf16[16,96,384]{2,1,0:T(8,128)(2,1)}), bf16[16,96,384]{2,1,0:T(8,128)(2,1)S(1)}, u32[]{:S(2)}, u32[]{:S(2)}) async-start(bf16[16,96,384]{2,1,0:T(8,128)(2,1)} %dynamic-slice_bitcast_fusion.2), calls=%async_computation.2 | async-start | bytes 2359296 | tf_op jit(solution)/shard_map/all_to_all | solution.py:271
  111.1 1.6 collective-permute-start.5
  112.7 30.1 %collective-permute-done.2 = bf16[256,2176]{1,0:T(8,128)(2,1)} collective-permute-done((bf16[256,2176]{1,0:T(8,128)(2,1)}, bf16[256,2176]{1,0:T(8,128)(2,1)}, u32[]{:S(2)}, u32[]{:S(2)}) %collective-permute-start.2) | collective-permute-done | bytes 1114144 | tf_op jit(solution)/shard_map/ppermute | solution.py:52
  142.8 2.9 %pad_maximum_fusion.first_ref = bf16[512,2176]{1,0:T(8,128)(2,1)} fusion(bf16[256,2176]{1,0:T(8,128)(2,1)} %collective-permute-done.2, bf16[128,2176]{1,0:T(8,128)(2,1)} %copy-done.7, bf16[64,2176]{1,0:T(8,128)(2,1)S(1)} %collective-permute-done, bf16[64,2176]{1,0:T(8,128)(2,1)S(1)} %concatenate.20), kind=kLoop, calls=%fused_computation.1 | loop fusion | flops 8912896 | bytes 4456448 | tf_op jit(solution)/shard_map/concatenate | solution.py:319
  145.7 2.2 collective-permute-done.5.refs_3_
  147.9 5.8 %all-to-all-start.3 = ((bf16[16,32,768]{2,1,0:T(8,128)(2,1)}), bf16[16,32,768]{2,1,0:T(8,128)(2,1)S(1)}, u32[]{:S(2)}, u32[]{:S(2)}) async-start(bf16[16,32,768]{2,1,0:T(8,128)(2,1)} %slice_bitcast_fusion), calls=%async_computation.3 | async-start | bytes 1572864 | tf_op jit(solution)/shard_map/all_to_all | solution.py:271
  153.7 0.1 constant_dynamic-slice_fusion.2
  153.8 1.1 pad_maximum_fusion.2
  154.9 1.5 collective-permute-start.6
  156.4 1.8 dynamic-slice_bitcast_fusion.3
  158.2 1.3 collective-permute-start.9
  159.5 0.6 collective-permute-start.7
  160.2 0.2 collective-permute-start.8
  160.3 0.6 pad_add_fusion.where_ref
  161.0 13.6 %shard_map.118.hidden_ref = bf16[1024,768]{1,0:T(8,128)(2,1)} custom-call(s32[2]{0:T(128)} %pad_add_fusion.where_ref, bf16[512,2176]{1,0:T(8,128)(2,1)} %pad_maximum_fusion.first_ref, bf16[512,2176]{1,0:T(8,128)(2,1)} %collective-permute-done.3.second_ref, bf16[16,128,384]{2,1,0:T(8,128)(2,1)} %all-to-all-done.refs_0_, ...), custom_call_target="tpu_custom_call" | custom-call | tf_op jit(solution)/shard_map/pallas_call | solution.py:172
  174.7 2.4 %collective-permute-done.6.refs_2_ = bf16[12,96,384]{2,1,0:T(8,128)(2,1)S(1)} collective-permute-done((bf16[12,96,384]{2,1,0:T(8,128)(2,1)}, bf16[12,96,384]{2,1,0:T(8,128)(2,1)S(1)}, u32[]{:S(2)}, u32[]{:S(2)}) %collective-permute-start.6) | collective-permute-done | bytes 884768 | tf_op jit(solution)/shard_map/ppermute | solution.py:56
  177.1 0.9 copy-done.9
  177.9 0.3 copy-done.6
  178.2 9.1 %shard_map.119 = (bf16[512,1024]{1,0:T(8,128)(2,1)}, bf16[512,1024]{1,0:T(8,128)(2,1)}, bf16[512,1024]{1,0:T(8,128)(2,1)}, bf16[512,1024]{1,0:T(8,128)(2,1)}) custom-call(s32[2]{0:T(128)} %pad_add_fusion.where_ref, bf16[1024,768]{1,0:T(8,128)(2,1)} %shard_map.118.hidden_ref, bf16[16,96,384]{2,1,0:T(8,128)(2,1)} %copy-done.2, bf16[16,32,768]{2,1,0:T(8,128)(2,1)} %copy-done.6, ...), custom_call_target="tpu_custom_call" | custom-call | tf_op jit(solution)/shard_map/pallas_call | solution.py:210
  187.3 0.5 collective-permute-start.14
  187.8 2.4 %collective-permute-done.10 = bf16[512,1024]{1,0:T(8,128)(2,1)S(1)} collective-permute-done((bf16[512,1024]{1,0:T(8,128)(2,1)}, bf16[512,1024]{1,0:T(8,128)(2,1)S(1)}, u32[]{:S(2)}, u32[]{:S(2)}) %collective-permute-start.10) | collective-permute-done | bytes 1048608 | tf_op jit(solution)/shard_map/ppermute | solution.py:52
  190.2 1.7 add_convert_fusion.1
  192.0 1.7 collective-permute-start.11
  193.7 0.4 add_convert_fusion
  194.1 0.1 fusion.24
  194.3 1.5 collective-permute-start.15
  195.8 10.2 %collective-permute-done.11 = bf16[2,2,64,1024]{3,2,1,0:T(8,128)(2,1)S(1)} collective-permute-done((bf16[2,2,64,1024]{3,2,1,0:T(8,128)(2,1)S(1)}, bf16[2,2,64,1024]{3,2,1,0:T(8,128)(2,1)S(1)}, u32[]{:S(2)}, u32[]{:S(2)}) %collective-permute-start.11) | collective-permute-done | bytes 524320 | tf_op jit(solution)/shard_map/ppermute | solution.py:52
  206.0 0.2 fusion.3
  206.2 1.7 collective-permute-start.12
  208.0 0.2 fusion.2
  208.2 2.4 %collective-permute-start.16 = (bf16[2,64,1024]{2,1,0:T(8,128)(2,1)S(1)}, bf16[2,64,1024]{2,1,0:T(8,128)(2,1)S(1)}, u32[]{:S(2)}, u32[]{:S(2)}) collective-permute-start(bf16[2,64,1024]{2,1,0:T(8,128)(2,1)S(1)} %slice_bitcast_fusion.1), channel_id=1, source_target_pairs={{0,8},{1,9},{2,10},{3,11},{4,12},{5,13},{6,14},{7,15},{8,0},{9,1},... | collective-permute-start | bytes 786440 | tf_op jit(solution)/shard_map/ppermute | solution.py:52
  210.7 8.2 %collective-permute-done.12 = bf16[2,64,1024]{2,1,0:T(8,128)(2,1)S(1)} collective-permute-done((bf16[2,64,1024]{2,1,0:T(8,128)(2,1)S(1)}, bf16[2,64,1024]{2,1,0:T(8,128)(2,1)S(1)}, u32[]{:S(2)}, u32[]{:S(2)}) %collective-permute-start.12) | collective-permute-done | bytes 262176 | tf_op jit(solution)/shard_map/ppermute | solution.py:52
  219.1 6.2 %collective-permute-done.16 = bf16[2,64,1024]{2,1,0:T(8,128)(2,1)S(1)} collective-permute-done((bf16[2,64,1024]{2,1,0:T(8,128)(2,1)S(1)}, bf16[2,64,1024]{2,1,0:T(8,128)(2,1)S(1)}, u32[]{:S(2)}, u32[]{:S(2)}) %collective-permute-start.16) | collective-permute-done | bytes 262176 | tf_op jit(solution)/shard_map/ppermute | solution.py:52
  225.4 1.5 collective-permute-start.17
  226.9 0.7 collective-permute-done.13
  227.7 2.7 %collective-permute-done.17 = bf16[64,1024]{1,0:T(8,128)(2,1)S(1)} collective-permute-done((bf16[64,1024]{1,0:T(8,128)(2,1)S(1)}, bf16[64,1024]{1,0:T(8,128)(2,1)S(1)}, u32[]{:S(2)}, u32[]{:S(2)}) %collective-permute-start.17) | collective-permute-done | bytes 131104 | tf_op jit(solution)/shard_map/ppermute | solution.py:52
  230.5 0.8 add_convert_fusion.2
  (71 shorter events, 1.0 us)
Async XLA Ops:
  0.0 19.9 %copy-start = (bf16[64,2,96,128]{3,2,1,0:T(8,128)(2,1)S(1)}, bf16[64,2,96,128]{3,2,1,0:T(8,128)(2,1)}, u32[]{:S(2)}) copy-start(bf16[64,2,96,128]{3,2,1,0:T(8,128)(2,1)} %param.16) | copy-start | bytes 9437188
  3.0 7.6 %copy-start.16 = (f32[64,8]{0,1:T(8,128)S(1)}, f32[64,8]{0,1:T(8,128)}, u32[]{:S(2)}) copy-start(f32[64,8]{0,1:T(8,128)} %param.22) | copy-start | bytes 6148
  3.0 7.6 %copy-start.17 = (s32[64,8]{0,1:T(8,128)S(1)}, s32[64,8]{0,1:T(8,128)}, u32[]{:S(2)}) copy-start(s32[64,8]{0,1:T(8,128)} %param.21) | copy-start | bytes 6148
  3.0 7.7 %copy-start.18 = (s32[64]{0:T(128)S(1)}, s32[64]{0:T(128)}, u32[]{:S(2)}) copy-start(s32[64]{0:T(128)} %param.17) | copy-start | bytes 772
  3.0 7.9 %copy-start.11 = (bf16[64,16,128]{2,1,0:T(8,128)(2,1)S(1)}, bf16[64,16,128]{2,1,0:T(8,128)(2,1)}, u32[]{:S(2)}) copy-start(bf16[64,16,128]{2,1,0:T(8,128)(2,1)} %param.12) | copy-start | bytes 786436
  3.0 45.6 %all-to-all-start = ((bf16[16,128,384]{2,1,0:T(8,128)(2,1)}), bf16[16,128,384]{2,1,0:T(8,128)(2,1)}, u32[]{:S(2)}, u32[]{:S(2)}) async-start(bf16[16,128,384]{2,1,0:T(8,128)(2,1)} %dynamic-slice_bitcast_fusion.1), calls=%async_computation | async-start | bytes 3145728 | tf_op jit(solution)/shard_map/all_to_all | solution.py:271
  19.9 2.1 copy-start.10
  22.0 5.1 %copy-start.15 = (f32[2048]{0:T(1024)S(1)}, f32[2048]{0:T(1024)}, u32[]{:S(2)}) copy-start(f32[2048]{0:T(1024)} %param.20) | copy-start | bytes 24580
  27.1 6.6 %copy-start.4 = (f32[64,2048]{1,0:T(8,128)}, f32[64,2048]{1,0:T(8,128)S(1)}, u32[]{:S(2)}) copy-start(f32[64,2048]{1,0:T(8,128)S(1)} %get-tuple-element.41) | copy-start | bytes 1572868
  27.3 32.9 %collective-permute-start = (bf16[64,2176]{1,0:T(8,128)(2,1)S(1)}, bf16[64,2176]{1,0:T(8,128)(2,1)S(1)}, u32[]{:S(2)}, u32[]{:S(2)}) collective-permute-start(bf16[64,2176]{1,0:T(8,128)(2,1)S(1)} %concatenate.20), channel_id=1, source_target_pairs={{0,8},{1,9},{2,10},{3,11},{4,12},{5,13},{6,14},{7,15},{8,0},{9,1},... | collective-permute-start | bytes 835592 | tf_op jit(solution)/shard_map/ppermute | solution.py:52
  60.3 46.8 %all-to-all-start.1 = ((bf16[16,128,384]{2,1,0:T(8,128)(2,1)}), bf16[16,128,384]{2,1,0:T(8,128)(2,1)S(1)}, u32[]{:S(2)}, u32[]{:S(2)}) async-start(bf16[16,128,384]{2,1,0:T(8,128)(2,1)} %dynamic-slice_bitcast_fusion), calls=%async_computation.1 | async-start | bytes 3145728 | tf_op jit(solution)/shard_map/all_to_all | solution.py:271
  64.0 43.1 %collective-permute-start.4 = (bf16[16,128,384]{2,1,0:T(8,128)(2,1)}, bf16[16,128,384]{2,1,0:T(8,128)(2,1)}, u32[]{:S(2)}, u32[]{:S(2)}) collective-permute-start(bf16[16,128,384]{2,1,0:T(8,128)(2,1)} %all-to-all-done.refs_0_), channel_id=1, source_target_pairs={{0,16},{16,0},{1,17},{17,1},{2,18},{18,2},{3,19},{19,3},{4,20},{20... | collective-permute-start | bytes 4718600 | tf_op jit(solution)/shard_map/ppermute | solution.py:56
  65.6 38.7 %collective-permute-start.1 = (bf16[128,2176]{1,0:T(8,128)(2,1)S(1)}, bf16[128,2176]{1,0:T(8,128)(2,1)S(1)}, u32[]{:S(2)}, u32[]{:S(2)}) collective-permute-start(bf16[128,2176]{1,0:T(8,128)(2,1)S(1)} %pad_maximum_fusion.3), channel_id=1, source_target_pairs={{0,4},{1,5},{2,6},{3,7},{4,0},{5,1},{6,2},{7,3},{8,12},{9,13},{10,... | collective-permute-start | bytes 1671176 | tf_op jit(solution)/shard_map/ppermute | solution.py:52
  104.3 2.7 %copy-start.7 = (bf16[128,2176]{1,0:T(8,128)(2,1)}, bf16[128,2176]{1,0:T(8,128)(2,1)S(1)}, u32[]{:S(2)}) copy-start(bf16[128,2176]{1,0:T(8,128)(2,1)S(1)} %collective-permute-done.1) | copy-start | bytes 1671172
  105.5 37.3 %collective-permute-start.2 = (bf16[256,2176]{1,0:T(8,128)(2,1)}, bf16[256,2176]{1,0:T(8,128)(2,1)}, u32[]{:S(2)}, u32[]{:S(2)}) collective-permute-start(bf16[256,2176]{1,0:T(8,128)(2,1)} %pad_maximum_fusion.1), channel_id=1, source_target_pairs={{0,2},{1,3},{2,0},{3,1},{4,6},{5,7},{6,4},{7,5},{8,10},{9,11},{10,... | collective-permute-start | bytes 3342344 | tf_op jit(solution)/shard_map/ppermute | solution.py:52
  107.1 38.7 %copy-start.3 = (bf16[16,128,384]{2,1,0:T(8,128)(2,1)}, bf16[16,128,384]{2,1,0:T(8,128)(2,1)S(1)}, u32[]{:S(2)}) copy-start(bf16[16,128,384]{2,1,0:T(8,128)(2,1)S(1)} %all-to-all-done.1.refs_2_) | copy-start | bytes 4718596
  107.1 40.8 %all-to-all-start.2 = ((bf16[16,96,384]{2,1,0:T(8,128)(2,1)}), bf16[16,96,384]{2,1,0:T(8,128)(2,1)S(1)}, u32[]{:S(2)}, u32[]{:S(2)}) async-start(bf16[16,96,384]{2,1,0:T(8,128)(2,1)} %dynamic-slice_bitcast_fusion.2), calls=%async_computation.2 | async-start | bytes 2359296 | tf_op jit(solution)/shard_map/all_to_all | solution.py:271
  111.1 36.8 %collective-permute-start.5 = (bf16[16,128,384]{2,1,0:T(8,128)(2,1)S(1)}, bf16[16,128,384]{2,1,0:T(8,128)(2,1)}, u32[]{:S(2)}, u32[]{:S(2)}) collective-permute-start(bf16[16,128,384]{2,1,0:T(8,128)(2,1)S(1)} %all-to-all-done.1.refs_2_), channel_id=1, source_target_pairs={{0,16},{16,0},{1,17},{17,1},{2,18},{18,2},{3,19},{19,3},{4,20},{20... | collective-permute-start | bytes 4718600 | tf_op jit(solution)/shard_map/ppermute | solution.py:56
  145.7 15.3 %collective-permute-start.3 = (bf16[512,2176]{1,0:T(8,128)(2,1)}, bf16[512,2176]{1,0:T(8,128)(2,1)}, u32[]{:S(2)}, u32[]{:S(2)}) collective-permute-start(bf16[512,2176]{1,0:T(8,128)(2,1)} %pad_maximum_fusion.first_ref), channel_id=1, source_target_pairs={{0,1},{1,0},{2,3},{3,2},{4,5},{5,4},{6,7},{7,6},{8,9},{9,8},{10,11... | collective-permute-start | bytes 6684680 | tf_op jit(solution)/shard_map/ppermute | solution.py:52
  147.9 7.0 %copy-start.2 = (bf16[16,96,384]{2,1,0:T(8,128)(2,1)}, bf16[16,96,384]{2,1,0:T(8,128)(2,1)S(1)}, u32[]{:S(2)}) copy-start(bf16[16,96,384]{2,1,0:T(8,128)(2,1)S(1)} %all-to-all-done.2.refs_0_) | copy-start | bytes 3538948
  147.9 29.1 %all-to-all-start.3 = ((bf16[16,32,768]{2,1,0:T(8,128)(2,1)}), bf16[16,32,768]{2,1,0:T(8,128)(2,1)S(1)}, u32[]{:S(2)}, u32[]{:S(2)}) async-start(bf16[16,32,768]{2,1,0:T(8,128)(2,1)} %slice_bitcast_fusion), calls=%async_computation.3 | async-start | bytes 1572864 | tf_op jit(solution)/shard_map/all_to_all | solution.py:271
  154.9 22.1 %collective-permute-start.6 = (bf16[12,96,384]{2,1,0:T(8,128)(2,1)}, bf16[12,96,384]{2,1,0:T(8,128)(2,1)S(1)}, u32[]{:S(2)}, u32[]{:S(2)}) collective-permute-start(bf16[12,96,384]{2,1,0:T(8,128)(2,1)} %pad_maximum_fusion.2), channel_id=1, source_target_pairs={{0,16},{16,0},{1,17},{17,1},{2,18},{18,2},{3,19},{19,3},{4,20},{20... | collective-permute-start | bytes 2654216 | tf_op jit(solution)/shard_map/ppermute | solution.py:56
  158.2 16.4 %collective-permute-start.9 = (bf16[1,96,384]{2,1,0:T(8,128)(2,1)S(1)}, bf16[1,96,384]{2,1,0:T(8,128)(2,1)S(1)}, u32[]{:S(2)}, u32[]{:S(2)}) collective-permute-start(bf16[1,96,384]{2,1,0:T(8,128)(2,1)S(1)} %get-tuple-element.25), channel_id=1, source_target_pairs={{0,3},{1,2},{2,1},{3,0},{4,7},{5,6},{6,5},{7,4},{8,11},{9,10},{10,... | collective-permute-start | bytes 221192 | tf_op jit(solution)/shard_map/ppermute | solution.py:52
  159.5 15.1 %collective-permute-start.7 = (bf16[1,96,384]{2,1,0:T(8,128)(2,1)S(1)}, bf16[1,96,384]{2,1,0:T(8,128)(2,1)S(1)}, u32[]{:S(2)}, u32[]{:S(2)}) collective-permute-start(bf16[1,96,384]{2,1,0:T(8,128)(2,1)S(1)} %get-tuple-element.26), channel_id=1, source_target_pairs={{0,1},{1,0},{2,3},{3,2},{4,5},{5,4},{6,7},{7,6},{8,9},{9,8},{10,11... | collective-permute-start | bytes 221192 | tf_op jit(solution)/shard_map/ppermute | solution.py:52
  160.2 14.5 %collective-permute-start.8 = (bf16[1,96,384]{2,1,0:T(8,128)(2,1)S(1)}, bf16[1,96,384]{2,1,0:T(8,128)(2,1)S(1)}, u32[]{:S(2)}, u32[]{:S(2)}) collective-permute-start(bf16[1,96,384]{2,1,0:T(8,128)(2,1)S(1)} %get-tuple-element.28), channel_id=1, source_target_pairs={{0,2},{1,3},{2,0},{3,1},{4,6},{5,7},{6,4},{7,5},{8,10},{9,11},{10,... | collective-permute-start | bytes 221192 | tf_op jit(solution)/shard_map/ppermute | solution.py:52
  174.6 2.4 %copy-start.12 = (bf16[1,96,384]{2,1,0:T(8,128)(2,1)}, bf16[1,96,384]{2,1,0:T(8,128)(2,1)S(1)}, u32[]{:S(2)}) copy-start(bf16[1,96,384]{2,1,0:T(8,128)(2,1)S(1)} %collective-permute-done.9.refs_6_) | copy-start | bytes 221188
  174.6 2.4 %copy-start.13 = (bf16[1,96,384]{2,1,0:T(8,128)(2,1)}, bf16[1,96,384]{2,1,0:T(8,128)(2,1)S(1)}, u32[]{:S(2)}) copy-start(bf16[1,96,384]{2,1,0:T(8,128)(2,1)S(1)} %collective-permute-done.7.refs_4_) | copy-start | bytes 221188
  174.6 2.4 %copy-start.14 = (bf16[1,96,384]{2,1,0:T(8,128)(2,1)}, bf16[1,96,384]{2,1,0:T(8,128)(2,1)S(1)}, u32[]{:S(2)}) copy-start(bf16[1,96,384]{2,1,0:T(8,128)(2,1)S(1)} %collective-permute-done.8.refs_5_) | copy-start | bytes 221188
  177.0 0.9 copy-start.9
  177.0 1.2 copy-start.6
  187.3 2.9 %collective-permute-start.10 = (bf16[512,1024]{1,0:T(8,128)(2,1)}, bf16[512,1024]{1,0:T(8,128)(2,1)S(1)}, u32[]{:S(2)}, u32[]{:S(2)}) collective-permute-start(bf16[512,1024]{1,0:T(8,128)(2,1)} %get-tuple-element.22), channel_id=1, source_target_pairs={{0,1},{1,0},{2,3},{3,2},{4,5},{5,4},{6,7},{7,6},{8,9},{9,8},{10,11... | collective-permute-start | bytes 3145736 | tf_op jit(solution)/shard_map/ppermute | solution.py:52
  187.3 6.4 %collective-permute-start.14 = (bf16[512,1024]{1,0:T(8,128)(2,1)}, bf16[512,1024]{1,0:T(8,128)(2,1)S(1)}, u32[]{:S(2)}, u32[]{:S(2)}) collective-permute-start(bf16[512,1024]{1,0:T(8,128)(2,1)} %get-tuple-element.24), channel_id=1, source_target_pairs={{0,1},{1,0},{2,3},{3,2},{4,5},{5,4},{6,7},{7,6},{8,9},{9,8},{10,11... | collective-permute-start | bytes 3145736 | tf_op jit(solution)/shard_map/ppermute | solution.py:52
  190.2 3.5 %copy-start.8 = (bf16[512,1024]{1,0:T(8,128)(2,1)S(1)}, bf16[512,1024]{1,0:T(8,128)(2,1)}, u32[]{:S(2)}) copy-start(bf16[512,1024]{1,0:T(8,128)(2,1)} %get-tuple-element.23) | copy-start | bytes 3145732
  192.0 14.0 %collective-permute-start.11 = (bf16[2,2,64,1024]{3,2,1,0:T(8,128)(2,1)S(1)}, bf16[2,2,64,1024]{3,2,1,0:T(8,128)(2,1)S(1)}, u32[]{:S(2)}, u32[]{:S(2)}) collective-permute-start(bf16[2,2,64,1024]{3,2,1,0:T(8,128)(2,1)S(1)} %bitcast.98), channel_id=1, source_target_pairs={{0,2},{1,3},{2,0},{3,1},{4,6},{5,7},{6,4},{7,5},{8,10},{9,11},{10,... | collective-permute-start | bytes 1572872 | tf_op jit(solution)/shard_map/ppermute | solution.py:52
  194.3 13.8 %collective-permute-start.15 = (bf16[2,2,64,1024]{3,2,0,1:T(8,128)(2,1)S(1)}, bf16[2,2,64,1024]{3,2,0,1:T(8,128)(2,1)S(1)}, u32[]{:S(2)}, u32[]{:S(2)}) collective-permute-start(bf16[2,2,64,1024]{3,2,0,1:T(8,128)(2,1)S(1)} %bitcast.97), channel_id=1, source_target_pairs={{0,4},{1,5},{2,6},{3,7},{4,0},{5,1},{6,2},{7,3},{8,12},{9,13},{10,... | collective-permute-start | bytes 1572872 | tf_op jit(solution)/shard_map/ppermute | solution.py:52
  206.2 12.7 %collective-permute-start.12 = (bf16[2,64,1024]{2,1,0:T(8,128)(2,1)S(1)}, bf16[2,64,1024]{2,1,0:T(8,128)(2,1)S(1)}, u32[]{:S(2)}, u32[]{:S(2)}) collective-permute-start(bf16[2,64,1024]{2,1,0:T(8,128)(2,1)S(1)} %slice_bitcast_fusion.3), channel_id=1, source_target_pairs={{0,4},{1,5},{2,6},{3,7},{4,0},{5,1},{6,2},{7,3},{8,12},{9,13},{10,... | collective-permute-start | bytes 786440 | tf_op jit(solution)/shard_map/ppermute | solution.py:52
  208.0 22.5 %copy-start.5 = (f32[64,2048]{1,0:T(8,128)S(1)}, f32[64,2048]{1,0:T(8,128)}, u32[]{:S(2)}) copy-start(f32[64,2048]{1,0:T(8,128)} %copy-done.4) | copy-start | bytes 1572868
  208.0 23.3 %copy-start.1 = (bf16[64,2,96,128]{3,2,1,0:T(8,128)(2,1)S(1)}, bf16[64,2,96,128]{3,2,1,0:T(8,128)(2,1)}, u32[]{:S(2)}) copy-start(bf16[64,2,96,128]{3,2,1,0:T(8,128)(2,1)} %param.16) | copy-start | bytes 9437188
  208.2 17.1 %collective-permute-start.16 = (bf16[2,64,1024]{2,1,0:T(8,128)(2,1)S(1)}, bf16[2,64,1024]{2,1,0:T(8,128)(2,1)S(1)}, u32[]{:S(2)}, u32[]{:S(2)}) collective-permute-start(bf16[2,64,1024]{2,1,0:T(8,128)(2,1)S(1)} %slice_bitcast_fusion.1), channel_id=1, source_target_pairs={{0,8},{1,9},{2,10},{3,11},{4,12},{5,13},{6,14},{7,15},{8,0},{9,1},... | collective-permute-start | bytes 786440 | tf_op jit(solution)/shard_map/ppermute | solution.py:52
  219.0 8.7 %collective-permute-start.13 = (bf16[64,1024]{1,0:T(8,128)(2,1)S(1)}, bf16[64,1024]{1,0:T(8,128)(2,1)S(1)}, u32[]{:S(2)}, u32[]{:S(2)}) collective-permute-start(bf16[64,1024]{1,0:T(8,128)(2,1)S(1)} %slice_bitcast_fusion.7), channel_id=1, source_target_pairs={{0,8},{1,9},{2,10},{3,11},{4,12},{5,13},{6,14},{7,15},{8,0},{9,1},... | collective-permute-start | bytes 393224 | tf_op jit(solution)/shard_map/ppermute | solution.py:52
  225.4 5.0 %collective-permute-start.17 = (bf16[64,1024]{1,0:T(8,128)(2,1)S(1)}, bf16[64,1024]{1,0:T(8,128)(2,1)S(1)}, u32[]{:S(2)}, u32[]{:S(2)}) collective-permute-start(bf16[64,1024]{1,0:T(8,128)(2,1)S(1)} %slice_bitcast_fusion.5), channel_id=1, source_target_pairs={{0,2},{1,3},{2,0},{3,1},{4,6},{5,7},{6,4},{7,5},{8,10},{9,11},{10,... | collective-permute-start | bytes 393224 | tf_op jit(solution)/shard_map/ppermute | solution.py:52

commit v5 on v4

--- a/solution.py
+++ b/solution.py
@@ -62,16 +62,25 @@
     return lax.optimization_barrier((tuple(values), tuple(others)))[0]
 
 
-def load_weights(places, piece_refs, weights, sems, grp):
+def load_weights(places, piece_refs, weights, sems, me, grp):
     half = weights.shape[-1] // 2
     copies = []
-    for number, (matrix, side) in enumerate(places):
+    for index, (number, part, matrix, sources, side) in enumerate(places):
+        if sources is None:
+            span = pl.ds(0, weights.shape[1])
+        elif sources < PLANE:
+            span = pl.ds(me ^ sources, 1)
+        else:
+            span = pl.ds(((me // PLANE) ^ (sources // PLANE)) * PLANE, PLANE)
         if side is None:
             lanes = pl.ds(0, 2 * half)
         else:
             lanes = pl.ds(pl.multiple_of((grp ^ side) * half, LANES), half)
-        target = weights.at[matrix, :, :, lanes]
-        copies.append(pltpu.make_async_copy(piece_refs[number], target, sems.at[number]))
+        piece = piece_refs[number]
+        if part is not None:
+            piece = piece.at[part]
+        target = weights.at[matrix, span, :, lanes]
+        copies.append(pltpu.make_async_copy(piece, target, sems.at[index]))
     for copy in copies:
         copy.start()
     for copy in copies:
@@ -85,7 +94,7 @@
 
     @pl.when(step == 0)
     def load():
-        load_weights(places, piece_refs, weights, sems, where_ref[1])
+        load_weights(places, piece_refs, weights, sems, me, where_ref[1])
 
     @pl.when(step < pl.num_programs(0) // 2)
     def early():
@@ -123,7 +132,7 @@
         @pl.when(step == me // PLANE)
         def near():
             for bits, ref in enumerate(near_refs):
-                weights[pl.ds((me ^ bits) % PLANE, 1), :cut, other] = ref[...]
+                weights[pl.ds((me ^ bits) % PLANE, 1), :cut, other] = ref[:, :cut, :]
 
         @pl.when(step != me // PLANE)
         def far():
@@ -198,7 +207,7 @@
                 (block, cut, size), lambda i, w: (jnp.maximum((i ^ (w[0] // PLANE)) - 1, 0), 0, 0)
             )
         )
-        in_specs += [pl.BlockSpec((1, cut, size), lambda i, w: (0, 0, 0))] * len(near)
+        in_specs += [pl.BlockSpec((1, rows, size), lambda i, w: (1, 0, 0))] * len(near)
         pieces += [far] + near
     grid_spec = pltpu.PrefetchScalarGridSpec(
         num_scalar_prefetch=1,
@@ -281,7 +290,7 @@
 
     def beside(bits, deps):
         (start,) = after([(1 - grp) * half], deps)
-        block = lax.dynamic_slice(learner_weights, (me ^ bits, 2, 0, start), (1, 1, cut, half))[0]
+        block = lax.dynamic_slice(learner_weights, (me ^ bits, 1, 0, start), (1, 2, rows, half))[0]
         return swap_ep(block, bits) if bits else block
 
     def arrays(*values):
@@ -321,12 +330,12 @@
     rest = len(stages) - 3
     for bits in stages[:rest]:
         tokens, other = gather(tokens, bits)
-    up = bring(up_block, [gate, other])
+    near = [beside(bits, []) for bits in range(PLANE)] if split else []
+    up = bring(up_block, [gate, other] + near)
     gate_far = swap_grp(gate) if split else None
     tokens, other = gather(tokens, stages[rest])
     down_a = bring(down_a_block, [up, other] + arrays(gate_far))
-    near = [beside(bits, [up]) for bits in range(PLANE)] if split else []
-    up_far = swap_grp(up) if split else None
+    up_far = swapped(up)
     tokens, other = gather(tokens, stages[rest + 1])
     down_b = bring(down_b_block, [down_a, other] + arrays(up_far))
     down_a_far = swapped(down_a)
@@ -335,14 +344,22 @@
     pieces, places = [], []
     side = 0 if split else None
     for matrix, (mine, far) in enumerate(((gate, gate_far), (up, up_far))):
-        places.append((matrix, side))
+        places.append((len(pieces), None, matrix, None, side))
         pieces.append(mine)
-        if split:
-            places.append((matrix, 1))
+        if split and matrix == 0:
+            places.append((len(pieces), None, matrix, None, 1))
             pieces.append(far)
+        elif split:
+            for k in range(1, count // PLANE):
+                part = pl.ds((k - 1) * PLANE, PLANE)
+                places.append((len(pieces), part, matrix, k * PLANE, 1))
+            pieces.append(far)
+    for bits, block in enumerate(near):
+        places.append((len(pieces), pl.ds(0, 1), 1, bits, 1))
+        pieces.append(block)
     hidden = run_hidden(tokens, other, pieces, places, (2, count, rows, ff), experts)
     lower = stages[-2::-1]
-    orders = (lower, lower[1:] + lower[:1])
+    orders = (lower, lower[1:-1] + lower[:1] + lower[-1:])
     products = run_down(hidden, down_a, down_b, down_a_far, near, rows, width)
     kept = products[0::2]
     given = [swap_ep(give, 1) for give in products[1::2]]

time: 232 us -> 226 us (0.974)
  waiting for transfers between devices: 124 us -> 118 us
  other arithmetic: 12.5 us -> 10 us
    ppermute x15, waiting for transfers between devices: 109 us -> 104 us  [swap_ep(): return lax.ppermute(x, 'ep', [(i, i ^ bits) for i in range(count)])]
  transfers between devices with their start and end apart: 22 -> 22, of which waited for: 13 -> 10; matrix products, arithmetic and copies ran while one was open for 16% -> 15% of each run, Pallas kernels for 6% -> 6%
where the time goes in v5:
time: 226 us
  waiting for transfers between devices  118 us (52%)
  starting transfers between devices  44.4 us (20%)
  Pallas kernels  22.8 us (10%)
  local copies, waits for them, and re-layouts  17.8 us (8%)
  matrix products  12 us (5%)
  other arithmetic  10 us (4%)
    ppermute x15, waiting for transfers between devices, swap_ep(): return lax.ppermute(x, 'ep', [(i, i ^ bits) for i in range(count)])  104 us
    all_to_all x4, starting transfers between devices, bring(): return lax.all_to_all(block, 'ep', split_axis=0, concat_axis=0, tiled=True)  20.3 us
    ppermute x15, starting transfers between devices, swap_ep(): return lax.ppermute(x, 'ep', [(i, i ^ bits) for i in range(count)])  19.3 us
    pallas_call x1, Pallas kernels, run_hidden(): pl.pallas_call(functools.partial(hidden_kernel, places, experts), grid_sp...  13.6 us
    squeeze x4, local copies, waits for them, and re-layouts, cut_out(): lax.dynamic_slice(learner_weights, (0, matrix, low, start), (experts, 1,...  11.6 us
    pallas_call x1, Pallas kernels, run_down(): pl.pallas_call(functools.partial(down_kernel, cut, far is not None), grid...  9.13 us
    all_to_all x4, waiting for transfers between devices, bring(): return lax.all_to_all(block, 'ep', split_axis=0, concat_axis=0, tiled=True)  7.69 us
    ppermute x3, waiting for transfers between devices, swap_grp(): return lax.ppermute(x, 'grp', [(0, 1), (1, 0)])  6.25 us
  transfers between devices with their start and end apart: 22, of which 10 were waited for; matrix products, arithmetic and copies ran while one was open for 15% of the time, Pallas kernels for 6%

profile of v5, /device:TPU:0, one launch (start us, length us, event | category | flops | bytes accessed | tf_op | source)
XLA Modules:
  0.0 225.6 jit_solution(7586277932238373273)
XLA Ops:
  0.0 3.0 %dynamic-slice_bitcast_fusion.1 = bf16[16,128,384]{2,1,0:T(8,128)(2,1)} fusion(bf16[16,3,128,768]{3,2,1,0:T(8,128)(2,1)} %param.23, s32[]{:T(128)S(6)} %select_n.61), kind=kLoop, calls=%fused_computation.5 | loop fusion | bytes 3145732 | tf_op jit(solution)/shard_map/squeeze | solution.py:274
  3.0 7.5 %all-to-all-start = ((bf16[16,128,384]{2,1,0:T(8,128)(2,1)}), bf16[16,128,384]{2,1,0:T(8,128)(2,1)}, u32[]{:S(2)}, u32[]{:S(2)}) async-start(bf16[16,128,384]{2,1,0:T(8,128)(2,1)} %dynamic-slice_bitcast_fusion.1), calls=%async_computation | async-start | bytes 3145728 | tf_op jit(solution)/shard_map/all_to_all | solution.py:280
  10.6 0.3 fusion.11
  11.0 4.5 %fusion.24 = (f32[64,2,8]{2,1,0:T(2,128)S(1)}, f32[64,2,8,96]{3,2,1,0:T(8,128)}) fusion(bf16[64,2,96,128]{3,2,1,0:T(8,128)(2,1)} %param.15, bf16[64,16,128]{2,1,0:T(8,128)(2,1)S(1)} %copy-done.16, pred[64,96]{1,0:T(8,128)(4,1)S(1)} %iota_compare_fusion.1), kind=kOutput, calls=%fused_computation.78 | convolution fusion | flops 25459712 | bytes 3811328 | tf_op jit(solution)/shard_map/skgd,skld->skgl/dot_general | solution.py:22
  15.6 0.1 copy.33
  15.7 1.4 fusion.6
  17.2 0.1 copy.38
  17.3 0.1 copy.39
  17.5 0.1 copy.35
  17.6 0.1 copy.36
  17.8 2.1 fusion.1
  19.9 5.1 %multiply_reduce_fusion = (f32[64]{0:T(128)S(1)}, f32[64,2048]{1,0:T(8,128)S(1)}) fusion(bf16[2048,2048]{1,0:T(8,128)(2,1)} %param.19, bf16[8,8,16,128]{3,2,1,0:T(8,128)(2,1)S(1)} %bitcast.100, bf16[64,2048]{1,0:T(8,128)(2,1)S(1)} %copy-done.15), kind=kOutput, calls=%fused_computation.28 | convolution fusion | flops 537395136 | bytes 9437440 | tf_op jit(solution)/shard_map/dot_general | solution.py:310
  25.0 0.1 multiply_convert_fusion
  25.1 0.1 concatenate.23
  25.2 2.8 %collective-permute-start = (bf16[64,2176]{1,0:T(8,128)(2,1)S(1)}, bf16[64,2176]{1,0:T(8,128)(2,1)S(1)}, u32[]{:S(2)}, u32[]{:S(2)}) collective-permute-start(bf16[64,2176]{1,0:T(8,128)(2,1)S(1)} %concatenate.23), channel_id=1, source_target_pairs={{0,8},{1,9},{2,10},{3,11},{4,12},{5,13},{6,14},{7,15},{8,0},{9,1},... | collective-permute-start | bytes 835592 | tf_op jit(solution)/shard_map/ppermute | solution.py:52
  28.1 2.0 dynamic-slice_bitcast_fusion.3
  30.1 0.9 collective-permute-start.7
  31.0 0.6 collective-permute-start.5
  31.6 0.6 collective-permute-start.6
  32.2 2.1 slice_bitcast_fusion
  34.3 3.0 %dynamic-slice_bitcast_fusion.2 = bf16[16,96,384]{2,1,0:T(8,128)(2,1)} fusion(bf16[16,3,128,768]{3,2,1,0:T(8,128)(2,1)} %param.23, s32[]{:T(128)S(6)} %select_n.62), kind=kLoop, calls=%fused_computation.11 | loop fusion | bytes 2359300 | tf_op jit(solution)/shard_map/squeeze | solution.py:274
  37.3 3.5 %dynamic-slice_bitcast_fusion = bf16[16,128,384]{2,1,0:T(8,128)(2,1)} fusion(bf16[16,3,128,768]{3,2,1,0:T(8,128)(2,1)} %param.23, s32[]{:T(128)S(6)} %select_n.62), kind=kLoop, calls=%fused_computation.4 | loop fusion | bytes 3145732 | tf_op jit(solution)/shard_map/squeeze | solution.py:274
  40.8 7.7 %all-to-all-done.refs_0_ = bf16[16,128,384]{2,1,0:T(8,128)(2,1)} async-done(((bf16[16,128,384]{2,1,0:T(8,128)(2,1)}), bf16[16,128,384]{2,1,0:T(8,128)(2,1)}, u32[]{:S(2)}, u32[]{:S(2)}) %all-to-all-start) | async-done | bytes 1572896 | tf_op jit(solution)/shard_map/all_to_all | solution.py:280
  48.6 11.7 %collective-permute-done = bf16[64,2176]{1,0:T(8,128)(2,1)S(1)} collective-permute-done((bf16[64,2176]{1,0:T(8,128)(2,1)S(1)}, bf16[64,2176]{1,0:T(8,128)(2,1)S(1)}, u32[]{:S(2)}, u32[]{:S(2)}) %collective-permute-start) | collective-permute-done | bytes 278560 | tf_op jit(solution)/shard_map/ppermute | solution.py:52
  60.2 3.7 %all-to-all-start.1 = ((bf16[16,128,384]{2,1,0:T(8,128)(2,1)}), bf16[16,128,384]{2,1,0:T(8,128)(2,1)S(1)}, u32[]{:S(2)}, u32[]{:S(2)}) async-start(bf16[16,128,384]{2,1,0:T(8,128)(2,1)} %dynamic-slice_bitcast_fusion), calls=%async_computation.1 | async-start | bytes 3145728 | tf_op jit(solution)/shard_map/all_to_all | solution.py:280
  64.0 1.6 collective-permute-start.4
  65.6 1.9 collective-permute-start.1
  67.5 36.8 %collective-permute-done.1 = bf16[128,2176]{1,0:T(8,128)(2,1)S(1)} collective-permute-done((bf16[128,2176]{1,0:T(8,128)(2,1)S(1)}, bf16[128,2176]{1,0:T(8,128)(2,1)S(1)}, u32[]{:S(2)}, u32[]{:S(2)}) %collective-permute-start.1) | collective-permute-done | bytes 557088 | tf_op jit(solution)/shard_map/ppermute | solution.py:52
  104.3 1.2 pad_maximum_fusion.2
  105.5 1.5 collective-permute-start.2
  107.0 4.0 %all-to-all-start.2 = ((bf16[16,96,384]{2,1,0:T(8,128)(2,1)}), bf16[16,96,384]{2,1,0:T(8,128)(2,1)S(1)}, u32[]{:S(2)}, u32[]{:S(2)}) async-start(bf16[16,96,384]{2,1,0:T(8,128)(2,1)} %dynamic-slice_bitcast_fusion.2), calls=%async_computation.2 | async-start | bytes 2359296 | tf_op jit(solution)/shard_map/all_to_all | solution.py:280
  111.1 0.1 constant_dynamic-slice_fusion.5
  111.3 0.2 pad_maximum_fusion.1
  111.4 1.6 collective-permute-start.8
  113.0 29.7 %collective-permute-done.2 = bf16[256,2176]{1,0:T(8,128)(2,1)} collective-permute-done((bf16[256,2176]{1,0:T(8,128)(2,1)}, bf16[256,2176]{1,0:T(8,128)(2,1)}, u32[]{:S(2)}, u32[]{:S(2)}) %collective-permute-start.2) | collective-permute-done | bytes 1114144 | tf_op jit(solution)/shard_map/ppermute | solution.py:52
  142.8 2.8 %pad_maximum_fusion.first_ref = bf16[512,2176]{1,0:T(8,128)(2,1)} fusion(bf16[256,2176]{1,0:T(8,128)(2,1)} %collective-permute-done.2, bf16[128,2176]{1,0:T(8,128)(2,1)S(1)} %copy-done.8, bf16[64,2176]{1,0:T(8,128)(2,1)S(1)} %collective-permute-done, bf16[64,2176]{1,0:T(8,128)(2,1)S(1)} %concatenate.23), kind=kLoop, calls=%fused_computation.1 | loop fusion | flops 8912896 | bytes 4456448 | tf_op jit(solution)/shard_map/concatenate | solution.py:328
  145.6 1.1 copy-done.9
  146.6 5.1 %all-to-all-start.3 = ((bf16[16,32,768]{2,1,0:T(8,128)(2,1)}), bf16[16,32,768]{2,1,0:T(8,128)(2,1)S(1)}, u32[]{:S(2)}, u32[]{:S(2)}) async-start(bf16[16,32,768]{2,1,0:T(8,128)(2,1)} %slice_bitcast_fusion), calls=%async_computation.3 | async-start | bytes 1572864 | tf_op jit(solution)/shard_map/all_to_all | solution.py:280
  151.7 0.1 constant_dynamic-slice_fusion.2
  151.8 0.1 pad_maximum_fusion.3
  152.0 1.6 collective-permute-start.9
  153.6 0.6 pad_add_fusion.where_ref
  154.1 13.6 %shard_map.118.hidden_ref = bf16[1024,768]{1,0:T(8,128)(2,1)} custom-call(s32[2]{0:T(128)} %pad_add_fusion.where_ref, bf16[512,2176]{1,0:T(8,128)(2,1)} %pad_maximum_fusion.first_ref, bf16[512,2176]{1,0:T(8,128)(2,1)} %collective-permute-done.3.second_ref, bf16[16,128,384]{2,1,0:T(8,128)(2,1)} %all-to-all-done.refs_0_, ...), custom_call_target="tpu_custom_call" | custom-call | tf_op jit(solution)/shard_map/pallas_call | solution.py:181
  167.8 6.2 %collective-permute-done.9.refs_2_ = bf16[12,96,384]{2,1,0:T(8,128)(2,1)S(1)} collective-permute-done((bf16[12,96,384]{2,1,0:T(8,128)(2,1)S(1)}, bf16[12,96,384]{2,1,0:T(8,128)(2,1)S(1)}, u32[]{:S(2)}, u32[]{:S(2)}) %collective-permute-start.9) | collective-permute-done | bytes 884768 | tf_op jit(solution)/shard_map/ppermute | solution.py:56
  174.0 0.9 copy-done.11
  174.9 0.9 copy-done.6
  175.8 9.1 %shard_map.119 = (bf16[512,1024]{1,0:T(8,128)(2,1)}, bf16[512,1024]{1,0:T(8,128)(2,1)}, bf16[512,1024]{1,0:T(8,128)(2,1)}, bf16[512,1024]{1,0:T(8,128)(2,1)}) custom-call(s32[2]{0:T(128)} %pad_add_fusion.where_ref, bf16[1024,768]{1,0:T(8,128)(2,1)} %shard_map.118.hidden_ref, bf16[16,96,384]{2,1,0:T(8,128)(2,1)} %copy-done.3, bf16[16,32,768]{2,1,0:T(8,128)(2,1)} %copy-done.6, ...), custom_call_target="tpu_custom_call" | custom-call | tf_op jit(solution)/shard_map/pallas_call | solution.py:219
  185.0 0.5 collective-permute-start.14
  185.5 2.4 %collective-permute-done.10 = bf16[512,1024]{1,0:T(8,128)(2,1)S(1)} collective-permute-done((bf16[512,1024]{1,0:T(8,128)(2,1)}, bf16[512,1024]{1,0:T(8,128)(2,1)S(1)}, u32[]{:S(2)}, u32[]{:S(2)}) %collective-permute-start.10) | collective-permute-done | bytes 1048608 | tf_op jit(solution)/shard_map/ppermute | solution.py:52
  187.8 1.7 add_convert_fusion.1
  189.6 1.7 collective-permute-start.11
  191.3 0.4 add_convert_fusion
  191.8 1.5 collective-permute-start.15
  193.3 10.4 %collective-permute-done.11 = bf16[2,2,64,1024]{3,2,1,0:T(8,128)(2,1)S(1)} collective-permute-done((bf16[2,2,64,1024]{3,2,1,0:T(8,128)(2,1)S(1)}, bf16[2,2,64,1024]{3,2,1,0:T(8,128)(2,1)S(1)}, u32[]{:S(2)}, u32[]{:S(2)}) %collective-permute-start.11) | collective-permute-done | bytes 524320 | tf_op jit(solution)/shard_map/ppermute | solution.py:52
  203.7 0.2 fusion.3
  203.9 1.7 collective-permute-start.12
  205.6 0.2 fusion.2
  205.8 1.5 collective-permute-start.16
  207.4 4.1 %collective-permute-done.12 = bf16[2,64,1024]{2,1,0:T(8,128)(2,1)S(1)} collective-permute-done((bf16[2,64,1024]{2,1,0:T(8,128)(2,1)S(1)}, bf16[2,64,1024]{2,1,0:T(8,128)(2,1)S(1)}, u32[]{:S(2)}, u32[]{:S(2)}) %collective-permute-start.12) | collective-permute-done | bytes 262176 | tf_op jit(solution)/shard_map/ppermute | solution.py:52
  211.6 2.6 %collective-permute-start.13 = (bf16[64,1024]{1,0:T(8,128)(2,1)S(1)}, bf16[64,1024]{1,0:T(8,128)(2,1)S(1)}, u32[]{:S(2)}, u32[]{:S(2)}) collective-permute-start(bf16[64,1024]{1,0:T(8,128)(2,1)S(1)} %slice_bitcast_fusion.9), channel_id=1, source_target_pairs={{0,8},{1,9},{2,10},{3,11},{4,12},{5,13},{6,14},{7,15},{8,0},{9,1},... | collective-permute-start | bytes 393224 | tf_op jit(solution)/shard_map/ppermute | solution.py:52
  214.3 1.4 collective-permute-start.17
  215.7 7.5 %collective-permute-done.13 = bf16[64,1024]{1,0:T(8,128)(2,1)S(1)} collective-permute-done((bf16[64,1024]{1,0:T(8,128)(2,1)S(1)}, bf16[64,1024]{1,0:T(8,128)(2,1)S(1)}, u32[]{:S(2)}, u32[]{:S(2)}) %collective-permute-start.13) | collective-permute-done | bytes 131104 | tf_op jit(solution)/shard_map/ppermute | solution.py:52
  223.2 1.5 collective-permute-done.17
  224.8 0.8 add_convert_fusion.2
  (80 shorter events, 0.9 us)
Async XLA Ops:
  0.0 17.7 %copy-start = (bf16[64,2,96,128]{3,2,1,0:T(8,128)(2,1)S(1)}, bf16[64,2,96,128]{3,2,1,0:T(8,128)(2,1)}, u32[]{:S(2)}) copy-start(bf16[64,2,96,128]{3,2,1,0:T(8,128)(2,1)} %param.16) | copy-start | bytes 9437188
  3.0 7.5 %copy-start.21 = (s32[64]{0:T(128)S(1)}, s32[64]{0:T(128)}, u32[]{:S(2)}) copy-start(s32[64]{0:T(128)} %param.17) | copy-start | bytes 772
  3.0 7.6 %copy-start.16 = (bf16[64,16,128]{2,1,0:T(8,128)(2,1)S(1)}, bf16[64,16,128]{2,1,0:T(8,128)(2,1)}, u32[]{:S(2)}) copy-start(bf16[64,16,128]{2,1,0:T(8,128)(2,1)} %param.12) | copy-start | bytes 786436
  3.0 7.6 %copy-start.22 = (bf16[64,2,128]{2,1,0:T(2,128)(2,1)S(1)}, bf16[64,2,128]{2,1,0:T(2,128)(2,1)}, u32[]{:S(2)}) copy-start(bf16[64,2,128]{2,1,0:T(2,128)(2,1)} %param.13) | copy-start | bytes 98308
  3.0 45.5 %all-to-all-start = ((bf16[16,128,384]{2,1,0:T(8,128)(2,1)}), bf16[16,128,384]{2,1,0:T(8,128)(2,1)}, u32[]{:S(2)}, u32[]{:S(2)}) async-start(bf16[16,128,384]{2,1,0:T(8,128)(2,1)} %dynamic-slice_bitcast_fusion.1), calls=%async_computation | async-start | bytes 3145728 | tf_op jit(solution)/shard_map/all_to_all | solution.py:280
  11.0 6.2 %copy-start.19 = (f32[64,8]{0,1:T(8,128)S(1)}, f32[64,8]{0,1:T(8,128)}, u32[]{:S(2)}) copy-start(f32[64,8]{0,1:T(8,128)} %param.22) | copy-start | bytes 6148
  11.0 6.2 %copy-start.20 = (s32[64,8]{0,1:T(8,128)S(1)}, s32[64,8]{0,1:T(8,128)}, u32[]{:S(2)}) copy-start(s32[64,8]{0,1:T(8,128)} %param.21) | copy-start | bytes 6148
  11.0 6.4 %copy-start.17 = (bf16[64,2,128]{2,1,0:T(2,128)(2,1)S(1)}, bf16[64,2,128]{2,1,0:T(2,128)(2,1)}, u32[]{:S(2)}) copy-start(bf16[64,2,128]{2,1,0:T(2,128)(2,1)} %param.14) | copy-start | bytes 98308
  17.7 2.1 copy-start.15
  19.8 5.1 %copy-start.18 = (f32[2048]{0:T(1024)S(1)}, f32[2048]{0:T(1024)}, u32[]{:S(2)}) copy-start(f32[2048]{0:T(1024)} %param.20) | copy-start | bytes 24580
  24.9 9.3 %copy-start.4 = (f32[64,2048]{1,0:T(8,128)}, f32[64,2048]{1,0:T(8,128)S(1)}, u32[]{:S(2)}) copy-start(f32[64,2048]{1,0:T(8,128)S(1)} %get-tuple-element.40) | copy-start | bytes 1572868
  25.2 35.0 %collective-permute-start = (bf16[64,2176]{1,0:T(8,128)(2,1)S(1)}, bf16[64,2176]{1,0:T(8,128)(2,1)S(1)}, u32[]{:S(2)}, u32[]{:S(2)}) collective-permute-start(bf16[64,2176]{1,0:T(8,128)(2,1)S(1)} %concatenate.23), channel_id=1, source_target_pairs={{0,8},{1,9},{2,10},{3,11},{4,12},{5,13},{6,14},{7,15},{8,0},{9,1},... | collective-permute-start | bytes 835592 | tf_op jit(solution)/shard_map/ppermute | solution.py:52
  30.1 18.5 %collective-permute-start.7 = (bf16[2,128,384]{2,1,0:T(8,128)(2,1)S(1)}, bf16[2,128,384]{2,1,0:T(8,128)(2,1)S(1)}, u32[]{:S(2)}, u32[]{:S(2)}) collective-permute-start(bf16[2,128,384]{2,1,0:T(8,128)(2,1)S(1)} %get-tuple-element.23), channel_id=1, source_target_pairs={{0,3},{1,2},{2,1},{3,0},{4,7},{5,6},{6,5},{7,4},{8,11},{9,10},{10,... | collective-permute-start | bytes 589832 | tf_op jit(solution)/shard_map/ppermute | solution.py:52
  31.0 17.5 %collective-permute-start.5 = (bf16[2,128,384]{2,1,0:T(8,128)(2,1)S(1)}, bf16[2,128,384]{2,1,0:T(8,128)(2,1)S(1)}, u32[]{:S(2)}, u32[]{:S(2)}) collective-permute-start(bf16[2,128,384]{2,1,0:T(8,128)(2,1)S(1)} %get-tuple-element.24), channel_id=1, source_target_pairs={{0,1},{1,0},{2,3},{3,2},{4,5},{5,4},{6,7},{7,6},{8,9},{9,8},{10,11... | collective-permute-start | bytes 589832 | tf_op jit(solution)/shard_map/ppermute | solution.py:52
  31.6 16.9 %collective-permute-start.6 = (bf16[2,128,384]{2,1,0:T(8,128)(2,1)S(1)}, bf16[2,128,384]{2,1,0:T(8,128)(2,1)S(1)}, u32[]{:S(2)}, u32[]{:S(2)}) collective-permute-start(bf16[2,128,384]{2,1,0:T(8,128)(2,1)S(1)} %get-tuple-element.26), channel_id=1, source_target_pairs={{0,2},{1,3},{2,0},{3,1},{4,6},{5,7},{6,4},{7,5},{8,10},{9,11},{10,... | collective-permute-start | bytes 589832 | tf_op jit(solution)/shard_map/ppermute | solution.py:52
  48.5 17.0 %copy-start.12 = (bf16[2,128,384]{2,1,0:T(8,128)(2,1)}, bf16[2,128,384]{2,1,0:T(8,128)(2,1)S(1)}, u32[]{:S(2)}) copy-start(bf16[2,128,384]{2,1,0:T(8,128)(2,1)S(1)} %collective-permute-done.7.refs_7_.refs_6_) | copy-start | bytes 589828
  48.5 56.9 %copy-start.13 = (bf16[2,128,384]{2,1,0:T(8,128)(2,1)}, bf16[2,128,384]{2,1,0:T(8,128)(2,1)S(1)}, u32[]{:S(2)}) copy-start(bf16[2,128,384]{2,1,0:T(8,128)(2,1)S(1)} %collective-permute-done.5.refs_5_.refs_4_) | copy-start | bytes 589828
  48.6 56.9 %copy-start.14 = (bf16[2,128,384]{2,1,0:T(8,128)(2,1)}, bf16[2,128,384]{2,1,0:T(8,128)(2,1)S(1)}, u32[]{:S(2)}) copy-start(bf16[2,128,384]{2,1,0:T(8,128)(2,1)S(1)} %collective-permute-done.6.refs_6_.refs_5_) | copy-start | bytes 589828
  60.2 46.8 %all-to-all-start.1 = ((bf16[16,128,384]{2,1,0:T(8,128)(2,1)}), bf16[16,128,384]{2,1,0:T(8,128)(2,1)S(1)}, u32[]{:S(2)}, u32[]{:S(2)}) async-start(bf16[16,128,384]{2,1,0:T(8,128)(2,1)} %dynamic-slice_bitcast_fusion), calls=%async_computation.1 | async-start | bytes 3145728 | tf_op jit(solution)/shard_map/all_to_all | solution.py:280
  64.0 43.0 %collective-permute-start.4 = (bf16[16,128,384]{2,1,0:T(8,128)(2,1)}, bf16[16,128,384]{2,1,0:T(8,128)(2,1)}, u32[]{:S(2)}, u32[]{:S(2)}) collective-permute-start(bf16[16,128,384]{2,1,0:T(8,128)(2,1)} %all-to-all-done.refs_0_), channel_id=1, source_target_pairs={{0,16},{16,0},{1,17},{17,1},{2,18},{18,2},{3,19},{19,3},{4,20},{20... | collective-permute-start | bytes 4718600 | tf_op jit(solution)/shard_map/ppermute | solution.py:56
  65.6 38.7 %collective-permute-start.1 = (bf16[128,2176]{1,0:T(8,128)(2,1)S(1)}, bf16[128,2176]{1,0:T(8,128)(2,1)S(1)}, u32[]{:S(2)}, u32[]{:S(2)}) collective-permute-start(bf16[128,2176]{1,0:T(8,128)(2,1)S(1)} %pad_maximum_fusion.4), channel_id=1, source_target_pairs={{0,4},{1,5},{2,6},{3,7},{4,0},{5,1},{6,2},{7,3},{8,12},{9,13},{10,... | collective-permute-start | bytes 1671176 | tf_op jit(solution)/shard_map/ppermute | solution.py:52
  104.3 2.7 %copy-start.7 = (bf16[128,2176]{1,0:T(8,128)(2,1)}, bf16[128,2176]{1,0:T(8,128)(2,1)S(1)}, u32[]{:S(2)}) copy-start(bf16[128,2176]{1,0:T(8,128)(2,1)S(1)} %collective-permute-done.1) | copy-start | bytes 1671172
  105.5 37.3 %collective-permute-start.2 = (bf16[256,2176]{1,0:T(8,128)(2,1)}, bf16[256,2176]{1,0:T(8,128)(2,1)}, u32[]{:S(2)}, u32[]{:S(2)}) collective-permute-start(bf16[256,2176]{1,0:T(8,128)(2,1)} %pad_maximum_fusion.2), channel_id=1, source_target_pairs={{0,2},{1,3},{2,0},{3,1},{4,6},{5,7},{6,4},{7,5},{8,10},{9,11},{10,... | collective-permute-start | bytes 3342344 | tf_op jit(solution)/shard_map/ppermute | solution.py:52
  107.0 4.2 %copy-start.2 = (bf16[16,128,384]{2,1,0:T(8,128)(2,1)}, bf16[16,128,384]{2,1,0:T(8,128)(2,1)S(1)}, u32[]{:S(2)}) copy-start(bf16[16,128,384]{2,1,0:T(8,128)(2,1)S(1)} %all-to-all-done.1.refs_2_) | copy-start | bytes 4718596
  107.0 38.5 %all-to-all-start.2 = ((bf16[16,96,384]{2,1,0:T(8,128)(2,1)}), bf16[16,96,384]{2,1,0:T(8,128)(2,1)S(1)}, u32[]{:S(2)}, u32[]{:S(2)}) async-start(bf16[16,96,384]{2,1,0:T(8,128)(2,1)} %dynamic-slice_bitcast_fusion.2), calls=%async_computation.2 | async-start | bytes 2359296 | tf_op jit(solution)/shard_map/all_to_all | solution.py:280
  111.1 31.7 %copy-start.8 = (bf16[128,2176]{1,0:T(8,128)(2,1)S(1)}, bf16[128,2176]{1,0:T(8,128)(2,1)}, u32[]{:S(2)}) copy-start(bf16[128,2176]{1,0:T(8,128)(2,1)} %copy-done.7) | copy-start | bytes 1671172
  111.4 34.1 %collective-permute-start.8 = (bf16[12,128,384]{2,1,0:T(8,128)(2,1)S(1)}, bf16[12,128,384]{2,1,0:T(8,128)(2,1)S(1)}, u32[]{:S(2)}, u32[]{:S(2)}) collective-permute-start(bf16[12,128,384]{2,1,0:T(8,128)(2,1)S(1)} %pad_maximum_fusion.1), channel_id=1, source_target_pairs={{0,16},{16,0},{1,17},{17,1},{2,18},{18,2},{3,19},{19,3},{4,20},{20... | collective-permute-start | bytes 3538952 | tf_op jit(solution)/shard_map/ppermute | solution.py:56
  145.5 8.6 %collective-permute-start.3 = (bf16[512,2176]{1,0:T(8,128)(2,1)}, bf16[512,2176]{1,0:T(8,128)(2,1)}, u32[]{:S(2)}, u32[]{:S(2)}) collective-permute-start(bf16[512,2176]{1,0:T(8,128)(2,1)} %pad_maximum_fusion.first_ref), channel_id=1, source_target_pairs={{0,1},{1,0},{2,3},{3,2},{4,5},{5,4},{6,7},{7,6},{8,9},{9,8},{10,11... | collective-permute-start | bytes 6684680 | tf_op jit(solution)/shard_map/ppermute | solution.py:52
  145.5 1.1 copy-start.9
  145.6 6.4 %copy-start.3 = (bf16[16,96,384]{2,1,0:T(8,128)(2,1)}, bf16[16,96,384]{2,1,0:T(8,128)(2,1)S(1)}, u32[]{:S(2)}) copy-start(bf16[16,96,384]{2,1,0:T(8,128)(2,1)S(1)} %all-to-all-done.2.refs_0_) | copy-start | bytes 3538948
  146.6 27.4 %all-to-all-start.3 = ((bf16[16,32,768]{2,1,0:T(8,128)(2,1)}), bf16[16,32,768]{2,1,0:T(8,128)(2,1)S(1)}, u32[]{:S(2)}, u32[]{:S(2)}) async-start(bf16[16,32,768]{2,1,0:T(8,128)(2,1)} %slice_bitcast_fusion), calls=%async_computation.3 | async-start | bytes 1572864 | tf_op jit(solution)/shard_map/all_to_all | solution.py:280
  152.0 22.0 %collective-permute-start.9 = (bf16[12,96,384]{2,1,0:T(8,128)(2,1)S(1)}, bf16[12,96,384]{2,1,0:T(8,128)(2,1)S(1)}, u32[]{:S(2)}, u32[]{:S(2)}) collective-permute-start(bf16[12,96,384]{2,1,0:T(8,128)(2,1)S(1)} %pad_maximum_fusion.3), channel_id=1, source_target_pairs={{0,16},{16,0},{1,17},{17,1},{2,18},{18,2},{3,19},{19,3},{4,20},{20... | collective-permute-start | bytes 2654216 | tf_op jit(solution)/shard_map/ppermute | solution.py:56
  174.0 0.9 copy-start.11
  174.9 0.9 copy-start.6
  185.0 2.9 %collective-permute-start.10 = (bf16[512,1024]{1,0:T(8,128)(2,1)}, bf16[512,1024]{1,0:T(8,128)(2,1)S(1)}, u32[]{:S(2)}, u32[]{:S(2)}) collective-permute-start(bf16[512,1024]{1,0:T(8,128)(2,1)} %get-tuple-element.20), channel_id=1, source_target_pairs={{0,1},{1,0},{2,3},{3,2},{4,5},{5,4},{6,7},{7,6},{8,9},{9,8},{10,11... | collective-permute-start | bytes 3145736 | tf_op jit(solution)/shard_map/ppermute | solution.py:52
  185.0 6.4 %collective-permute-start.14 = (bf16[512,1024]{1,0:T(8,128)(2,1)}, bf16[512,1024]{1,0:T(8,128)(2,1)S(1)}, u32[]{:S(2)}, u32[]{:S(2)}) collective-permute-start(bf16[512,1024]{1,0:T(8,128)(2,1)} %get-tuple-element.22), channel_id=1, source_target_pairs={{0,1},{1,0},{2,3},{3,2},{4,5},{5,4},{6,7},{7,6},{8,9},{9,8},{10,11... | collective-permute-start | bytes 3145736 | tf_op jit(solution)/shard_map/ppermute | solution.py:52
  187.8 3.5 %copy-start.10 = (bf16[512,1024]{1,0:T(8,128)(2,1)S(1)}, bf16[512,1024]{1,0:T(8,128)(2,1)}, u32[]{:S(2)}) copy-start(bf16[512,1024]{1,0:T(8,128)(2,1)} %get-tuple-element.21) | copy-start | bytes 3145732
  189.6 14.0 %collective-permute-start.11 = (bf16[2,2,64,1024]{3,2,1,0:T(8,128)(2,1)S(1)}, bf16[2,2,64,1024]{3,2,1,0:T(8,128)(2,1)S(1)}, u32[]{:S(2)}, u32[]{:S(2)}) collective-permute-start(bf16[2,2,64,1024]{3,2,1,0:T(8,128)(2,1)S(1)} %bitcast.101), channel_id=1, source_target_pairs={{0,2},{1,3},{2,0},{3,1},{4,6},{5,7},{6,4},{7,5},{8,10},{9,11},{10,... | collective-permute-start | bytes 1572872 | tf_op jit(solution)/shard_map/ppermute | solution.py:52
  191.8 13.8 %collective-permute-start.15 = (bf16[2,2,64,1024]{3,2,1,0:T(8,128)(2,1)S(1)}, bf16[2,2,64,1024]{3,2,1,0:T(8,128)(2,1)S(1)}, u32[]{:S(2)}, u32[]{:S(2)}) collective-permute-start(bf16[2,2,64,1024]{3,2,1,0:T(8,128)(2,1)S(1)} %slice_bitcast_fusion.1), channel_id=1, source_target_pairs={{0,4},{1,5},{2,6},{3,7},{4,0},{5,1},{6,2},{7,3},{8,12},{9,13},{10,... | collective-permute-start | bytes 1572872 | tf_op jit(solution)/shard_map/ppermute | solution.py:52
  203.9 20.9 %copy-start.5 = (f32[64,2048]{1,0:T(8,128)S(1)}, f32[64,2048]{1,0:T(8,128)}, u32[]{:S(2)}) copy-start(f32[64,2048]{1,0:T(8,128)} %copy-done.4) | copy-start | bytes 1572868
  203.9 7.6 %collective-permute-start.12 = (bf16[2,64,1024]{2,1,0:T(8,128)(2,1)S(1)}, bf16[2,64,1024]{2,1,0:T(8,128)(2,1)S(1)}, u32[]{:S(2)}, u32[]{:S(2)}) collective-permute-start(bf16[2,64,1024]{2,1,0:T(8,128)(2,1)S(1)} %slice_bitcast_fusion.5), channel_id=1, source_target_pairs={{0,4},{1,5},{2,6},{3,7},{4,0},{5,1},{6,2},{7,3},{8,12},{9,13},{10,... | collective-permute-start | bytes 786440 | tf_op jit(solution)/shard_map/ppermute | solution.py:52
  205.6 20.0 %copy-start.1 = (bf16[64,2,96,128]{3,2,1,0:T(8,128)(2,1)S(1)}, bf16[64,2,96,128]{3,2,1,0:T(8,128)(2,1)}, u32[]{:S(2)}) copy-start(bf16[64,2,96,128]{3,2,1,0:T(8,128)(2,1)} %param.16) | copy-start | bytes 9437188
  205.8 8.3 %collective-permute-start.16 = (bf16[2,64,1024]{2,1,0:T(8,128)(2,1)S(1)}, bf16[2,64,1024]{2,1,0:T(8,128)(2,1)S(1)}, u32[]{:S(2)}, u32[]{:S(2)}) collective-permute-start(bf16[2,64,1024]{2,1,0:T(8,128)(2,1)S(1)} %slice_bitcast_fusion.3), channel_id=1, source_target_pairs={{0,2},{1,3},{2,0},{3,1},{4,6},{5,7},{6,4},{7,5},{8,10},{9,11},{10,... | collective-permute-start | bytes 786440 | tf_op jit(solution)/shard_map/ppermute | solution.py:52
  211.6 11.6 %collective-permute-start.13 = (bf16[64,1024]{1,0:T(8,128)(2,1)S(1)}, bf16[64,1024]{1,0:T(8,128)(2,1)S(1)}, u32[]{:S(2)}, u32[]{:S(2)}) collective-permute-start(bf16[64,1024]{1,0:T(8,128)(2,1)S(1)} %slice_bitcast_fusion.9), channel_id=1, source_target_pairs={{0,8},{1,9},{2,10},{3,11},{4,12},{5,13},{6,14},{7,15},{8,0},{9,1},... | collective-permute-start | bytes 393224 | tf_op jit(solution)/shard_map/ppermute | solution.py:52
  214.3 10.5 %collective-permute-start.17 = (bf16[64,1024]{1,0:T(8,128)(2,1)S(1)}, bf16[64,1024]{1,0:T(8,128)(2,1)S(1)}, u32[]{:S(2)}, u32[]{:S(2)}) collective-permute-start(bf16[64,1024]{1,0:T(8,128)(2,1)S(1)} %slice_bitcast_fusion.7), channel_id=1, source_target_pairs={{0,8},{1,9},{2,10},{3,11},{4,12},{5,13},{6,14},{7,15},{8,0},{9,1},... | collective-permute-start | bytes 393224 | tf_op jit(solution)/shard_map/ppermute | solution.py:52

commit v6 on v5

--- a/solution.py
+++ b/solution.py
@@ -8,7 +8,7 @@
 from jax.sharding import PartitionSpec as P
 
 LANES = 128
-PLANE = 4
+PLANE, NEAR = 4, 2
 
 
 def attend(queries, new_keys, new_values, cache_keys, cache_values, cache_lengths):
@@ -129,12 +129,16 @@
         far_ref, near_refs = refs[2], refs[3:-5]
         weights[:, :cut, own] = mine_ref[...]
 
-        @pl.when(step == me // PLANE)
-        def near():
-            for bits, ref in enumerate(near_refs):
-                weights[pl.ds((me ^ bits) % PLANE, 1), :cut, other] = ref[:, :cut, :]
-
-        @pl.when(step != me // PLANE)
+        flipped = step ^ (me // PLANE)
+        for plane in range(NEAR):
+
+            @pl.when(flipped == plane)
+            def near(plane=plane):
+                for bits in range(PLANE):
+                    block = near_refs[plane * PLANE + bits][:, :cut, :]
+                    weights[pl.ds((me ^ bits) % PLANE, 1), :cut, other] = block
+
+        @pl.when(flipped >= NEAR)
         def far():
             weights[:, :cut, other] = far_ref[...]
     else:
@@ -202,12 +206,14 @@
     ]
     pieces = [mine, whole]
     if far is not None:
-        in_specs.append(
-            pl.BlockSpec(
-                (block, cut, size), lambda i, w: (jnp.maximum((i ^ (w[0] // PLANE)) - 1, 0), 0, 0)
-            )
-        )
-        in_specs += [pl.BlockSpec((1, rows, size), lambda i, w: (1, 0, 0))] * len(near)
+
+        def from_far(i, w):
+            return jnp.maximum((i ^ (w[0] // PLANE)) - NEAR, 0), 0, 0
+
+        in_specs.append(pl.BlockSpec((block, cut, size), from_far))
+        for array in near:
+            last, height = array.shape[0] - 1, array.shape[1]
+            in_specs.append(pl.BlockSpec((1, height, size), lambda i, w, last=last: (last, 0, 0)))
         pieces += [far] + near
     grid_spec = pltpu.PrefetchScalarGridSpec(
         num_scalar_prefetch=1,
@@ -266,7 +272,7 @@
     grp = lax.axis_index("grp")
     stages = [1 << b for b in range(count.bit_length() - 2, -1, -1)]
     split = ff % (2 * LANES) == 0 and lax.axis_size("grp") == 2
-    split = split and count % (2 * PLANE) == 0 and PLANE * rows % LANES == 0
+    split = split and count >= 2 * NEAR * PLANE and PLANE * rows % LANES == 0
     half = ff // 2
 
     def cut_out(matrix, low, high, halved, start):
@@ -279,18 +285,21 @@
         (block,) = after([block], deps)
         return lax.all_to_all(block, "ep", split_axis=0, concat_axis=0, tiled=True)
 
-    def swapped(mine):
+    def swapped(mine, first):
         if not split:
             return None
         planes = [
             lax.dynamic_slice_in_dim(mine, ((me // PLANE) ^ k) * PLANE, PLANE, 0)
-            for k in range(1, count // PLANE)
+            for k in range(first, count // PLANE)
         ]
         return swap_grp(jnp.concatenate(planes, axis=0))
 
     def beside(bits, deps):
         (start,) = after([(1 - grp) * half], deps)
-        block = lax.dynamic_slice(learner_weights, (me ^ bits, 1, 0, start), (1, 2, rows, half))[0]
+        first, height = (1, rows) if bits < PLANE else (2, cut)
+        block = lax.dynamic_slice(
+            learner_weights, (me ^ bits, first, 0, start), (1, 3 - first, height, half)
+        )[0]
         return swap_ep(block, bits) if bits else block
 
     def arrays(*values):
@@ -333,12 +342,14 @@
     near = [beside(bits, []) for bits in range(PLANE)] if split else []
     up = bring(up_block, [gate, other] + near)
     gate_far = swap_grp(gate) if split else None
+    if split:
+        near += [beside(bits, [gate]) for bits in range(PLANE, NEAR * PLANE)]
     tokens, other = gather(tokens, stages[rest])
-    down_a = bring(down_a_block, [up, other] + arrays(gate_far))
-    up_far = swapped(up)
+    down_a = bring(down_a_block, [up, other] + arrays(gate_far) + near[PLANE:])
+    up_far = swapped(up, 1)
     tokens, other = gather(tokens, stages[rest + 1])
     down_b = bring(down_b_block, [down_a, other] + arrays(up_far))
-    down_a_far = swapped(down_a)
+    down_a_far = swapped(down_a, NEAR)
     other = swap_ep(tokens, stages[rest + 2])
 
     pieces, places = [], []
@@ -354,7 +365,7 @@
                 part = pl.ds((k - 1) * PLANE, PLANE)
                 places.append((len(pieces), part, matrix, k * PLANE, 1))
             pieces.append(far)
-    for bits, block in enumerate(near):
+    for bits, block in enumerate(near[:PLANE]):
         places.append((len(pieces), pl.ds(0, 1), 1, bits, 1))
         pieces.append(block)
     hidden = run_hidden(tokens, other, pieces, places, (2, count, rows, ff), experts)

time: 226 us -> 223 us (0.987)
  waiting for transfers between devices: 118 us -> 112 us
  starting transfers between devices: 44.4 us -> 48.1 us
    ppermute x3, waiting for transfers between devices: 6.25 us -> 0.01 us  [swap_grp(): return lax.ppermute(x, 'grp', [(0, 1), (1, 0)])]
    ppermute x15 -> x19, starting transfers between devices: 19.3 us -> 23.3 us  [swap_ep(): return lax.ppermute(x, 'ep', [(i, i ^ bits) for i in range(count)])]
    unnamed x46 -> x50, local copies, waits for them, and re-layouts: 2.96 us -> 0.1 us
    all_to_all x4, waiting for transfers between devices: 7.69 us -> 10.3 us  [bring(): return lax.all_to_all(block, 'ep', split_axis=0, concat_axis=0, tiled=True)]
    ppermute x15 -> x19, waiting for transfers between devices: 104 us -> 102 us  [swap_ep(): return lax.ppermute(x, 'ep', [(i, i ^ bits) for i in range(count)])]
  transfers between devices with their start and end apart: 22 -> 26, of which waited for: 10 -> 13; matrix products, arithmetic and copies ran while one was open for 15% -> 16% of each run, Pallas kernels for 6% -> 6%
where the time goes in v6:
time: 223 us; the launch traced here: 222 us
  waiting for transfers between devices  112 us (50%)
  starting transfers between devices  48.1 us (22%)
  Pallas kernels  22.8 us (10%)
  local copies, waits for them, and re-layouts  17 us (8%)
  matrix products  11.9 us (5%)
  other arithmetic  9.39 us (4%)
    ppermute x19, waiting for transfers between devices, swap_ep(): return lax.ppermute(x, 'ep', [(i, i ^ bits) for i in range(count)])  102 us
    ppermute x19, starting transfers between devices, swap_ep(): return lax.ppermute(x, 'ep', [(i, i ^ bits) for i in range(count)])  23.3 us
    all_to_all x4, starting transfers between devices, bring(): return lax.all_to_all(block, 'ep', split_axis=0, concat_axis=0, tiled=True)  20.1 us
    pallas_call x1, Pallas kernels, run_hidden(): pl.pallas_call(functools.partial(hidden_kernel, places, experts), grid_sp...  13.7 us
    squeeze x4, local copies, waits for them, and re-layouts, cut_out(): lax.dynamic_slice(learner_weights, (0, matrix, low, start), (experts, 1,...  11.6 us
    all_to_all x4, waiting for transfers between devices, bring(): return lax.all_to_all(block, 'ep', split_axis=0, concat_axis=0, tiled=True)  10.3 us
    pallas_call x1, Pallas kernels, run_down(): pl.pallas_call(functools.partial(down_kernel, cut, far is not None), grid...  9.1 us
    dot_general x1, matrix products, shards(): attn = jnp.dot(context, out_weight, preferred_element_type=jnp.float32)  5.09 us
  transfers between devices with their start and end apart: 26, of which 13 were waited for; matrix products, arithmetic and copies ran while one was open for 16% of the time, Pallas kernels for 6%

profile of v6, /device:TPU:0, one launch (start us, length us, event | category | flops | bytes accessed | tf_op | source)
XLA Modules:
  0.0 222.2 jit_solution(14665618657350557930)
XLA Ops:
  0.0 2.9 %dynamic-slice_bitcast_fusion.1 = bf16[16,128,384]{2,1,0:T(8,128)(2,1)} fusion(bf16[16,3,128,768]{3,2,1,0:T(8,128)(2,1)} %param.23, s32[]{:T(128)S(6)} %select_n.77), kind=kLoop, calls=%fused_computation.5 | loop fusion | bytes 3145732 | tf_op jit(solution)/shard_map/squeeze | solution.py:280
  2.9 7.5 %all-to-all-start = ((bf16[16,128,384]{2,1,0:T(8,128)(2,1)}), bf16[16,128,384]{2,1,0:T(8,128)(2,1)}, u32[]{:S(2)}, u32[]{:S(2)}) async-start(bf16[16,128,384]{2,1,0:T(8,128)(2,1)} %dynamic-slice_bitcast_fusion.1), calls=%async_computation | async-start | bytes 3145728 | tf_op jit(solution)/shard_map/all_to_all | solution.py:286
  10.6 0.3 fusion.11
  11.0 4.5 %fusion.24 = (f32[64,2,8]{2,1,0:T(2,128)S(1)}, f32[64,2,8,96]{3,2,1,0:T(8,128)}) fusion(bf16[64,2,96,128]{3,2,1,0:T(8,128)(2,1)} %param.15, bf16[64,16,128]{2,1,0:T(8,128)(2,1)S(1)} %copy-done.14, pred[64,96]{1,0:T(8,128)(4,1)S(1)} %iota_compare_fusion.1), kind=kOutput, calls=%fused_computation.81 | convolution fusion | flops 25459712 | bytes 3811328 | tf_op jit(solution)/shard_map/skgd,skld->skgl/dot_general | solution.py:22
  15.5 0.1 copy.33
  15.6 1.4 fusion.6
  17.7 2.1 fusion.1
  19.8 5.1 %multiply_reduce_fusion = (f32[64]{0:T(128)S(1)}, f32[64,2048]{1,0:T(8,128)S(1)}) fusion(bf16[2048,2048]{1,0:T(8,128)(2,1)} %param.19, bf16[8,8,16,128]{3,2,1,0:T(8,128)(2,1)S(1)} %bitcast.108, bf16[64,2048]{1,0:T(8,128)(2,1)S(1)} %copy-done.13), kind=kOutput, calls=%fused_computation.28 | convolution fusion | flops 537395136 | bytes 9437440 | tf_op jit(solution)/shard_map/dot_general | solution.py:319
  25.0 0.1 multiply_convert_fusion
  25.2 2.8 %collective-permute-start = (bf16[64,2176]{1,0:T(8,128)(2,1)S(1)}, bf16[64,2176]{1,0:T(8,128)(2,1)S(1)}, u32[]{:S(2)}, u32[]{:S(2)}) collective-permute-start(bf16[64,2176]{1,0:T(8,128)(2,1)S(1)} %concatenate.23), channel_id=1, source_target_pairs={{0,8},{1,9},{2,10},{3,11},{4,12},{5,13},{6,14},{7,15},{8,0},{9,1},... | collective-permute-start | bytes 835592 | tf_op jit(solution)/shard_map/ppermute | solution.py:52
  28.0 2.0 dynamic-slice_bitcast_fusion.3
  30.0 0.9 collective-permute-start.7
  31.0 0.6 collective-permute-start.6
  31.5 0.3 collective-permute-start.5
  31.9 2.1 slice_bitcast_fusion
  34.0 3.0 %dynamic-slice_bitcast_fusion.2 = bf16[16,96,384]{2,1,0:T(8,128)(2,1)} fusion(bf16[16,3,128,768]{3,2,1,0:T(8,128)(2,1)} %param.23, s32[]{:T(128)S(6)} %select_n.78), kind=kLoop, calls=%fused_computation.11 | loop fusion | bytes 2359300 | tf_op jit(solution)/shard_map/squeeze | solution.py:280
  37.0 3.5 %dynamic-slice_bitcast_fusion = bf16[16,128,384]{2,1,0:T(8,128)(2,1)} fusion(bf16[16,3,128,768]{3,2,1,0:T(8,128)(2,1)} %param.23, s32[]{:T(128)S(6)} %select_n.78), kind=kLoop, calls=%fused_computation.4 | loop fusion | bytes 3145732 | tf_op jit(solution)/shard_map/squeeze | solution.py:280
  40.5 8.0 %all-to-all-done.refs_0_ = bf16[16,128,384]{2,1,0:T(8,128)(2,1)} async-done(((bf16[16,128,384]{2,1,0:T(8,128)(2,1)}), bf16[16,128,384]{2,1,0:T(8,128)(2,1)}, u32[]{:S(2)}, u32[]{:S(2)}) %all-to-all-start) | async-done | bytes 1572896 | tf_op jit(solution)/shard_map/all_to_all | solution.py:286
  48.5 11.7 %collective-permute-done = bf16[64,2176]{1,0:T(8,128)(2,1)S(1)} collective-permute-done((bf16[64,2176]{1,0:T(8,128)(2,1)S(1)}, bf16[64,2176]{1,0:T(8,128)(2,1)S(1)}, u32[]{:S(2)}, u32[]{:S(2)}) %collective-permute-start) | collective-permute-done | bytes 278560 | tf_op jit(solution)/shard_map/ppermute | solution.py:52
  60.2 3.7 %all-to-all-start.1 = ((bf16[16,128,384]{2,1,0:T(8,128)(2,1)}), bf16[16,128,384]{2,1,0:T(8,128)(2,1)S(1)}, u32[]{:S(2)}, u32[]{:S(2)}) async-start(bf16[16,128,384]{2,1,0:T(8,128)(2,1)} %dynamic-slice_bitcast_fusion), calls=%async_computation.1 | async-start | bytes 3145728 | tf_op jit(solution)/shard_map/all_to_all | solution.py:286
  63.9 1.6 collective-permute-start.4
  65.5 0.8 pad_maximum_fusion.4
  66.3 1.8 collective-permute-start.1
  68.2 1.1 dynamic-slice_bitcast_fusion.7
  69.4 0.7 collective-permute-start.12
  70.1 2.0 collective-permute-start.10
  72.1 0.6 collective-permute-start.9
  72.7 32.1 %collective-permute-done.1 = bf16[128,2176]{1,0:T(8,128)(2,1)S(1)} collective-permute-done((bf16[128,2176]{1,0:T(8,128)(2,1)}, bf16[128,2176]{1,0:T(8,128)(2,1)S(1)}, u32[]{:S(2)}, u32[]{:S(2)}) %collective-permute-start.1) | collective-permute-done | bytes 557088 | tf_op jit(solution)/shard_map/ppermute | solution.py:52
  104.7 1.7 collective-permute-start.11
  106.4 1.1 pad_maximum_fusion.2
  107.6 1.9 collective-permute-done.9.refs_7_
  109.5 2.2 collective-permute-done.11.refs_9_
  111.7 4.4 %all-to-all-start.2 = ((bf16[16,96,384]{2,1,0:T(8,128)(2,1)}), bf16[16,96,384]{2,1,0:T(8,128)(2,1)}, u32[]{:S(2)}, u32[]{:S(2)}) async-start(bf16[16,96,384]{2,1,0:T(8,128)(2,1)} %dynamic-slice_bitcast_fusion.2), calls=%async_computation.2 | async-start | bytes 2359296 | tf_op jit(solution)/shard_map/all_to_all | solution.py:286
  116.1 0.1 constant_dynamic-slice_fusion.4
  116.3 0.2 pad_maximum_fusion.1
  116.5 1.6 collective-permute-start.8
  118.0 27.1 %collective-permute-done.2 = bf16[256,2176]{1,0:T(8,128)(2,1)} collective-permute-done((bf16[256,2176]{1,0:T(8,128)(2,1)}, bf16[256,2176]{1,0:T(8,128)(2,1)}, u32[]{:S(2)}, u32[]{:S(2)}) %collective-permute-start.2) | collective-permute-done | bytes 1114144 | tf_op jit(solution)/shard_map/ppermute | solution.py:52
  145.1 1.4 pad_maximum_fusion.first_ref
  146.6 0.8 all-to-all-done.2.refs_0_
  147.5 4.5 %all-to-all-start.3 = ((bf16[16,32,768]{2,1,0:T(8,128)(2,1)}), bf16[16,32,768]{2,1,0:T(8,128)(2,1)}, u32[]{:S(2)}, u32[]{:S(2)}) async-start(bf16[16,32,768]{2,1,0:T(8,128)(2,1)} %slice_bitcast_fusion), calls=%async_computation.3 | async-start | bytes 1572864 | tf_op jit(solution)/shard_map/all_to_all | solution.py:286
  151.9 1.1 constant_dynamic-slice_fusion.1
  153.1 1.6 collective-permute-start.13
  154.7 0.6 pad_add_fusion.where_ref
  155.4 13.7 %shard_map.118.hidden_ref = bf16[1024,768]{1,0:T(8,128)(2,1)} custom-call(s32[2]{0:T(128)} %pad_add_fusion.where_ref, bf16[512,2176]{1,0:T(8,128)(2,1)} %copy-done.3, bf16[512,2176]{1,0:T(8,128)(2,1)} %collective-permute-done.3.second_ref, bf16[16,128,384]{2,1,0:T(8,128)(2,1)} %all-to-all-done.refs_0_, bf16[16,128,384]{2,1,0:T(8,128)(2,1)} %collective-permute-done.4.refs_1_, ...), custom_call_target="tpu_custom_call" | custom-call | tf_op jit(solution)/shard_map/pallas_call | solution.py:185
  169.1 1.5 all-to-all-done.3.refs_1_
  170.5 9.1 %shard_map.119 = (bf16[512,1024]{1,0:T(8,128)(2,1)}, bf16[512,1024]{1,0:T(8,128)(2,1)}, bf16[512,1024]{1,0:T(8,128)(2,1)}, bf16[512,1024]{1,0:T(8,128)(2,1)}) custom-call(s32[2]{0:T(128)} %pad_add_fusion.where_ref, bf16[1024,768]{1,0:T(8,128)(2,1)} %shard_map.118.hidden_ref, bf16[16,96,384]{2,1,0:T(8,128)(2,1)} %all-to-all-done.2.refs_0_, ...), custom_call_target="tpu_custom_call" | custom-call | tf_op jit(solution)/shard_map/pallas_call | solution.py:225
  179.6 0.3 collective-permute-start.14
  179.9 0.3 collective-permute-start.18
  180.2 2.4 %collective-permute-done.14 = bf16[512,1024]{1,0:T(8,128)(2,1)S(1)} collective-permute-done((bf16[512,1024]{1,0:T(8,128)(2,1)}, bf16[512,1024]{1,0:T(8,128)(2,1)S(1)}, u32[]{:S(2)}, u32[]{:S(2)}) %collective-permute-start.14) | collective-permute-done | bytes 1048608 | tf_op jit(solution)/shard_map/ppermute | solution.py:52
  182.5 1.7 add_convert_fusion.1
  184.3 1.6 collective-permute-start.15
  185.9 0.4 add_convert_fusion
  186.4 2.4 %collective-permute-start.19 = (bf16[2,2,64,1024]{3,2,1,0:T(8,128)(2,1)S(1)}, bf16[2,2,64,1024]{3,2,1,0:T(8,128)(2,1)S(1)}, u32[]{:S(2)}, u32[]{:S(2)}) collective-permute-start(bf16[2,2,64,1024]{3,2,1,0:T(8,128)(2,1)S(1)} %slice_bitcast_fusion.1), channel_id=1, source_target_pairs={{0,4},{1,5},{2,6},{3,7},{4,0},{5,1},{6,2},{7,3},{8,12},{9,13},{10,... | collective-permute-start | bytes 1572872 | tf_op jit(solution)/shard_map/ppermute | solution.py:52
  188.8 9.7 %collective-permute-done.15 = bf16[2,2,64,1024]{3,2,1,0:T(8,128)(2,1)S(1)} collective-permute-done((bf16[2,2,64,1024]{3,2,1,0:T(8,128)(2,1)S(1)}, bf16[2,2,64,1024]{3,2,1,0:T(8,128)(2,1)S(1)}, u32[]{:S(2)}, u32[]{:S(2)}) %collective-permute-start.15) | collective-permute-done | bytes 524320 | tf_op jit(solution)/shard_map/ppermute | solution.py:52
  198.5 0.2 fusion.3
  198.7 2.8 %collective-permute-start.16 = (bf16[2,64,1024]{2,1,0:T(8,128)(2,1)S(1)}, bf16[2,64,1024]{2,1,0:T(8,128)(2,1)S(1)}, u32[]{:S(2)}, u32[]{:S(2)}) collective-permute-start(bf16[2,64,1024]{2,1,0:T(8,128)(2,1)S(1)} %slice_bitcast_fusion.5), channel_id=1, source_target_pairs={{0,4},{1,5},{2,6},{3,7},{4,0},{5,1},{6,2},{7,3},{8,12},{9,13},{10,... | collective-permute-start | bytes 786440 | tf_op jit(solution)/shard_map/ppermute | solution.py:52
  201.5 0.2 fusion.2
  201.8 1.2 collective-permute-start.20
  203.0 4.6 %collective-permute-done.16 = bf16[2,64,1024]{2,1,0:T(8,128)(2,1)S(1)} collective-permute-done((bf16[2,64,1024]{2,1,0:T(8,128)(2,1)S(1)}, bf16[2,64,1024]{2,1,0:T(8,128)(2,1)S(1)}, u32[]{:S(2)}, u32[]{:S(2)}) %collective-permute-start.16) | collective-permute-done | bytes 262176 | tf_op jit(solution)/shard_map/ppermute | solution.py:52
  207.7 2.5 %collective-permute-start.17 = (bf16[64,1024]{1,0:T(8,128)(2,1)S(1)}, bf16[64,1024]{1,0:T(8,128)(2,1)S(1)}, u32[]{:S(2)}, u32[]{:S(2)}) collective-permute-start(bf16[64,1024]{1,0:T(8,128)(2,1)S(1)} %slice_bitcast_fusion.9), channel_id=1, source_target_pairs={{0,8},{1,9},{2,10},{3,11},{4,12},{5,13},{6,14},{7,15},{8,0},{9,1},... | collective-permute-start | bytes 393224 | tf_op jit(solution)/shard_map/ppermute | solution.py:52
  210.2 0.6 collective-permute-start.21
  210.8 8.8 %collective-permute-done.17 = bf16[64,1024]{1,0:T(8,128)(2,1)S(1)} collective-permute-done((bf16[64,1024]{1,0:T(8,128)(2,1)S(1)}, bf16[64,1024]{1,0:T(8,128)(2,1)S(1)}, u32[]{:S(2)}, u32[]{:S(2)}) %collective-permute-start.17) | collective-permute-done | bytes 131104 | tf_op jit(solution)/shard_map/ppermute | solution.py:52
  219.7 1.7 collective-permute-done.21
  221.5 0.8 add_convert_fusion.2
  (93 shorter events, 1.6 us)
Async XLA Ops:
  0.0 17.7 %copy-start = (bf16[64,2,96,128]{3,2,1,0:T(8,128)(2,1)S(1)}, bf16[64,2,96,128]{3,2,1,0:T(8,128)(2,1)}, u32[]{:S(2)}) copy-start(bf16[64,2,96,128]{3,2,1,0:T(8,128)(2,1)} %param.16) | copy-start | bytes 9437188
  2.9 7.5 %copy-start.23 = (s32[64]{0:T(128)S(1)}, s32[64]{0:T(128)}, u32[]{:S(2)}) copy-start(s32[64]{0:T(128)} %param.17) | copy-start | bytes 772
  2.9 7.6 %copy-start.14 = (bf16[64,16,128]{2,1,0:T(8,128)(2,1)S(1)}, bf16[64,16,128]{2,1,0:T(8,128)(2,1)}, u32[]{:S(2)}) copy-start(bf16[64,16,128]{2,1,0:T(8,128)(2,1)} %param.12) | copy-start | bytes 786436
  2.9 7.6 %copy-start.24 = (bf16[64,2,128]{2,1,0:T(2,128)(2,1)S(1)}, bf16[64,2,128]{2,1,0:T(2,128)(2,1)}, u32[]{:S(2)}) copy-start(bf16[64,2,128]{2,1,0:T(2,128)(2,1)} %param.13) | copy-start | bytes 98308
  2.9 45.5 %all-to-all-start = ((bf16[16,128,384]{2,1,0:T(8,128)(2,1)}), bf16[16,128,384]{2,1,0:T(8,128)(2,1)}, u32[]{:S(2)}, u32[]{:S(2)}) async-start(bf16[16,128,384]{2,1,0:T(8,128)(2,1)} %dynamic-slice_bitcast_fusion.1), calls=%async_computation | async-start | bytes 3145728 | tf_op jit(solution)/shard_map/all_to_all | solution.py:286
  10.9 6.2 %copy-start.21 = (f32[64,8]{0,1:T(8,128)S(1)}, f32[64,8]{0,1:T(8,128)}, u32[]{:S(2)}) copy-start(f32[64,8]{0,1:T(8,128)} %param.22) | copy-start | bytes 6148
  10.9 6.2 %copy-start.22 = (s32[64,8]{0,1:T(8,128)S(1)}, s32[64,8]{0,1:T(8,128)}, u32[]{:S(2)}) copy-start(s32[64,8]{0,1:T(8,128)} %param.21) | copy-start | bytes 6148
  10.9 6.4 %copy-start.19 = (bf16[64,2,128]{2,1,0:T(2,128)(2,1)S(1)}, bf16[64,2,128]{2,1,0:T(2,128)(2,1)}, u32[]{:S(2)}) copy-start(bf16[64,2,128]{2,1,0:T(2,128)(2,1)} %param.14) | copy-start | bytes 98308
  17.7 2.1 copy-start.13
  19.8 5.1 %copy-start.20 = (f32[2048]{0:T(1024)S(1)}, f32[2048]{0:T(1024)}, u32[]{:S(2)}) copy-start(f32[2048]{0:T(1024)} %param.20) | copy-start | bytes 24580
  24.9 9.0 %copy-start.4 = (f32[64,2048]{1,0:T(8,128)}, f32[64,2048]{1,0:T(8,128)S(1)}, u32[]{:S(2)}) copy-start(f32[64,2048]{1,0:T(8,128)S(1)} %get-tuple-element.45) | copy-start | bytes 1572868
  25.2 35.0 %collective-permute-start = (bf16[64,2176]{1,0:T(8,128)(2,1)S(1)}, bf16[64,2176]{1,0:T(8,128)(2,1)S(1)}, u32[]{:S(2)}, u32[]{:S(2)}) collective-permute-start(bf16[64,2176]{1,0:T(8,128)(2,1)S(1)} %concatenate.23), channel_id=1, source_target_pairs={{0,8},{1,9},{2,10},{3,11},{4,12},{5,13},{6,14},{7,15},{8,0},{9,1},... | collective-permute-start | bytes 835592 | tf_op jit(solution)/shard_map/ppermute | solution.py:52
  30.0 18.5 %collective-permute-start.7 = (bf16[2,128,384]{2,1,0:T(8,128)(2,1)S(1)}, bf16[2,128,384]{2,1,0:T(8,128)(2,1)S(1)}, u32[]{:S(2)}, u32[]{:S(2)}) collective-permute-start(bf16[2,128,384]{2,1,0:T(8,128)(2,1)S(1)} %get-tuple-element.29), channel_id=1, source_target_pairs={{0,3},{1,2},{2,1},{3,0},{4,7},{5,6},{6,5},{7,4},{8,11},{9,10},{10,... | collective-permute-start | bytes 589832 | tf_op jit(solution)/shard_map/ppermute | solution.py:52
  31.0 17.5 %collective-permute-start.6 = (bf16[2,128,384]{2,1,0:T(8,128)(2,1)S(1)}, bf16[2,128,384]{2,1,0:T(8,128)(2,1)S(1)}, u32[]{:S(2)}, u32[]{:S(2)}) collective-permute-start(bf16[2,128,384]{2,1,0:T(8,128)(2,1)S(1)} %get-tuple-element.30), channel_id=1, source_target_pairs={{0,2},{1,3},{2,0},{3,1},{4,6},{5,7},{6,4},{7,5},{8,10},{9,11},{10,... | collective-permute-start | bytes 589832 | tf_op jit(solution)/shard_map/ppermute | solution.py:52
  31.5 17.0 %collective-permute-start.5 = (bf16[2,128,384]{2,1,0:T(8,128)(2,1)S(1)}, bf16[2,128,384]{2,1,0:T(8,128)(2,1)S(1)}, u32[]{:S(2)}, u32[]{:S(2)}) collective-permute-start(bf16[2,128,384]{2,1,0:T(8,128)(2,1)S(1)} %get-tuple-element.31), channel_id=1, source_target_pairs={{0,1},{1,0},{2,3},{3,2},{4,5},{5,4},{6,7},{7,6},{8,9},{9,8},{10,11... | collective-permute-start | bytes 589832 | tf_op jit(solution)/shard_map/ppermute | solution.py:52
  48.5 20.9 %copy-start.9 = (bf16[2,128,384]{2,1,0:T(8,128)(2,1)}, bf16[2,128,384]{2,1,0:T(8,128)(2,1)S(1)}, u32[]{:S(2)}) copy-start(bf16[2,128,384]{2,1,0:T(8,128)(2,1)S(1)} %collective-permute-done.7.refs_7_.refs_6_) | copy-start | bytes 589828
  48.5 20.9 %copy-start.10 = (bf16[2,128,384]{2,1,0:T(8,128)(2,1)}, bf16[2,128,384]{2,1,0:T(8,128)(2,1)S(1)}, u32[]{:S(2)}) copy-start(bf16[2,128,384]{2,1,0:T(8,128)(2,1)S(1)} %collective-permute-done.6.refs_6_.refs_5_) | copy-start | bytes 589828
  48.5 20.8 %copy-start.11 = (bf16[2,128,384]{2,1,0:T(8,128)(2,1)}, bf16[2,128,384]{2,1,0:T(8,128)(2,1)S(1)}, u32[]{:S(2)}) copy-start(bf16[2,128,384]{2,1,0:T(8,128)(2,1)S(1)} %collective-permute-done.5.refs_5_.refs_4_) | copy-start | bytes 589828
  60.2 51.4 %all-to-all-start.1 = ((bf16[16,128,384]{2,1,0:T(8,128)(2,1)}), bf16[16,128,384]{2,1,0:T(8,128)(2,1)S(1)}, u32[]{:S(2)}, u32[]{:S(2)}) async-start(bf16[16,128,384]{2,1,0:T(8,128)(2,1)} %dynamic-slice_bitcast_fusion), calls=%async_computation.1 | async-start | bytes 3145728 | tf_op jit(solution)/shard_map/all_to_all | solution.py:286
  63.9 47.7 %collective-permute-start.4 = (bf16[16,128,384]{2,1,0:T(8,128)(2,1)}, bf16[16,128,384]{2,1,0:T(8,128)(2,1)}, u32[]{:S(2)}, u32[]{:S(2)}) collective-permute-start(bf16[16,128,384]{2,1,0:T(8,128)(2,1)} %all-to-all-done.refs_0_), channel_id=1, source_target_pairs={{0,16},{16,0},{1,17},{17,1},{2,18},{18,2},{3,19},{19,3},{4,20},{20... | collective-permute-start | bytes 4718600 | tf_op jit(solution)/shard_map/ppermute | solution.py:56
  66.3 38.4 %collective-permute-start.1 = (bf16[128,2176]{1,0:T(8,128)(2,1)}, bf16[128,2176]{1,0:T(8,128)(2,1)S(1)}, u32[]{:S(2)}, u32[]{:S(2)}) collective-permute-start(bf16[128,2176]{1,0:T(8,128)(2,1)} %pad_maximum_fusion.4), channel_id=1, source_target_pairs={{0,4},{1,5},{2,6},{3,7},{4,0},{5,1},{6,2},{7,3},{8,12},{9,13},{10,... | collective-permute-start | bytes 1671176 | tf_op jit(solution)/shard_map/ppermute | solution.py:52
  69.4 38.1 %collective-permute-start.12 = (bf16[1,96,384]{2,1,0:T(8,128)(2,1)S(1)}, bf16[1,96,384]{2,1,0:T(8,128)(2,1)S(1)}, u32[]{:S(2)}, u32[]{:S(2)}) collective-permute-start(bf16[1,96,384]{2,1,0:T(8,128)(2,1)S(1)} %get-tuple-element.25), channel_id=1, source_target_pairs={{0,7},{1,6},{2,5},{3,4},{4,3},{5,2},{6,1},{7,0},{8,15},{9,14},{10,... | collective-permute-start | bytes 221192 | tf_op jit(solution)/shard_map/ppermute | solution.py:52
  70.1 37.5 %collective-permute-start.10 = (bf16[1,96,384]{2,1,0:T(8,128)(2,1)S(1)}, bf16[1,96,384]{2,1,0:T(8,128)(2,1)S(1)}, u32[]{:S(2)}, u32[]{:S(2)}) collective-permute-start(bf16[1,96,384]{2,1,0:T(8,128)(2,1)S(1)} %get-tuple-element.26), channel_id=1, source_target_pairs={{0,5},{1,4},{2,7},{3,6},{4,1},{5,0},{6,3},{7,2},{8,13},{9,12},{10,... | collective-permute-start | bytes 221192 | tf_op jit(solution)/shard_map/ppermute | solution.py:52
  72.1 37.4 %collective-permute-start.9 = (bf16[1,96,384]{2,1,0:T(8,128)(2,1)S(1)}, bf16[1,96,384]{2,1,0:T(8,128)(2,1)S(1)}, u32[]{:S(2)}, u32[]{:S(2)}) collective-permute-start(bf16[1,96,384]{2,1,0:T(8,128)(2,1)S(1)} %get-tuple-element.27), channel_id=1, source_target_pairs={{0,4},{1,5},{2,6},{3,7},{4,0},{5,1},{6,2},{7,3},{8,12},{9,13},{10,... | collective-permute-start | bytes 221192 | tf_op jit(solution)/shard_map/ppermute | solution.py:52
  104.7 6.9 %copy-start.6 = (bf16[128,2176]{1,0:T(8,128)(2,1)}, bf16[128,2176]{1,0:T(8,128)(2,1)S(1)}, u32[]{:S(2)}) copy-start(bf16[128,2176]{1,0:T(8,128)(2,1)S(1)} %collective-permute-done.1) | copy-start | bytes 1671172
  104.7 6.9 %collective-permute-start.11 = (bf16[1,96,384]{2,1,0:T(8,128)(2,1)S(1)}, bf16[1,96,384]{2,1,0:T(8,128)(2,1)S(1)}, u32[]{:S(2)}, u32[]{:S(2)}) collective-permute-start(bf16[1,96,384]{2,1,0:T(8,128)(2,1)S(1)} %get-tuple-element.28), channel_id=1, source_target_pairs={{0,6},{1,7},{2,4},{3,5},{4,2},{5,3},{6,0},{7,1},{8,14},{9,15},{10,... | collective-permute-start | bytes 221192 | tf_op jit(solution)/shard_map/ppermute | solution.py:52
  107.5 8.7 %copy-start.15 = (bf16[1,96,384]{2,1,0:T(8,128)(2,1)}, bf16[1,96,384]{2,1,0:T(8,128)(2,1)S(1)}, u32[]{:S(2)}) copy-start(bf16[1,96,384]{2,1,0:T(8,128)(2,1)S(1)} %collective-permute-done.12.refs_10_) | copy-start | bytes 221188
  107.5 37.6 %collective-permute-start.2 = (bf16[256,2176]{1,0:T(8,128)(2,1)}, bf16[256,2176]{1,0:T(8,128)(2,1)}, u32[]{:S(2)}, u32[]{:S(2)}) collective-permute-start(bf16[256,2176]{1,0:T(8,128)(2,1)} %pad_maximum_fusion.2), channel_id=1, source_target_pairs={{0,2},{1,3},{2,0},{3,1},{4,6},{5,7},{6,4},{7,5},{8,10},{9,11},{10,... | collective-permute-start | bytes 3342344 | tf_op jit(solution)/shard_map/ppermute | solution.py:52
  107.6 8.7 %copy-start.16 = (bf16[1,96,384]{2,1,0:T(8,128)(2,1)}, bf16[1,96,384]{2,1,0:T(8,128)(2,1)S(1)}, u32[]{:S(2)}) copy-start(bf16[1,96,384]{2,1,0:T(8,128)(2,1)S(1)} %collective-permute-done.10.refs_8_) | copy-start | bytes 221188
  109.5 6.8 %copy-start.17 = (bf16[1,96,384]{2,1,0:T(8,128)(2,1)}, bf16[1,96,384]{2,1,0:T(8,128)(2,1)S(1)}, u32[]{:S(2)}) copy-start(bf16[1,96,384]{2,1,0:T(8,128)(2,1)S(1)} %collective-permute-done.9.refs_7_) | copy-start | bytes 221188
  111.6 4.6 %copy-start.18 = (bf16[1,96,384]{2,1,0:T(8,128)(2,1)}, bf16[1,96,384]{2,1,0:T(8,128)(2,1)S(1)}, u32[]{:S(2)}) copy-start(bf16[1,96,384]{2,1,0:T(8,128)(2,1)S(1)} %collective-permute-done.11.refs_9_) | copy-start | bytes 221188
  111.6 4.6 %copy-start.2 = (bf16[16,128,384]{2,1,0:T(8,128)(2,1)}, bf16[16,128,384]{2,1,0:T(8,128)(2,1)S(1)}, u32[]{:S(2)}) copy-start(bf16[16,128,384]{2,1,0:T(8,128)(2,1)S(1)} %all-to-all-done.1.refs_2_) | copy-start | bytes 4718596
  111.7 35.8 %all-to-all-start.2 = ((bf16[16,96,384]{2,1,0:T(8,128)(2,1)}), bf16[16,96,384]{2,1,0:T(8,128)(2,1)}, u32[]{:S(2)}, u32[]{:S(2)}) async-start(bf16[16,96,384]{2,1,0:T(8,128)(2,1)} %dynamic-slice_bitcast_fusion.2), calls=%async_computation.2 | async-start | bytes 2359296 | tf_op jit(solution)/shard_map/all_to_all | solution.py:286
  116.1 29.0 %copy-start.7 = (bf16[128,2176]{1,0:T(8,128)(2,1)S(1)}, bf16[128,2176]{1,0:T(8,128)(2,1)}, u32[]{:S(2)}) copy-start(bf16[128,2176]{1,0:T(8,128)(2,1)} %copy-done.6) | copy-start | bytes 1671172
  116.5 30.2 %collective-permute-start.8 = (bf16[12,128,384]{2,1,0:T(8,128)(2,1)S(1)}, bf16[12,128,384]{2,1,0:T(8,128)(2,1)}, u32[]{:S(2)}, u32[]{:S(2)}) collective-permute-start(bf16[12,128,384]{2,1,0:T(8,128)(2,1)S(1)} %pad_maximum_fusion.1), channel_id=1, source_target_pairs={{0,16},{16,0},{1,17},{17,1},{2,18},{18,2},{3,19},{19,3},{4,20},{20... | collective-permute-start | bytes 3538952 | tf_op jit(solution)/shard_map/ppermute | solution.py:56
  146.5 8.8 %copy-start.3 = (bf16[512,2176]{1,0:T(8,128)(2,1)}, bf16[512,2176]{1,0:T(8,128)(2,1)S(1)}, u32[]{:S(2)}) copy-start(bf16[512,2176]{1,0:T(8,128)(2,1)S(1)} %pad_maximum_fusion.first_ref) | copy-start | bytes 6684676
  146.6 8.8 %collective-permute-start.3 = (bf16[512,2176]{1,0:T(8,128)(2,1)S(1)}, bf16[512,2176]{1,0:T(8,128)(2,1)}, u32[]{:S(2)}, u32[]{:S(2)}) collective-permute-start(bf16[512,2176]{1,0:T(8,128)(2,1)S(1)} %pad_maximum_fusion.first_ref), channel_id=1, source_target_pairs={{0,1},{1,0},{2,3},{3,2},{4,5},{5,4},{6,7},{7,6},{8,9},{9,8},{10,11... | collective-permute-start | bytes 6684680 | tf_op jit(solution)/shard_map/ppermute | solution.py:52
  147.5 23.1 %all-to-all-start.3 = ((bf16[16,32,768]{2,1,0:T(8,128)(2,1)}), bf16[16,32,768]{2,1,0:T(8,128)(2,1)}, u32[]{:S(2)}, u32[]{:S(2)}) async-start(bf16[16,32,768]{2,1,0:T(8,128)(2,1)} %slice_bitcast_fusion), calls=%async_computation.3 | async-start | bytes 1572864 | tf_op jit(solution)/shard_map/all_to_all | solution.py:286
  153.1 15.9 %collective-permute-start.13 = (bf16[8,96,384]{2,1,0:T(8,128)(2,1)S(1)}, bf16[8,96,384]{2,1,0:T(8,128)(2,1)S(1)}, u32[]{:S(2)}, u32[]{:S(2)}) collective-permute-start(bf16[8,96,384]{2,1,0:T(8,128)(2,1)S(1)} %pad_maximum_fusion.3), channel_id=1, source_target_pairs={{0,16},{16,0},{1,17},{17,1},{2,18},{18,2},{3,19},{19,3},{4,20},{20... | collective-permute-start | bytes 1769480 | tf_op jit(solution)/shard_map/ppermute | solution.py:56
  169.0 1.5 copy-start.12
  179.6 2.9 %collective-permute-start.14 = (bf16[512,1024]{1,0:T(8,128)(2,1)}, bf16[512,1024]{1,0:T(8,128)(2,1)S(1)}, u32[]{:S(2)}, u32[]{:S(2)}) collective-permute-start(bf16[512,1024]{1,0:T(8,128)(2,1)} %get-tuple-element.22), channel_id=1, source_target_pairs={{0,1},{1,0},{2,3},{3,2},{4,5},{5,4},{6,7},{7,6},{8,9},{9,8},{10,11... | collective-permute-start | bytes 3145736 | tf_op jit(solution)/shard_map/ppermute | solution.py:52
  179.9 6.0 %collective-permute-start.18 = (bf16[512,1024]{1,0:T(8,128)(2,1)}, bf16[512,1024]{1,0:T(8,128)(2,1)S(1)}, u32[]{:S(2)}, u32[]{:S(2)}) collective-permute-start(bf16[512,1024]{1,0:T(8,128)(2,1)} %get-tuple-element.24), channel_id=1, source_target_pairs={{0,1},{1,0},{2,3},{3,2},{4,5},{5,4},{6,7},{7,6},{8,9},{9,8},{10,11... | collective-permute-start | bytes 3145736 | tf_op jit(solution)/shard_map/ppermute | solution.py:52
  182.5 3.4 %copy-start.8 = (bf16[512,1024]{1,0:T(8,128)(2,1)S(1)}, bf16[512,1024]{1,0:T(8,128)(2,1)}, u32[]{:S(2)}) copy-start(bf16[512,1024]{1,0:T(8,128)(2,1)} %get-tuple-element.23) | copy-start | bytes 3145732
  184.3 14.2 %collective-permute-start.15 = (bf16[2,2,64,1024]{3,2,1,0:T(8,128)(2,1)S(1)}, bf16[2,2,64,1024]{3,2,1,0:T(8,128)(2,1)S(1)}, u32[]{:S(2)}, u32[]{:S(2)}) collective-permute-start(bf16[2,2,64,1024]{3,2,1,0:T(8,128)(2,1)S(1)} %bitcast.109), channel_id=1, source_target_pairs={{0,2},{1,3},{2,0},{3,1},{4,6},{5,7},{6,4},{7,5},{8,10},{9,11},{10,... | collective-permute-start | bytes 1572872 | tf_op jit(solution)/shard_map/ppermute | solution.py:52
  186.4 15.2 %collective-permute-start.19 = (bf16[2,2,64,1024]{3,2,1,0:T(8,128)(2,1)S(1)}, bf16[2,2,64,1024]{3,2,1,0:T(8,128)(2,1)S(1)}, u32[]{:S(2)}, u32[]{:S(2)}) collective-permute-start(bf16[2,2,64,1024]{3,2,1,0:T(8,128)(2,1)S(1)} %slice_bitcast_fusion.1), channel_id=1, source_target_pairs={{0,4},{1,5},{2,6},{3,7},{4,0},{5,1},{6,2},{7,3},{8,12},{9,13},{10,... | collective-permute-start | bytes 1572872 | tf_op jit(solution)/shard_map/ppermute | solution.py:52
  198.7 22.8 %copy-start.5 = (f32[64,2048]{1,0:T(8,128)S(1)}, f32[64,2048]{1,0:T(8,128)}, u32[]{:S(2)}) copy-start(f32[64,2048]{1,0:T(8,128)} %copy-done.4) | copy-start | bytes 1572868
  198.7 8.8 %collective-permute-start.16 = (bf16[2,64,1024]{2,1,0:T(8,128)(2,1)S(1)}, bf16[2,64,1024]{2,1,0:T(8,128)(2,1)S(1)}, u32[]{:S(2)}, u32[]{:S(2)}) collective-permute-start(bf16[2,64,1024]{2,1,0:T(8,128)(2,1)S(1)} %slice_bitcast_fusion.5), channel_id=1, source_target_pairs={{0,4},{1,5},{2,6},{3,7},{4,0},{5,1},{6,2},{7,3},{8,12},{9,13},{10,... | collective-permute-start | bytes 786440 | tf_op jit(solution)/shard_map/ppermute | solution.py:52
  201.5 20.7 %copy-start.1 = (bf16[64,2,96,128]{3,2,1,0:T(8,128)(2,1)S(1)}, bf16[64,2,96,128]{3,2,1,0:T(8,128)(2,1)}, u32[]{:S(2)}) copy-start(bf16[64,2,96,128]{3,2,1,0:T(8,128)(2,1)} %param.16) | copy-start | bytes 9437188
  201.8 8.3 %collective-permute-start.20 = (bf16[2,64,1024]{2,1,0:T(8,128)(2,1)S(1)}, bf16[2,64,1024]{2,1,0:T(8,128)(2,1)S(1)}, u32[]{:S(2)}, u32[]{:S(2)}) collective-permute-start(bf16[2,64,1024]{2,1,0:T(8,128)(2,1)S(1)} %slice_bitcast_fusion.3), channel_id=1, source_target_pairs={{0,2},{1,3},{2,0},{3,1},{4,6},{5,7},{6,4},{7,5},{8,10},{9,11},{10,... | collective-permute-start | bytes 786440 | tf_op jit(solution)/shard_map/ppermute | solution.py:52
  207.7 12.0 %collective-permute-start.17 = (bf16[64,1024]{1,0:T(8,128)(2,1)S(1)}, bf16[64,1024]{1,0:T(8,128)(2,1)S(1)}, u32[]{:S(2)}, u32[]{:S(2)}) collective-permute-start(bf16[64,1024]{1,0:T(8,128)(2,1)S(1)} %slice_bitcast_fusion.9), channel_id=1, source_target_pairs={{0,8},{1,9},{2,10},{3,11},{4,12},{5,13},{6,14},{7,15},{8,0},{9,1},... | collective-permute-start | bytes 393224 | tf_op jit(solution)/shard_map/ppermute | solution.py:52
  210.2 11.2 %collective-permute-start.21 = (bf16[64,1024]{1,0:T(8,128)(2,1)S(1)}, bf16[64,1024]{1,0:T(8,128)(2,1)S(1)}, u32[]{:S(2)}, u32[]{:S(2)}) collective-permute-start(bf16[64,1024]{1,0:T(8,128)(2,1)S(1)} %slice_bitcast_fusion.7), channel_id=1, source_target_pairs={{0,8},{1,9},{2,10},{3,11},{4,12},{5,13},{6,14},{7,15},{8,0},{9,1},... | collective-permute-start | bytes 393224 | tf_op jit(solution)/shard_map/ppermute | solution.py:52

commit v7 on v6

--- a/solution.py
+++ b/solution.py
@@ -345,7 +345,7 @@
     if split:
         near += [beside(bits, [gate]) for bits in range(PLANE, NEAR * PLANE)]
     tokens, other = gather(tokens, stages[rest])
-    down_a = bring(down_a_block, [up, other] + arrays(gate_far) + near[PLANE:])
+    down_a = bring(down_a_block, [up, other] + arrays(gate_far) + near[PLANE:-2])
     up_far = swapped(up, 1)
     tokens, other = gather(tokens, stages[rest + 1])
     down_b = bring(down_b_block, [down_a, other] + arrays(up_far))

time: 223 us -> 222 us (level)
  waiting for transfers between devices: 112 us -> 108 us
    all_to_all x4, waiting for transfers between devices: 10.3 us -> 7.98 us  [bring(): return lax.all_to_all(block, 'ep', split_axis=0, concat_axis=0, tiled=True)]
  transfers between devices with their start and end apart: 26 -> 26, of which waited for: 13 -> 9; matrix products, arithmetic and copies ran while one was open for 16% -> 16% of each run, Pallas kernels for 6% -> 6%
where the time goes in v7:
time: 222 us; the launch traced here: 221 us
  waiting for transfers between devices  108 us (49%)
  starting transfers between devices  49.4 us (22%)
  Pallas kernels  22.8 us (10%)
  local copies, waits for them, and re-layouts  18.5 us (8%)
  matrix products  12 us (5%)
  other arithmetic  9.47 us (4%)
    ppermute x19, waiting for transfers between devices, swap_ep(): return lax.ppermute(x, 'ep', [(i, i ^ bits) for i in range(count)])  100 us
    ppermute x19, starting transfers between devices, swap_ep(): return lax.ppermute(x, 'ep', [(i, i ^ bits) for i in range(count)])  23.2 us
    all_to_all x4, starting transfers between devices, bring(): return lax.all_to_all(block, 'ep', split_axis=0, concat_axis=0, tiled=True)  21.4 us
    pallas_call x1, Pallas kernels, run_hidden(): pl.pallas_call(functools.partial(hidden_kernel, places, experts), grid_sp...  13.7 us
    squeeze x4, local copies, waits for them, and re-layouts, cut_out(): lax.dynamic_slice(learner_weights, (0, matrix, low, start), (experts, 1,...  11.6 us
    pallas_call x1, Pallas kernels, run_down(): pl.pallas_call(functools.partial(down_kernel, cut, far is not None), grid...  9.09 us
    all_to_all x4, waiting for transfers between devices, bring(): return lax.all_to_all(block, 'ep', split_axis=0, concat_axis=0, tiled=True)  7.98 us
    dot_general x1, matrix products, shards(): attn = jnp.dot(context, out_weight, preferred_element_type=jnp.float32)  5.09 us
  transfers between devices with their start and end apart: 26, of which 9 were waited for; matrix products, arithmetic and copies ran while one was open for 16% of the time, Pallas kernels for 6%

profile of v7, /device:TPU:0, one launch (start us, length us, event | category | flops | bytes accessed | tf_op | source)
XLA Modules:
  0.0 221.1 jit_solution(5175429479698424089)
XLA Ops:
  0.0 2.9 %dynamic-slice_bitcast_fusion.1 = bf16[16,128,384]{2,1,0:T(8,128)(2,1)} fusion(bf16[16,3,128,768]{3,2,1,0:T(8,128)(2,1)} %param.23, s32[]{:T(128)S(6)} %select_n.77), kind=kLoop, calls=%fused_computation.5 | loop fusion | bytes 3145732 | tf_op jit(solution)/shard_map/squeeze | solution.py:280
  3.0 7.5 %all-to-all-start = ((bf16[16,128,384]{2,1,0:T(8,128)(2,1)}), bf16[16,128,384]{2,1,0:T(8,128)(2,1)}, u32[]{:S(2)}, u32[]{:S(2)}) async-start(bf16[16,128,384]{2,1,0:T(8,128)(2,1)} %dynamic-slice_bitcast_fusion.1), calls=%async_computation | async-start | bytes 3145728 | tf_op jit(solution)/shard_map/all_to_all | solution.py:286
  10.6 0.3 fusion.11
  11.0 4.5 %fusion.24 = (f32[64,2,8]{2,1,0:T(2,128)S(1)}, f32[64,2,8,96]{3,2,1,0:T(8,128)}) fusion(bf16[64,2,96,128]{3,2,1,0:T(8,128)(2,1)} %param.15, bf16[64,16,128]{2,1,0:T(8,128)(2,1)S(1)} %copy-done.14, pred[64,96]{1,0:T(8,128)(4,1)S(1)} %iota_compare_fusion.1), kind=kOutput, calls=%fused_computation.81 | convolution fusion | flops 25459712 | bytes 3811328 | tf_op jit(solution)/shard_map/skgd,skld->skgl/dot_general | solution.py:22
  15.5 0.1 copy.33
  15.7 1.4 fusion.6
  17.5 0.1 copy.35
  17.6 0.1 copy.36
  17.7 2.1 fusion.1
  19.8 5.1 %multiply_reduce_fusion = (f32[64]{0:T(128)S(1)}, f32[64,2048]{1,0:T(8,128)S(1)}) fusion(bf16[2048,2048]{1,0:T(8,128)(2,1)} %param.19, bf16[8,8,16,128]{3,2,1,0:T(8,128)(2,1)S(1)} %bitcast.108, bf16[64,2048]{1,0:T(8,128)(2,1)S(1)} %copy-done.13), kind=kOutput, calls=%fused_computation.28 | convolution fusion | flops 537395136 | bytes 9437440 | tf_op jit(solution)/shard_map/dot_general | solution.py:319
  25.0 0.1 multiply_convert_fusion
  25.1 0.1 concatenate.23
  25.2 2.8 %collective-permute-start = (bf16[64,2176]{1,0:T(8,128)(2,1)S(1)}, bf16[64,2176]{1,0:T(8,128)(2,1)S(1)}, u32[]{:S(2)}, u32[]{:S(2)}) collective-permute-start(bf16[64,2176]{1,0:T(8,128)(2,1)S(1)} %concatenate.23), channel_id=1, source_target_pairs={{0,8},{1,9},{2,10},{3,11},{4,12},{5,13},{6,14},{7,15},{8,0},{9,1},... | collective-permute-start | bytes 835592 | tf_op jit(solution)/shard_map/ppermute | solution.py:52
  28.0 2.0 dynamic-slice_bitcast_fusion.3
  30.0 0.9 collective-permute-start.7
  31.0 0.6 collective-permute-start.6
  31.6 0.3 collective-permute-start.5
  31.9 2.1 slice_bitcast_fusion
  34.0 3.0 %dynamic-slice_bitcast_fusion.2 = bf16[16,96,384]{2,1,0:T(8,128)(2,1)} fusion(bf16[16,3,128,768]{3,2,1,0:T(8,128)(2,1)} %param.23, s32[]{:T(128)S(6)} %select_n.78), kind=kLoop, calls=%fused_computation.11 | loop fusion | bytes 2359300 | tf_op jit(solution)/shard_map/squeeze | solution.py:280
  37.0 3.5 %dynamic-slice_bitcast_fusion = bf16[16,128,384]{2,1,0:T(8,128)(2,1)} fusion(bf16[16,3,128,768]{3,2,1,0:T(8,128)(2,1)} %param.23, s32[]{:T(128)S(6)} %select_n.78), kind=kLoop, calls=%fused_computation.4 | loop fusion | bytes 3145732 | tf_op jit(solution)/shard_map/squeeze | solution.py:280
  40.5 8.0 %all-to-all-done.refs_0_ = bf16[16,128,384]{2,1,0:T(8,128)(2,1)} async-done(((bf16[16,128,384]{2,1,0:T(8,128)(2,1)}), bf16[16,128,384]{2,1,0:T(8,128)(2,1)}, u32[]{:S(2)}, u32[]{:S(2)}) %all-to-all-start) | async-done | bytes 1572896 | tf_op jit(solution)/shard_map/all_to_all | solution.py:286
  48.5 11.7 %collective-permute-done = bf16[64,2176]{1,0:T(8,128)(2,1)S(1)} collective-permute-done((bf16[64,2176]{1,0:T(8,128)(2,1)S(1)}, bf16[64,2176]{1,0:T(8,128)(2,1)S(1)}, u32[]{:S(2)}, u32[]{:S(2)}) %collective-permute-start) | collective-permute-done | bytes 278560 | tf_op jit(solution)/shard_map/ppermute | solution.py:52
  60.2 3.7 %all-to-all-start.1 = ((bf16[16,128,384]{2,1,0:T(8,128)(2,1)}), bf16[16,128,384]{2,1,0:T(8,128)(2,1)S(1)}, u32[]{:S(2)}, u32[]{:S(2)}) async-start(bf16[16,128,384]{2,1,0:T(8,128)(2,1)} %dynamic-slice_bitcast_fusion), calls=%async_computation.1 | async-start | bytes 3145728 | tf_op jit(solution)/shard_map/all_to_all | solution.py:286
  63.9 1.6 collective-permute-start.4
  65.5 0.8 pad_maximum_fusion.4
  66.4 1.8 collective-permute-start.1
  68.2 1.8 dynamic-slice_bitcast_fusion.7
  70.1 1.2 collective-permute-start.9
  71.3 33.4 %collective-permute-done.1 = bf16[128,2176]{1,0:T(8,128)(2,1)S(1)} collective-permute-done((bf16[128,2176]{1,0:T(8,128)(2,1)}, bf16[128,2176]{1,0:T(8,128)(2,1)S(1)}, u32[]{:S(2)}, u32[]{:S(2)}) %collective-permute-start.1) | collective-permute-done | bytes 557088 | tf_op jit(solution)/shard_map/ppermute | solution.py:52
  104.7 1.2 pad_maximum_fusion.2
  105.9 1.5 collective-permute-start.2
  107.5 5.0 %all-to-all-start.2 = ((bf16[16,96,384]{2,1,0:T(8,128)(2,1)}), bf16[16,96,384]{2,1,0:T(8,128)(2,1)}, u32[]{:S(2)}, u32[]{:S(2)}) async-start(bf16[16,96,384]{2,1,0:T(8,128)(2,1)} %dynamic-slice_bitcast_fusion.2), calls=%async_computation.2 | async-start | bytes 2359296 | tf_op jit(solution)/shard_map/all_to_all | solution.py:286
  112.5 0.1 constant_dynamic-slice_fusion.4
  112.7 0.2 pad_maximum_fusion.1
  112.8 1.6 collective-permute-start.8
  114.4 28.5 %collective-permute-done.2 = bf16[256,2176]{1,0:T(8,128)(2,1)} collective-permute-done((bf16[256,2176]{1,0:T(8,128)(2,1)}, bf16[256,2176]{1,0:T(8,128)(2,1)}, u32[]{:S(2)}, u32[]{:S(2)}) %collective-permute-start.2) | collective-permute-done | bytes 1114144 | tf_op jit(solution)/shard_map/ppermute | solution.py:52
  142.9 1.4 pad_maximum_fusion.first_ref
  144.5 5.2 %all-to-all-start.3 = ((bf16[16,32,768]{2,1,0:T(8,128)(2,1)}), bf16[16,32,768]{2,1,0:T(8,128)(2,1)}, u32[]{:S(2)}, u32[]{:S(2)}) async-start(bf16[16,32,768]{2,1,0:T(8,128)(2,1)} %slice_bitcast_fusion), calls=%async_computation.3 | async-start | bytes 1572864 | tf_op jit(solution)/shard_map/all_to_all | solution.py:286
  149.7 1.1 constant_dynamic-slice_fusion.1
  150.9 1.6 collective-permute-start.11
  152.5 2.2 %collective-permute-start.13 = (bf16[1,96,384]{2,1,0:T(8,128)(2,1)S(1)}, bf16[1,96,384]{2,1,0:T(8,128)(2,1)S(1)}, u32[]{:S(2)}, u32[]{:S(2)}) collective-permute-start(bf16[1,96,384]{2,1,0:T(8,128)(2,1)S(1)} %copy-done.16), channel_id=1, source_target_pairs={{0,7},{1,6},{2,5},{3,4},{4,3},{5,2},{6,1},{7,0},{8,15},{9,14},{10,... | collective-permute-start | bytes 221192 | tf_op jit(solution)/shard_map/ppermute | solution.py:52
  154.7 0.6 collective-permute-start.12
  155.3 0.6 pad_add_fusion.where_ref
  155.9 13.7 %shard_map.118.hidden_ref = bf16[1024,768]{1,0:T(8,128)(2,1)} custom-call(s32[2]{0:T(128)} %pad_add_fusion.where_ref, bf16[512,2176]{1,0:T(8,128)(2,1)} %copy-done.3, bf16[512,2176]{1,0:T(8,128)(2,1)} %collective-permute-done.3.second_ref, bf16[16,128,384]{2,1,0:T(8,128)(2,1)} %all-to-all-done.refs_0_, bf16[16,128,384]{2,1,0:T(8,128)(2,1)} %collective-permute-done.4.refs_1_, ...), custom_call_target="tpu_custom_call" | custom-call | tf_op jit(solution)/shard_map/pallas_call | solution.py:185
  169.7 0.6 copy-done.19
  170.3 0.2 copy-done.12
  170.5 9.1 %shard_map.119 = (bf16[512,1024]{1,0:T(8,128)(2,1)}, bf16[512,1024]{1,0:T(8,128)(2,1)}, bf16[512,1024]{1,0:T(8,128)(2,1)}, bf16[512,1024]{1,0:T(8,128)(2,1)}) custom-call(s32[2]{0:T(128)} %pad_add_fusion.where_ref, bf16[1024,768]{1,0:T(8,128)(2,1)} %shard_map.118.hidden_ref, bf16[16,96,384]{2,1,0:T(8,128)(2,1)} %all-to-all-done.2.refs_0_, ...), custom_call_target="tpu_custom_call" | custom-call | tf_op jit(solution)/shard_map/pallas_call | solution.py:225
  179.7 0.5 collective-permute-start.18
  180.2 2.4 %collective-permute-done.14 = bf16[512,1024]{1,0:T(8,128)(2,1)S(1)} collective-permute-done((bf16[512,1024]{1,0:T(8,128)(2,1)}, bf16[512,1024]{1,0:T(8,128)(2,1)S(1)}, u32[]{:S(2)}, u32[]{:S(2)}) %collective-permute-start.14) | collective-permute-done | bytes 1048608 | tf_op jit(solution)/shard_map/ppermute | solution.py:52
  182.5 1.7 add_convert_fusion.1
  184.3 1.5 collective-permute-start.15
  185.8 0.4 add_convert_fusion
  186.3 1.6 collective-permute-start.19
  187.9 10.5 %collective-permute-done.15 = bf16[2,2,64,1024]{3,2,1,0:T(8,128)(2,1)S(1)} collective-permute-done((bf16[2,2,64,1024]{3,2,1,0:T(8,128)(2,1)S(1)}, bf16[2,2,64,1024]{3,2,1,0:T(8,128)(2,1)S(1)}, u32[]{:S(2)}, u32[]{:S(2)}) %collective-permute-start.15) | collective-permute-done | bytes 524320 | tf_op jit(solution)/shard_map/ppermute | solution.py:52
  198.3 0.2 fusion.3
  198.6 1.8 collective-permute-start.16
  200.4 0.2 fusion.2
  200.6 1.5 collective-permute-start.20
  202.1 4.3 %collective-permute-done.16 = bf16[2,64,1024]{2,1,0:T(8,128)(2,1)S(1)} collective-permute-done((bf16[2,64,1024]{2,1,0:T(8,128)(2,1)S(1)}, bf16[2,64,1024]{2,1,0:T(8,128)(2,1)S(1)}, u32[]{:S(2)}, u32[]{:S(2)}) %collective-permute-start.16) | collective-permute-done | bytes 262176 | tf_op jit(solution)/shard_map/ppermute | solution.py:52
  206.5 3.3 %collective-permute-start.17 = (bf16[64,1024]{1,0:T(8,128)(2,1)S(1)}, bf16[64,1024]{1,0:T(8,128)(2,1)S(1)}, u32[]{:S(2)}, u32[]{:S(2)}) collective-permute-start(bf16[64,1024]{1,0:T(8,128)(2,1)S(1)} %slice_bitcast_fusion.9), channel_id=1, source_target_pairs={{0,8},{1,9},{2,10},{3,11},{4,12},{5,13},{6,14},{7,15},{8,0},{9,1},... | collective-permute-start | bytes 393224 | tf_op jit(solution)/shard_map/ppermute | solution.py:52
  209.9 0.7 collective-permute-start.21
  210.6 7.9 %collective-permute-done.17 = bf16[64,1024]{1,0:T(8,128)(2,1)S(1)} collective-permute-done((bf16[64,1024]{1,0:T(8,128)(2,1)S(1)}, bf16[64,1024]{1,0:T(8,128)(2,1)S(1)}, u32[]{:S(2)}, u32[]{:S(2)}) %collective-permute-start.17) | collective-permute-done | bytes 131104 | tf_op jit(solution)/shard_map/ppermute | solution.py:52
  218.5 1.8 collective-permute-done.21
  220.3 0.8 add_convert_fusion.2
  (97 shorter events, 1.4 us)
Async XLA Ops:
  0.0 17.7 %copy-start = (bf16[64,2,96,128]{3,2,1,0:T(8,128)(2,1)S(1)}, bf16[64,2,96,128]{3,2,1,0:T(8,128)(2,1)}, u32[]{:S(2)}) copy-start(bf16[64,2,96,128]{3,2,1,0:T(8,128)(2,1)} %param.16) | copy-start | bytes 9437188
  3.0 7.5 %copy-start.25 = (s32[64]{0:T(128)S(1)}, s32[64]{0:T(128)}, u32[]{:S(2)}) copy-start(s32[64]{0:T(128)} %param.17) | copy-start | bytes 772
  3.0 7.6 %copy-start.14 = (bf16[64,16,128]{2,1,0:T(8,128)(2,1)S(1)}, bf16[64,16,128]{2,1,0:T(8,128)(2,1)}, u32[]{:S(2)}) copy-start(bf16[64,16,128]{2,1,0:T(8,128)(2,1)} %param.12) | copy-start | bytes 786436
  3.0 7.6 %copy-start.26 = (bf16[64,2,128]{2,1,0:T(2,128)(2,1)S(1)}, bf16[64,2,128]{2,1,0:T(2,128)(2,1)}, u32[]{:S(2)}) copy-start(bf16[64,2,128]{2,1,0:T(2,128)(2,1)} %param.13) | copy-start | bytes 98308
  3.0 45.5 %all-to-all-start = ((bf16[16,128,384]{2,1,0:T(8,128)(2,1)}), bf16[16,128,384]{2,1,0:T(8,128)(2,1)}, u32[]{:S(2)}, u32[]{:S(2)}) async-start(bf16[16,128,384]{2,1,0:T(8,128)(2,1)} %dynamic-slice_bitcast_fusion.1), calls=%async_computation | async-start | bytes 3145728 | tf_op jit(solution)/shard_map/all_to_all | solution.py:286
  11.0 6.2 %copy-start.23 = (f32[64,8]{0,1:T(8,128)S(1)}, f32[64,8]{0,1:T(8,128)}, u32[]{:S(2)}) copy-start(f32[64,8]{0,1:T(8,128)} %param.22) | copy-start | bytes 6148
  11.0 6.2 %copy-start.24 = (s32[64,8]{0,1:T(8,128)S(1)}, s32[64,8]{0,1:T(8,128)}, u32[]{:S(2)}) copy-start(s32[64,8]{0,1:T(8,128)} %param.21) | copy-start | bytes 6148
  11.0 6.4 %copy-start.21 = (bf16[64,2,128]{2,1,0:T(2,128)(2,1)S(1)}, bf16[64,2,128]{2,1,0:T(2,128)(2,1)}, u32[]{:S(2)}) copy-start(bf16[64,2,128]{2,1,0:T(2,128)(2,1)} %param.14) | copy-start | bytes 98308
  17.7 2.1 copy-start.13
  19.8 5.1 %copy-start.22 = (f32[2048]{0:T(1024)S(1)}, f32[2048]{0:T(1024)}, u32[]{:S(2)}) copy-start(f32[2048]{0:T(1024)} %param.20) | copy-start | bytes 24580
  24.9 9.1 %copy-start.4 = (f32[64,2048]{1,0:T(8,128)}, f32[64,2048]{1,0:T(8,128)S(1)}, u32[]{:S(2)}) copy-start(f32[64,2048]{1,0:T(8,128)S(1)} %get-tuple-element.45) | copy-start | bytes 1572868
  25.2 35.0 %collective-permute-start = (bf16[64,2176]{1,0:T(8,128)(2,1)S(1)}, bf16[64,2176]{1,0:T(8,128)(2,1)S(1)}, u32[]{:S(2)}, u32[]{:S(2)}) collective-permute-start(bf16[64,2176]{1,0:T(8,128)(2,1)S(1)} %concatenate.23), channel_id=1, source_target_pairs={{0,8},{1,9},{2,10},{3,11},{4,12},{5,13},{6,14},{7,15},{8,0},{9,1},... | collective-permute-start | bytes 835592 | tf_op jit(solution)/shard_map/ppermute | solution.py:52
  30.0 18.5 %collective-permute-start.7 = (bf16[2,128,384]{2,1,0:T(8,128)(2,1)S(1)}, bf16[2,128,384]{2,1,0:T(8,128)(2,1)S(1)}, u32[]{:S(2)}, u32[]{:S(2)}) collective-permute-start(bf16[2,128,384]{2,1,0:T(8,128)(2,1)S(1)} %get-tuple-element.29), channel_id=1, source_target_pairs={{0,3},{1,2},{2,1},{3,0},{4,7},{5,6},{6,5},{7,4},{8,11},{9,10},{10,... | collective-permute-start | bytes 589832 | tf_op jit(solution)/shard_map/ppermute | solution.py:52
  31.0 17.5 %collective-permute-start.6 = (bf16[2,128,384]{2,1,0:T(8,128)(2,1)S(1)}, bf16[2,128,384]{2,1,0:T(8,128)(2,1)S(1)}, u32[]{:S(2)}, u32[]{:S(2)}) collective-permute-start(bf16[2,128,384]{2,1,0:T(8,128)(2,1)S(1)} %get-tuple-element.30), channel_id=1, source_target_pairs={{0,2},{1,3},{2,0},{3,1},{4,6},{5,7},{6,4},{7,5},{8,10},{9,11},{10,... | collective-permute-start | bytes 589832 | tf_op jit(solution)/shard_map/ppermute | solution.py:52
  31.6 17.0 %collective-permute-start.5 = (bf16[2,128,384]{2,1,0:T(8,128)(2,1)S(1)}, bf16[2,128,384]{2,1,0:T(8,128)(2,1)S(1)}, u32[]{:S(2)}, u32[]{:S(2)}) collective-permute-start(bf16[2,128,384]{2,1,0:T(8,128)(2,1)S(1)} %get-tuple-element.31), channel_id=1, source_target_pairs={{0,1},{1,0},{2,3},{3,2},{4,5},{5,4},{6,7},{7,6},{8,9},{9,8},{10,11... | collective-permute-start | bytes 589832 | tf_op jit(solution)/shard_map/ppermute | solution.py:52
  48.5 21.5 %copy-start.9 = (bf16[2,128,384]{2,1,0:T(8,128)(2,1)}, bf16[2,128,384]{2,1,0:T(8,128)(2,1)S(1)}, u32[]{:S(2)}) copy-start(bf16[2,128,384]{2,1,0:T(8,128)(2,1)S(1)} %collective-permute-done.7.refs_7_.refs_6_) | copy-start | bytes 589828
  48.5 21.5 %copy-start.10 = (bf16[2,128,384]{2,1,0:T(8,128)(2,1)}, bf16[2,128,384]{2,1,0:T(8,128)(2,1)S(1)}, u32[]{:S(2)}) copy-start(bf16[2,128,384]{2,1,0:T(8,128)(2,1)S(1)} %collective-permute-done.6.refs_6_.refs_5_) | copy-start | bytes 589828
  48.5 21.5 %copy-start.11 = (bf16[2,128,384]{2,1,0:T(8,128)(2,1)}, bf16[2,128,384]{2,1,0:T(8,128)(2,1)S(1)}, u32[]{:S(2)}) copy-start(bf16[2,128,384]{2,1,0:T(8,128)(2,1)S(1)} %collective-permute-done.5.refs_5_.refs_4_) | copy-start | bytes 589828
  60.2 47.3 %all-to-all-start.1 = ((bf16[16,128,384]{2,1,0:T(8,128)(2,1)}), bf16[16,128,384]{2,1,0:T(8,128)(2,1)S(1)}, u32[]{:S(2)}, u32[]{:S(2)}) async-start(bf16[16,128,384]{2,1,0:T(8,128)(2,1)} %dynamic-slice_bitcast_fusion), calls=%async_computation.1 | async-start | bytes 3145728 | tf_op jit(solution)/shard_map/all_to_all | solution.py:286
  63.9 43.5 %collective-permute-start.4 = (bf16[16,128,384]{2,1,0:T(8,128)(2,1)}, bf16[16,128,384]{2,1,0:T(8,128)(2,1)}, u32[]{:S(2)}, u32[]{:S(2)}) collective-permute-start(bf16[16,128,384]{2,1,0:T(8,128)(2,1)} %all-to-all-done.refs_0_), channel_id=1, source_target_pairs={{0,16},{16,0},{1,17},{17,1},{2,18},{18,2},{3,19},{19,3},{4,20},{20... | collective-permute-start | bytes 4718600 | tf_op jit(solution)/shard_map/ppermute | solution.py:56
  66.4 38.4 %collective-permute-start.1 = (bf16[128,2176]{1,0:T(8,128)(2,1)}, bf16[128,2176]{1,0:T(8,128)(2,1)S(1)}, u32[]{:S(2)}, u32[]{:S(2)}) collective-permute-start(bf16[128,2176]{1,0:T(8,128)(2,1)} %pad_maximum_fusion.4), channel_id=1, source_target_pairs={{0,4},{1,5},{2,6},{3,7},{4,0},{5,1},{6,2},{7,3},{8,12},{9,13},{10,... | collective-permute-start | bytes 1671176 | tf_op jit(solution)/shard_map/ppermute | solution.py:52
  70.0 37.4 %collective-permute-start.10 = (bf16[1,96,384]{2,1,0:T(8,128)(2,1)S(1)}, bf16[1,96,384]{2,1,0:T(8,128)(2,1)S(1)}, u32[]{:S(2)}, u32[]{:S(2)}) collective-permute-start(bf16[1,96,384]{2,1,0:T(8,128)(2,1)S(1)} %get-tuple-element.26), channel_id=1, source_target_pairs={{0,5},{1,4},{2,7},{3,6},{4,1},{5,0},{6,3},{7,2},{8,13},{9,12},{10,... | collective-permute-start | bytes 221192 | tf_op jit(solution)/shard_map/ppermute | solution.py:52
  70.1 37.4 %collective-permute-start.9 = (bf16[1,96,384]{2,1,0:T(8,128)(2,1)S(1)}, bf16[1,96,384]{2,1,0:T(8,128)(2,1)S(1)}, u32[]{:S(2)}, u32[]{:S(2)}) collective-permute-start(bf16[1,96,384]{2,1,0:T(8,128)(2,1)S(1)} %get-tuple-element.27), channel_id=1, source_target_pairs={{0,4},{1,5},{2,6},{3,7},{4,0},{5,1},{6,2},{7,3},{8,12},{9,13},{10,... | collective-permute-start | bytes 221192 | tf_op jit(solution)/shard_map/ppermute | solution.py:52
  104.7 2.8 %copy-start.6 = (bf16[128,2176]{1,0:T(8,128)(2,1)}, bf16[128,2176]{1,0:T(8,128)(2,1)S(1)}, u32[]{:S(2)}) copy-start(bf16[128,2176]{1,0:T(8,128)(2,1)S(1)} %collective-permute-done.1) | copy-start | bytes 1671172
  105.9 37.0 %collective-permute-start.2 = (bf16[256,2176]{1,0:T(8,128)(2,1)}, bf16[256,2176]{1,0:T(8,128)(2,1)}, u32[]{:S(2)}, u32[]{:S(2)}) collective-permute-start(bf16[256,2176]{1,0:T(8,128)(2,1)} %pad_maximum_fusion.2), channel_id=1, source_target_pairs={{0,2},{1,3},{2,0},{3,1},{4,6},{5,7},{6,4},{7,5},{8,10},{9,11},{10,... | collective-permute-start | bytes 3342344 | tf_op jit(solution)/shard_map/ppermute | solution.py:52
  107.5 5.2 %copy-start.17 = (bf16[1,96,384]{2,1,0:T(8,128)(2,1)}, bf16[1,96,384]{2,1,0:T(8,128)(2,1)S(1)}, u32[]{:S(2)}) copy-start(bf16[1,96,384]{2,1,0:T(8,128)(2,1)S(1)} %collective-permute-done.10.refs_8_) | copy-start | bytes 221188
  107.5 5.2 %copy-start.18 = (bf16[1,96,384]{2,1,0:T(8,128)(2,1)}, bf16[1,96,384]{2,1,0:T(8,128)(2,1)S(1)}, u32[]{:S(2)}) copy-start(bf16[1,96,384]{2,1,0:T(8,128)(2,1)S(1)} %collective-permute-done.9.refs_7_) | copy-start | bytes 221188
  107.5 5.2 %copy-start.2 = (bf16[16,128,384]{2,1,0:T(8,128)(2,1)}, bf16[16,128,384]{2,1,0:T(8,128)(2,1)S(1)}, u32[]{:S(2)}) copy-start(bf16[16,128,384]{2,1,0:T(8,128)(2,1)S(1)} %all-to-all-done.1.refs_2_) | copy-start | bytes 4718596
  107.5 37.0 %all-to-all-start.2 = ((bf16[16,96,384]{2,1,0:T(8,128)(2,1)}), bf16[16,96,384]{2,1,0:T(8,128)(2,1)}, u32[]{:S(2)}, u32[]{:S(2)}) async-start(bf16[16,96,384]{2,1,0:T(8,128)(2,1)} %dynamic-slice_bitcast_fusion.2), calls=%async_computation.2 | async-start | bytes 2359296 | tf_op jit(solution)/shard_map/all_to_all | solution.py:286
  112.5 30.4 %copy-start.7 = (bf16[128,2176]{1,0:T(8,128)(2,1)S(1)}, bf16[128,2176]{1,0:T(8,128)(2,1)}, u32[]{:S(2)}) copy-start(bf16[128,2176]{1,0:T(8,128)(2,1)} %copy-done.6) | copy-start | bytes 1671172
  112.8 31.6 %collective-permute-start.8 = (bf16[12,128,384]{2,1,0:T(8,128)(2,1)S(1)}, bf16[12,128,384]{2,1,0:T(8,128)(2,1)}, u32[]{:S(2)}, u32[]{:S(2)}) collective-permute-start(bf16[12,128,384]{2,1,0:T(8,128)(2,1)S(1)} %pad_maximum_fusion.1), channel_id=1, source_target_pairs={{0,16},{16,0},{1,17},{17,1},{2,18},{18,2},{3,19},{19,3},{4,20},{20... | collective-permute-start | bytes 3538952 | tf_op jit(solution)/shard_map/ppermute | solution.py:56
  144.4 11.6 %copy-start.3 = (bf16[512,2176]{1,0:T(8,128)(2,1)}, bf16[512,2176]{1,0:T(8,128)(2,1)S(1)}, u32[]{:S(2)}) copy-start(bf16[512,2176]{1,0:T(8,128)(2,1)S(1)} %pad_maximum_fusion.first_ref) | copy-start | bytes 6684676
  144.4 8.1 %copy-start.16 = (bf16[1,96,384]{2,1,0:T(8,128)(2,1)S(1)}, bf16[1,96,384]{2,1,0:T(8,128)(2,1)}, u32[]{:S(2)}) copy-start(bf16[1,96,384]{2,1,0:T(8,128)(2,1)} %get-tuple-element.25) | copy-start | bytes 221188
  144.4 10.3 %copy-start.15 = (bf16[1,96,384]{2,1,0:T(8,128)(2,1)S(1)}, bf16[1,96,384]{2,1,0:T(8,128)(2,1)}, u32[]{:S(2)}) copy-start(bf16[1,96,384]{2,1,0:T(8,128)(2,1)} %get-tuple-element.28) | copy-start | bytes 221188
  144.4 11.5 %collective-permute-start.3 = (bf16[512,2176]{1,0:T(8,128)(2,1)S(1)}, bf16[512,2176]{1,0:T(8,128)(2,1)}, u32[]{:S(2)}, u32[]{:S(2)}) collective-permute-start(bf16[512,2176]{1,0:T(8,128)(2,1)S(1)} %pad_maximum_fusion.first_ref), channel_id=1, source_target_pairs={{0,1},{1,0},{2,3},{3,2},{4,5},{5,4},{6,7},{7,6},{8,9},{9,8},{10,11... | collective-permute-start | bytes 6684680 | tf_op jit(solution)/shard_map/ppermute | solution.py:52
  144.5 25.2 %all-to-all-start.3 = ((bf16[16,32,768]{2,1,0:T(8,128)(2,1)}), bf16[16,32,768]{2,1,0:T(8,128)(2,1)}, u32[]{:S(2)}, u32[]{:S(2)}) async-start(bf16[16,32,768]{2,1,0:T(8,128)(2,1)} %slice_bitcast_fusion), calls=%async_computation.3 | async-start | bytes 1572864 | tf_op jit(solution)/shard_map/all_to_all | solution.py:286
  150.9 18.8 %collective-permute-start.11 = (bf16[8,96,384]{2,1,0:T(8,128)(2,1)S(1)}, bf16[8,96,384]{2,1,0:T(8,128)(2,1)S(1)}, u32[]{:S(2)}, u32[]{:S(2)}) collective-permute-start(bf16[8,96,384]{2,1,0:T(8,128)(2,1)S(1)} %pad_maximum_fusion.3), channel_id=1, source_target_pairs={{0,16},{16,0},{1,17},{17,1},{2,18},{18,2},{3,19},{19,3},{4,20},{20... | collective-permute-start | bytes 1769480 | tf_op jit(solution)/shard_map/ppermute | solution.py:56
  152.5 17.1 %collective-permute-start.13 = (bf16[1,96,384]{2,1,0:T(8,128)(2,1)S(1)}, bf16[1,96,384]{2,1,0:T(8,128)(2,1)S(1)}, u32[]{:S(2)}, u32[]{:S(2)}) collective-permute-start(bf16[1,96,384]{2,1,0:T(8,128)(2,1)S(1)} %copy-done.16), channel_id=1, source_target_pairs={{0,7},{1,6},{2,5},{3,4},{4,3},{5,2},{6,1},{7,0},{8,15},{9,14},{10,... | collective-permute-start | bytes 221192 | tf_op jit(solution)/shard_map/ppermute | solution.py:52
  154.7 14.9 %collective-permute-start.12 = (bf16[1,96,384]{2,1,0:T(8,128)(2,1)S(1)}, bf16[1,96,384]{2,1,0:T(8,128)(2,1)S(1)}, u32[]{:S(2)}, u32[]{:S(2)}) collective-permute-start(bf16[1,96,384]{2,1,0:T(8,128)(2,1)S(1)} %copy-done.15), channel_id=1, source_target_pairs={{0,6},{1,7},{2,4},{3,5},{4,2},{5,3},{6,0},{7,1},{8,14},{9,15},{10,... | collective-permute-start | bytes 221192 | tf_op jit(solution)/shard_map/ppermute | solution.py:52
  169.6 0.6 copy-start.19
  169.6 0.7 copy-start.20
  169.6 0.9 copy-start.12
  179.6 2.9 %collective-permute-start.14 = (bf16[512,1024]{1,0:T(8,128)(2,1)}, bf16[512,1024]{1,0:T(8,128)(2,1)S(1)}, u32[]{:S(2)}, u32[]{:S(2)}) collective-permute-start(bf16[512,1024]{1,0:T(8,128)(2,1)} %get-tuple-element.22), channel_id=1, source_target_pairs={{0,1},{1,0},{2,3},{3,2},{4,5},{5,4},{6,7},{7,6},{8,9},{9,8},{10,11... | collective-permute-start | bytes 3145736 | tf_op jit(solution)/shard_map/ppermute | solution.py:52
  179.7 6.1 %collective-permute-start.18 = (bf16[512,1024]{1,0:T(8,128)(2,1)}, bf16[512,1024]{1,0:T(8,128)(2,1)S(1)}, u32[]{:S(2)}, u32[]{:S(2)}) collective-permute-start(bf16[512,1024]{1,0:T(8,128)(2,1)} %get-tuple-element.24), channel_id=1, source_target_pairs={{0,1},{1,0},{2,3},{3,2},{4,5},{5,4},{6,7},{7,6},{8,9},{9,8},{10,11... | collective-permute-start | bytes 3145736 | tf_op jit(solution)/shard_map/ppermute | solution.py:52
  182.5 3.3 %copy-start.8 = (bf16[512,1024]{1,0:T(8,128)(2,1)S(1)}, bf16[512,1024]{1,0:T(8,128)(2,1)}, u32[]{:S(2)}) copy-start(bf16[512,1024]{1,0:T(8,128)(2,1)} %get-tuple-element.23) | copy-start | bytes 3145732
  184.3 14.0 %collective-permute-start.15 = (bf16[2,2,64,1024]{3,2,1,0:T(8,128)(2,1)S(1)}, bf16[2,2,64,1024]{3,2,1,0:T(8,128)(2,1)S(1)}, u32[]{:S(2)}, u32[]{:S(2)}) collective-permute-start(bf16[2,2,64,1024]{3,2,1,0:T(8,128)(2,1)S(1)} %bitcast.109), channel_id=1, source_target_pairs={{0,2},{1,3},{2,0},{3,1},{4,6},{5,7},{6,4},{7,5},{8,10},{9,11},{10,... | collective-permute-start | bytes 1572872 | tf_op jit(solution)/shard_map/ppermute | solution.py:52
  186.3 14.1 %collective-permute-start.19 = (bf16[2,2,64,1024]{3,2,1,0:T(8,128)(2,1)S(1)}, bf16[2,2,64,1024]{3,2,1,0:T(8,128)(2,1)S(1)}, u32[]{:S(2)}, u32[]{:S(2)}) collective-permute-start(bf16[2,2,64,1024]{3,2,1,0:T(8,128)(2,1)S(1)} %slice_bitcast_fusion.1), channel_id=1, source_target_pairs={{0,4},{1,5},{2,6},{3,7},{4,0},{5,1},{6,2},{7,3},{8,12},{9,13},{10,... | collective-permute-start | bytes 1572872 | tf_op jit(solution)/shard_map/ppermute | solution.py:52
  198.6 21.7 %copy-start.5 = (f32[64,2048]{1,0:T(8,128)S(1)}, f32[64,2048]{1,0:T(8,128)}, u32[]{:S(2)}) copy-start(f32[64,2048]{1,0:T(8,128)} %copy-done.4) | copy-start | bytes 1572868
  198.6 7.8 %collective-permute-start.16 = (bf16[2,64,1024]{2,1,0:T(8,128)(2,1)S(1)}, bf16[2,64,1024]{2,1,0:T(8,128)(2,1)S(1)}, u32[]{:S(2)}, u32[]{:S(2)}) collective-permute-start(bf16[2,64,1024]{2,1,0:T(8,128)(2,1)S(1)} %slice_bitcast_fusion.5), channel_id=1, source_target_pairs={{0,4},{1,5},{2,6},{3,7},{4,0},{5,1},{6,2},{7,3},{8,12},{9,13},{10,... | collective-permute-start | bytes 786440 | tf_op jit(solution)/shard_map/ppermute | solution.py:52
  200.4 20.7 %copy-start.1 = (bf16[64,2,96,128]{3,2,1,0:T(8,128)(2,1)S(1)}, bf16[64,2,96,128]{3,2,1,0:T(8,128)(2,1)}, u32[]{:S(2)}) copy-start(bf16[64,2,96,128]{3,2,1,0:T(8,128)(2,1)} %param.16) | copy-start | bytes 9437188
  200.6 9.2 %collective-permute-start.20 = (bf16[2,64,1024]{2,1,0:T(8,128)(2,1)S(1)}, bf16[2,64,1024]{2,1,0:T(8,128)(2,1)S(1)}, u32[]{:S(2)}, u32[]{:S(2)}) collective-permute-start(bf16[2,64,1024]{2,1,0:T(8,128)(2,1)S(1)} %slice_bitcast_fusion.3), channel_id=1, source_target_pairs={{0,2},{1,3},{2,0},{3,1},{4,6},{5,7},{6,4},{7,5},{8,10},{9,11},{10,... | collective-permute-start | bytes 786440 | tf_op jit(solution)/shard_map/ppermute | solution.py:52
  206.5 12.0 %collective-permute-start.17 = (bf16[64,1024]{1,0:T(8,128)(2,1)S(1)}, bf16[64,1024]{1,0:T(8,128)(2,1)S(1)}, u32[]{:S(2)}, u32[]{:S(2)}) collective-permute-start(bf16[64,1024]{1,0:T(8,128)(2,1)S(1)} %slice_bitcast_fusion.9), channel_id=1, source_target_pairs={{0,8},{1,9},{2,10},{3,11},{4,12},{5,13},{6,14},{7,15},{8,0},{9,1},... | collective-permute-start | bytes 393224 | tf_op jit(solution)/shard_map/ppermute | solution.py:52
  209.9 10.4 %collective-permute-start.21 = (bf16[64,1024]{1,0:T(8,128)(2,1)S(1)}, bf16[64,1024]{1,0:T(8,128)(2,1)S(1)}, u32[]{:S(2)}, u32[]{:S(2)}) collective-permute-start(bf16[64,1024]{1,0:T(8,128)(2,1)S(1)} %slice_bitcast_fusion.7), channel_id=1, source_target_pairs={{0,8},{1,9},{2,10},{3,11},{4,12},{5,13},{6,14},{7,15},{8,0},{9,1},... | collective-permute-start | bytes 393224 | tf_op jit(solution)/shard_map/ppermute | solution.py:52
